TPU v7x, 32 devices: a whole 2x2x4 slice. The times are simulated.
32 devices in a mesh: section: 2 (over core), dp: 4 (over y, x), seq: 4 (over z).
Axes of the slice: x: 2, y: 2, z: 4, core: 2. Of those that a mesh axis runs over, the one named last changes fastest.
Arguments:
- ends_in: bfloat16 [2, 4, 4, 1024, 1280], P('section', None, 'dp', 'seq'), may hold values from -6 to 6
- lengths: int32 [4, 4], P(None, 'dp'), may hold values from 30 to 1024, as said below
- outer_gain: float32 [2, 1280], P('section'), may hold values from 0.5 to 1.5
- inner_gains: float32 [2, 2, 640], P('section'), may hold values from 0.5 to 1.5
- outer_biases: float32 [2, 2, 1280], P('section'), may hold values from -1.75 to 1.75
- inner_biases: float32 [2, 4, 640], P('section'), may hold values from -1.75 to 1.75
- down_in: bfloat16 [2, 1280, 640], P('section'), may hold values from -0.15625 to 0.15625
- conv_weight: bfloat16 [2, 5, 640, 640], P('section'), may hold values from -0.109375 to 0.109375
- up_out: bfloat16 [2, 640, 1280], P('section'), may hold values from -0.25 to 0.25
Outputs:
- ends_out: float32 [2, 4, 4, 1024, 1280], P('section', None, 'dp', 'seq')
- grad_outer_gain: float32 [2, 1280], P('section')
- grad_inner_gains: float32 [2, 2, 640], P('section')
- grad_outer_biases: float32 [2, 2, 1280], P('section')
- grad_inner_biases: float32 [2, 4, 640], P('section')
- grad_down_in: float32 [2, 1280, 640], P('section')
- grad_conv_weight: float32 [2, 5, 640, 640], P('section')
- grad_up_out: float32 [2, 640, 1280], P('section')
- rms: float32 [2, 2], P('section')
Inputs may be any that keep to these rules, and one draw needn't show every extreme that they name: `lengths`: in every micro-batch, each block of 1 consecutive items holds one item of the full 1024 positions.
All inputs are finite; a program needn't handle non-finite values.
Results may differ from a plain program's by a relative error of at most 0.011.
Values may be sent and summed in bfloat16 or wider, within the bound.
A program may use at most 128 MiB of HBM per device.

v0:
```python
import jax
import jax.numpy as jnp
from jax import lax
from jax.sharding import PartitionSpec as P

FILTER_TAPS = 5
FIRST_DILATION = 2
SECOND_DILATION = 128


def passed_along(value, axis, steps):
    count = lax.axis_size(axis)
    leading, last = (max(0, -steps), min(count, count - steps))
    return lax.ppermute(value, axis, [(source, source + steps) for source in range(leading, last)])


def norm_gelu(value, gain, shift):
    mean = jnp.mean(value, axis=-1, keepdims=True)
    centred = value - mean
    spread = jnp.mean(centred * centred, axis=-1, keepdims=True)
    return jax.nn.gelu(centred * lax.rsqrt(spread + 1e-05) * gain + shift)


def extend(block_index, backward):
    lower_rows = []
    upper_rows = []
    step = 1
    if backward:
        lower_rows.append(passed_along(block_index, "seq", step))
    else:
        lower_rows.append(passed_along(block_index, "seq", step))
    step = 1
    if backward:
        upper_rows.append(passed_along(block_index, "seq", -step))
    else:
        upper_rows.append(passed_along(block_index, "seq", -step))
    return jnp.concatenate(lower_rows + [block_index] + upper_rows, axis=1)


def take_taps(wide, starts, rows):
    return jnp.concatenate(
        [lax.dynamic_slice_in_dim(wide, start, rows, 1) for start in starts], axis=2
    )


def forward(input_rows, valid_mask, weights, starts):
    (
        gain_a,
        shift_a,
        bias_out,
        gain_b,
        gain_c,
        shift_b,
        shift_c,
        bias_in,
        bias_conv,
        weight_in,
        weight_conv,
        weight_out,
    ) = weights
    hidden_a, back_a = jax.vjp(norm_gelu, input_rows, gain_a, shift_a)
    low_a = hidden_a.astype(jnp.bfloat16)
    proj = jnp.dot(low_a, weight_in, preferred_element_type=jnp.float32) + bias_in
    hidden_b, back_b = jax.vjp(
        lambda value, gain, shift: norm_gelu(value, gain, shift) * valid_mask, proj, gain_b, shift_b
    )
    conv_in = hidden_b.astype(jnp.bfloat16)
    wide = extend(conv_in, False)
    taps = take_taps(wide, starts, input_rows.shape[1])
    flat_weight = weight_conv.reshape(-1, weight_conv.shape[2])
    conv = jnp.dot(taps, flat_weight, preferred_element_type=jnp.float32) + bias_conv
    hidden_c, back_c = jax.vjp(norm_gelu, conv, gain_c, shift_c)
    low_c = hidden_c.astype(jnp.bfloat16)
    branch = (
        jnp.dot(low_c, weight_out, preferred_element_type=jnp.float32) + bias_out
    ) * valid_mask
    return (input_rows + branch, branch, wide, (low_a, taps, low_c, back_a, back_b, back_c))


def backward(grad_out, valid_mask, weights, back_starts, saved):
    (
        gain_a,
        shift_a,
        bias_out,
        gain_b,
        gain_c,
        shift_b,
        shift_c,
        bias_in,
        bias_conv,
        weight_in,
        weight_conv,
        weight_out,
    ) = weights
    low_a, taps, low_c, back_a, back_b, back_c = saved
    grad_branch = grad_out * valid_mask
    low_branch = grad_branch.astype(jnp.bfloat16)
    grad_bias_out = jnp.sum(grad_branch, axis=(0, 1))
    grad_weight_out = jnp.einsum(
        "bri,brd->id", low_c, low_branch, preferred_element_type=jnp.float32
    )
    grad_hidden_c = jnp.einsum(
        "brd,id->bri", low_branch, weight_out, preferred_element_type=jnp.float32
    )
    grad_conv, grad_gain_c, grad_shift_c = back_c(grad_hidden_c)
    low_conv = grad_conv.astype(jnp.bfloat16)
    grad_bias_conv = jnp.sum(grad_conv, axis=(0, 1))
    grad_weight_conv = jnp.einsum(
        "brk,bro->ko", taps, low_conv, preferred_element_type=jnp.float32
    ).reshape(weight_conv.shape)
    wide_grad = extend(low_conv, True)
    grad_taps = take_taps(wide_grad, back_starts, grad_out.shape[1])
    turned = jnp.transpose(weight_conv, (1, 0, 2)).reshape(weight_conv.shape[1], -1)
    grad_hidden_b = jnp.einsum("brk,ik->bri", grad_taps, turned, preferred_element_type=jnp.float32)
    grad_proj, grad_gain_b, grad_shift_b = back_b(grad_hidden_b)
    low_proj = grad_proj.astype(jnp.bfloat16)
    grad_bias_in = jnp.sum(grad_proj, axis=(0, 1))
    grad_weight_in = jnp.einsum("brd,bri->di", low_a, low_proj, preferred_element_type=jnp.float32)
    grad_hidden_a = jnp.einsum(
        "bri,di->brd", low_proj, weight_in, preferred_element_type=jnp.float32
    )
    grad_inputs, grad_gain_a, grad_shift_a = back_a(grad_hidden_a)
    grads = (
        grad_gain_a,
        jnp.stack([grad_gain_b, grad_gain_c]),
        jnp.stack([grad_shift_a, grad_bias_out]),
        jnp.stack([grad_shift_b, grad_shift_c, grad_bias_in, grad_bias_conv]),
        grad_weight_in,
        grad_weight_conv,
        grad_weight_out,
    )
    return (grad_out + grad_inputs, grads)


def body(
    ends_in,
    lengths,
    outer_gain,
    inner_gains,
    outer_biases,
    inner_biases,
    down_in,
    conv_weight,
    up_out,
):
    weights = (
        outer_gain[0],
        outer_biases[0, 0],
        outer_biases[0, 1],
        inner_gains[0, 0],
        inner_gains[0, 1],
        inner_biases[0, 0],
        inner_biases[0, 1],
        inner_biases[0, 2],
        inner_biases[0, 3],
        down_in[0],
        conv_weight[0],
        up_out[0],
    )
    section = lax.axis_index("section")
    first_result = section == 0
    local = ends_in[0]
    micro_count = local.shape[0]
    rows = local.shape[2]
    width = local.shape[3]
    position = lax.axis_index("seq") * rows + jnp.arange(rows, dtype=jnp.int32)
    dilation_step = jnp.where(first_result, FIRST_DILATION, SECOND_DILATION).astype(jnp.int32)
    receptive_reach = FILTER_TAPS // 2 * SECOND_DILATION
    offsets = [(tap - FILTER_TAPS // 2) * dilation_step for tap in range(FILTER_TAPS)]
    starts = [receptive_reach + offset for offset in offsets]
    back_starts = [receptive_reach - offset for offset in offsets]

    def valid_rows(micro_index):
        index = jnp.clip(micro_index, 0, micro_count - 1)
        item_lengths = lax.dynamic_index_in_dim(lengths, index, 0, keepdims=False)
        return (position[None, :] < item_lengths[:, None]).astype(jnp.float32)[:, :, None]

    received = jnp.zeros(local.shape[1:], jnp.bfloat16)
    inputs_seen = []
    outputs_seen = []
    kept = []
    stats = jnp.zeros((3,), jnp.float32)
    for step in range(micro_count + 1):
        own = local[min(step, micro_count - 1)].astype(jnp.float32)
        input_rows = jnp.where(first_result, own, received.astype(jnp.float32))
        valid_mask = valid_rows(step - section)
        output_rows, branch, wide, saved = forward(input_rows, valid_mask, weights, starts)
        active = jnp.where(first_result, float(step < micro_count), float(step >= 1))
        stats = stats + active * jnp.stack(
            [
                jnp.sum(input_rows * input_rows * valid_mask),
                jnp.sum(branch * branch),
                jnp.sum(valid_mask),
            ]
        )
        inputs_seen.append(input_rows)
        outputs_seen.append(output_rows)
        kept.append(wide)
        if step < micro_count:
            received = passed_along(output_rows.astype(jnp.bfloat16), "section", 1)
    handed_rows = jnp.zeros(local.shape[1:], jnp.bfloat16)
    totals = None
    grads_seen = []
    for step in range(micro_count + 1):
        index = micro_count - step
        input_rows = inputs_seen[index]
        valid_mask = valid_rows(index - section)
        cotangent = local[max(micro_count - 1 - step, 0)].astype(jnp.float32)
        grad_out = jnp.where(first_result, handed_rows.astype(jnp.float32), cotangent)
        output_rows, branch, wide, saved = forward(input_rows, valid_mask, weights, starts)
        grad_inputs, step_grads = backward(grad_out, valid_mask, weights, back_starts, saved)
        active = jnp.where(first_result, float(step >= 1), float(step < micro_count))
        scaled = tuple((active * grad for grad in step_grads))
        if totals is None:
            totals = scaled
        else:
            totals = tuple((total + grad for total, grad in zip(totals, scaled)))
        grads_seen.append(grad_inputs)
        if step < micro_count:
            handed_rows = passed_along(grad_inputs.astype(jnp.bfloat16), "section", -1)
    ends_out = jnp.stack(
        [
            jnp.where(first_result, grads_seen[micro_count - slot], outputs_seen[slot + 1])
            for slot in range(micro_count)
        ]
    )[None]
    summed = lax.psum(
        (totals[0], totals[1], totals[2], totals[3], totals[4], totals[5], totals[6], stats),
        ("dp", "seq"),
    )
    sums = summed[7]
    rms = jnp.sqrt(sums[:2] / (sums[2] * width))[None]
    return (
        ends_out,
        summed[0][None],
        summed[1][None],
        summed[2][None],
        summed[3][None],
        summed[4][None],
        summed[5][None],
        summed[6][None],
        rms,
    )


def solution(mesh):
    in_specs = (
        P("section", None, "dp", "seq", None),
        P(None, "dp"),
        P("section", None),
        P("section", None, None),
        P("section", None, None),
        P("section", None, None),
        P("section", None, None),
        P("section", None, None, None),
        P("section", None, None),
    )
    out_specs = (
        P("section", None, "dp", "seq", None),
        P("section", None),
        P("section", None, None),
        P("section", None, None),
        P("section", None, None),
        P("section", None, None),
        P("section", None, None, None),
        P("section", None, None),
        P("section", None),
    )
    return jax.shard_map(body, mesh=mesh, in_specs=in_specs, out_specs=out_specs, check_vma=False)
```

profile of v0, /device:TPU:0, one launch (start us, length us, event | category | flops | bytes accessed | tf_op | source)
XLA Modules:
  0.0 743.8 jit_solution(3475327615980546990)
XLA Ops:
  10.7 2.8 fusion.452
  16.8 6.3 collective-permute-start
  23.1 5.1 collective-permute-done.1
  42.3 5.2 collective-permute-start.3
  47.5 6.3 collective-permute-done.4
  57.8 2.1 fusion.343
  66.8 5.0 collective-permute-start.6
  71.9 6.3 collective-permute-done.7
  82.2 2.1 fusion.344
  91.2 5.0 collective-permute-start.9
  96.3 6.3 collective-permute-done.10
  106.6 2.1 fusion.345
  115.9 5.7 collective-permute-start.12
  121.6 7.8 %copy.24 = bf16[1,5,640,640]{2,3,1,0:T(8,128)(2,1)} copy(bf16[1,5,640,640]{3,2,1,0:T(8,128)(2,1)} %param.16) | data formatting | bytes 8192000 | tf_op args[7]
  129.5 3.7 copy.29
  133.1 3.7 copy.28
  136.8 3.7 copy.27
  140.5 3.7 copy.26
  148.2 2.3 multiply_reduce_fusion.29
  152.3 5.4 collective-permute-start.14
  157.7 3.7 copy.25
  161.4 3.0 fusion.353
  171.3 2.6 multiply_reduce_fusion.1
  182.9 4.6 collective-permute-start.17
  187.5 4.6 fusion.351
  199.9 2.5 multiply_reduce_fusion.11
  211.9 5.0 collective-permute-start.20
  216.9 4.6 fusion.349
  229.2 2.5 multiply_reduce_fusion.10
  241.6 5.0 collective-permute-start.23
  246.6 4.8 fusion.347
  258.9 2.4 multiply_reduce_fusion.9
  265.7 2.8 convolution_add_fusion
  268.4 3.1 convolution_add_fusion.3
  274.5 6.0 collective-permute-start.26
  280.4 13.9 %add_bitcast_fusion = f32[1,5,640,640]{3,2,1,0:T(8,128)} fusion(f32[5,640,640]{2,1,0:T(8,128)} %fusion.347, f32[5,640,640]{2,1,0:T(8,128)} %fusion.349, f32[5,640,640]{2,1,0:T(8,128)} %fusion.351, f32[5,640,640]{2,1,0:T(8,128)S(1)} %fusion.353, f32[]{:T(128)S(6)} %select_n.262, f32[]{:T(128)S(6)} %select_n.261, bf16[5,640,256]{2,1,0:T(8,128)(2,1)} %bitcast.708, ...), kind=kOutput, calls=%fused_computation | convolution fusion | flops 1060864000 | bytes 42926088 | tf_op jit(solution)/shard_map/brk,bro->ko/dot_general | solution.py:108
  294.3 5.1 fusion.3
  305.3 3.0 fusion.2
  313.5 2.4 multiply_reduce_fusion.6
  315.9 2.4 multiply_reduce_fusion.4
  318.4 2.4 multiply_reduce_fusion.2
  324.7 9.5 %fusion.395 = f32[3]{0:T(128)S(1)} fusion(f32[1]{0:T(128)} %bitcast.98, f32[1]{0:T(128)} %bitcast.97, f32[1]{0:T(128)} %bitcast.96, f32[1]{0:T(128)} %bitcast.101, f32[1]{0:T(128)} %bitcast.100, f32[1]{0:T(128)} %bitcast.99, f32[1]{0:T(128)} %bitcast.95, f32[1]{0:T(128)} %bitcast.94, f32[1]{0:T(128)} %bitcast.93, f32[1]{0:T(128)} %bitcast.92, ...), kind=kLoop, calls=%fused_computation.648 | loop fusion | flops 48 | bytes 80 | tf_op jit(solution)/shard_map/add | solution.py:189
  337.5 82.4 %all-reduce = (f32[1,1280]{1,0:T(1,128)}, f32[1,2,640]{2,1,0:T(2,128)}, f32[1,2,1280]{2,1,0:T(2,128)}, f32[1,4,640]{2,1,0:T(4,128)}, f32[3]{0:T(128)S(1)}) all-reduce(f32[1,1280]{1,0:T(1,128)S(1)} %broadcast_in_dim.109, f32[1,2,640]{2,1,0:T(2,128)S(1)} %fusion.377, ...), channel_id=1, replica_groups=mesh['section'=2,'dp'=4,'seq'=4] {'dp','seq'}, use_global_device_ids=true, to_apply=%region_65.66 | all-reduce | flops 7683 | bytes 61464 | tf_op jit(solution)/shard_map/psum | solution.py:227
  421.7 3.2 fusion.140
  425.1 2.8 maximum_bitcast_fusion
  427.9 295.7 %all-reduce.4.cloned.1.call-done = (f32[1,1280,640]{2,1,0:T(8,128)}, f32[1,5,640,640]{3,2,1,0:T(8,128)}, f32[1,640,1280]{2,1,0:T(8,128)}) async-done(((f32[1,1280,640]{2,1,0:T(8,128)}, f32[1,5,640,640]{3,2,1,0:T(8,128)}, f32[1,640,1280]{2,1,0:T(8,128)}), (f32[1,1280,640]{2,1,0:T(8,128)}, f32[1,5,640,640]{3,2,1,0:T(8,128)}, f32[1,640,1280]{2,1,0:T(8,128)})) %all-reduce.4.cloned.1.call-update) | async-done | bytes 14745616 | tf_op jit(solution)/shard_map/psum | solution.py:227
  723.6 3.8 copy.74
  727.4 7.3 copy.75
  (486 shorter events, 145.1 us)
Async XLA Ops:
  7.2 26.3 %copy-start = (bf16[1,640,1280]{2,1,0:T(8,128)(2,1)S(1)}, bf16[1,640,1280]{2,1,0:T(8,128)(2,1)}, u32[]{:S(2)}) copy-start(bf16[1,640,1280]{2,1,0:T(8,128)(2,1)} %param.17) | copy-start | bytes 4915204
  7.2 716.4 %all-reduce.4.cloned.1.call-start = ((), (), s32[]{:S(2)}) async-start(), calls=%async_computation | async-start | bytes 29491200 | tf_op jit(solution)/shard_map/psum | solution.py:227
  13.5 17.3 %copy-start.16 = (f32[256,640]{1,0:T(8,128)}, f32[256,640]{1,0:T(8,128)S(1)}, u32[]{:S(2)}) copy-start(f32[256,640]{1,0:T(8,128)S(1)} %get-tuple-element.150) | copy-start | bytes 1966084
  13.5 17.3 %copy-start.70 = (f32[256]{0:T(256)}, f32[256]{0:T(256)S(1)}, u32[]{:S(2)}) copy-start(f32[256]{0:T(256)S(1)} %broadcast_multiply_fusion.9) | copy-start | bytes 3076
  13.7 17.1 %copy-start.74 = (f32[256]{0:T(256)}, f32[256]{0:T(256)S(1)}, u32[]{:S(2)}) copy-start(f32[256]{0:T(256)S(1)} %fusion.379) | copy-start | bytes 3076
  15.5 12.6 %collective-permute-start.1 = (bf16[1,256,640]{2,1,0:T(8,128)(2,1)S(1)}, bf16[1,256,640]{2,1,0:T(8,128)(2,1)S(1)}, u32[]{:S(2)}, u32[]{:S(2)}) collective-permute-start(bf16[1,256,640]{2,1,0:T(8,128)(2,1)S(1)} %fusion.355), channel_id=1, source_target_pairs={{1,0},{2,1},{3,2},{5,4},{6,5},{7,6},{9,8},{10,9},{11,10},{13,12},{... | collective-permute-start | bytes 983048 | tf_op jit(solution)/shard_map/ppermute | solution.py:14
  16.8 12.5 %collective-permute-start = (bf16[1,256,640]{2,1,0:T(8,128)(2,1)S(1)}, bf16[1,256,640]{2,1,0:T(8,128)(2,1)}, u32[]{:S(2)}, u32[]{:S(2)}) collective-permute-start(bf16[1,256,640]{2,1,0:T(8,128)(2,1)S(1)} %fusion.355), channel_id=1, source_target_pairs={{0,1},{1,2},{2,3},{4,5},{5,6},{6,7},{8,9},{9,10},{10,11},{12,13},{... | collective-permute-start | bytes 983048 | tf_op jit(solution)/shard_map/ppermute | solution.py:14
  35.5 3.0 collective-permute-start.2
  38.5 19.3 %copy-start.4 = (bf16[1,256,1280]{2,1,0:T(8,128)(2,1)}, bf16[1,256,1280]{2,1,0:T(8,128)(2,1)S(1)}, u32[]{:S(2)}) copy-start(bf16[1,256,1280]{2,1,0:T(8,128)(2,1)S(1)} %collective-permute-done.2) | copy-start | bytes 1966084
  40.3 14.9 %copy-start.18 = (f32[256,640]{1,0:T(8,128)}, f32[256,640]{1,0:T(8,128)S(1)}, u32[]{:S(2)}) copy-start(f32[256,640]{1,0:T(8,128)S(1)} %get-tuple-element.154) | copy-start | bytes 1966084
  41.0 12.7 %collective-permute-start.4 = (bf16[1,256,640]{2,1,0:T(8,128)(2,1)S(1)}, bf16[1,256,640]{2,1,0:T(8,128)(2,1)S(1)}, u32[]{:S(2)}, u32[]{:S(2)}) collective-permute-start(bf16[1,256,640]{2,1,0:T(8,128)(2,1)S(1)} %fusion.356), channel_id=1, source_target_pairs={{1,0},{2,1},{3,2},{5,4},{6,5},{7,6},{9,8},{10,9},{11,10},{13,12},{... | collective-permute-start | bytes 983048 | tf_op jit(solution)/shard_map/ppermute | solution.py:14
  42.3 12.6 %collective-permute-start.3 = (bf16[1,256,640]{2,1,0:T(8,128)(2,1)S(1)}, bf16[1,256,640]{2,1,0:T(8,128)(2,1)S(1)}, u32[]{:S(2)}, u32[]{:S(2)}) collective-permute-start(bf16[1,256,640]{2,1,0:T(8,128)(2,1)S(1)} %fusion.356), channel_id=1, source_target_pairs={{0,1},{1,2},{2,3},{4,5},{5,6},{6,7},{8,9},{9,10},{10,11},{12,13},{... | collective-permute-start | bytes 983048 | tf_op jit(solution)/shard_map/ppermute | solution.py:14
  59.9 3.2 collective-permute-start.5
  63.0 19.2 %copy-start.7 = (bf16[1,256,1280]{2,1,0:T(8,128)(2,1)}, bf16[1,256,1280]{2,1,0:T(8,128)(2,1)S(1)}, u32[]{:S(2)}) copy-start(bf16[1,256,1280]{2,1,0:T(8,128)(2,1)S(1)} %collective-permute-done.5) | copy-start | bytes 1966084
  64.8 14.8 %copy-start.20 = (f32[256,640]{1,0:T(8,128)}, f32[256,640]{1,0:T(8,128)S(1)}, u32[]{:S(2)}) copy-start(f32[256,640]{1,0:T(8,128)S(1)} %get-tuple-element.160) | copy-start | bytes 1966084
  65.5 12.6 %collective-permute-start.7 = (bf16[1,256,640]{2,1,0:T(8,128)(2,1)S(1)}, bf16[1,256,640]{2,1,0:T(8,128)(2,1)S(1)}, u32[]{:S(2)}, u32[]{:S(2)}) collective-permute-start(bf16[1,256,640]{2,1,0:T(8,128)(2,1)S(1)} %fusion.357), channel_id=1, source_target_pairs={{1,0},{2,1},{3,2},{5,4},{6,5},{7,6},{9,8},{10,9},{11,10},{13,12},{... | collective-permute-start | bytes 983048 | tf_op jit(solution)/shard_map/ppermute | solution.py:14
  66.8 12.5 %collective-permute-start.6 = (bf16[1,256,640]{2,1,0:T(8,128)(2,1)S(1)}, bf16[1,256,640]{2,1,0:T(8,128)(2,1)S(1)}, u32[]{:S(2)}, u32[]{:S(2)}) collective-permute-start(bf16[1,256,640]{2,1,0:T(8,128)(2,1)S(1)} %fusion.357), channel_id=1, source_target_pairs={{0,1},{1,2},{2,3},{4,5},{5,6},{6,7},{8,9},{9,10},{10,11},{12,13},{... | collective-permute-start | bytes 983048 | tf_op jit(solution)/shard_map/ppermute | solution.py:14
  84.3 3.2 collective-permute-start.8
  87.4 19.2 %copy-start.9 = (bf16[1,256,1280]{2,1,0:T(8,128)(2,1)}, bf16[1,256,1280]{2,1,0:T(8,128)(2,1)S(1)}, u32[]{:S(2)}) copy-start(bf16[1,256,1280]{2,1,0:T(8,128)(2,1)S(1)} %collective-permute-done.8) | copy-start | bytes 1966084
  89.3 14.8 %copy-start.22 = (f32[256,640]{1,0:T(8,128)}, f32[256,640]{1,0:T(8,128)S(1)}, u32[]{:S(2)}) copy-start(f32[256,640]{1,0:T(8,128)S(1)} %get-tuple-element.166) | copy-start | bytes 1966084
  89.9 12.6 %collective-permute-start.10 = (bf16[1,256,640]{2,1,0:T(8,128)(2,1)S(1)}, bf16[1,256,640]{2,1,0:T(8,128)(2,1)S(1)}, u32[]{:S(2)}, u32[]{:S(2)}) collective-permute-start(bf16[1,256,640]{2,1,0:T(8,128)(2,1)S(1)} %fusion.358), channel_id=1, source_target_pairs={{1,0},{2,1},{3,2},{5,4},{6,5},{7,6},{9,8},{10,9},{11,10},{13,12},{... | collective-permute-start | bytes 983048 | tf_op jit(solution)/shard_map/ppermute | solution.py:14
  91.2 12.5 %collective-permute-start.9 = (bf16[1,256,640]{2,1,0:T(8,128)(2,1)S(1)}, bf16[1,256,640]{2,1,0:T(8,128)(2,1)S(1)}, u32[]{:S(2)}, u32[]{:S(2)}) collective-permute-start(bf16[1,256,640]{2,1,0:T(8,128)(2,1)S(1)} %fusion.358), channel_id=1, source_target_pairs={{0,1},{1,2},{2,3},{4,5},{5,6},{6,7},{8,9},{9,10},{10,11},{12,13},{... | collective-permute-start | bytes 983048 | tf_op jit(solution)/shard_map/ppermute | solution.py:14
  108.7 3.2 collective-permute-start.11
  113.9 31.7 %copy-start.24 = (f32[256,640]{1,0:T(8,128)}, f32[256,640]{1,0:T(8,128)S(1)}, u32[]{:S(2)}) copy-start(f32[256,640]{1,0:T(8,128)S(1)} %get-tuple-element.172) | copy-start | bytes 1966084
  114.6 29.6 %collective-permute-start.13 = (bf16[1,256,640]{2,1,0:T(8,128)(2,1)S(1)}, bf16[1,256,640]{2,1,0:T(8,128)(2,1)S(1)}, u32[]{:S(2)}, u32[]{:S(2)}) collective-permute-start(bf16[1,256,640]{2,1,0:T(8,128)(2,1)S(1)} %fusion.359), channel_id=1, source_target_pairs={{1,0},{2,1},{3,2},{5,4},{6,5},{7,6},{9,8},{10,9},{11,10},{13,12},{... | collective-permute-start | bytes 983048 | tf_op jit(solution)/shard_map/ppermute | solution.py:14
  115.9 28.3 %collective-permute-start.12 = (bf16[1,256,640]{2,1,0:T(8,128)(2,1)S(1)}, bf16[1,256,640]{2,1,0:T(8,128)(2,1)}, u32[]{:S(2)}, u32[]{:S(2)}) collective-permute-start(bf16[1,256,640]{2,1,0:T(8,128)(2,1)S(1)} %fusion.359), channel_id=1, source_target_pairs={{0,1},{1,2},{2,3},{4,5},{5,6},{6,7},{8,9},{9,10},{10,11},{12,13},{... | collective-permute-start | bytes 983048 | tf_op jit(solution)/shard_map/ppermute | solution.py:14
  151.0 14.5 %collective-permute-start.15 = (bf16[1,256,640]{2,1,0:T(8,128)(2,1)S(1)}, bf16[1,256,640]{2,1,0:T(8,128)(2,1)}, u32[]{:S(2)}, u32[]{:S(2)}) collective-permute-start(bf16[1,256,640]{2,1,0:T(8,128)(2,1)S(1)} %bitcast.712), channel_id=1, source_target_pairs={{1,0},{2,1},{3,2},{5,4},{6,5},{7,6},{9,8},{10,9},{11,10},{13,12},{... | collective-permute-start | bytes 983048 | tf_op jit(solution)/shard_map/ppermute | solution.py:14
  152.3 13.2 %collective-permute-start.14 = (bf16[1,256,640]{2,1,0:T(8,128)(2,1)S(1)}, bf16[1,256,640]{2,1,0:T(8,128)(2,1)}, u32[]{:S(2)}, u32[]{:S(2)}) collective-permute-start(bf16[1,256,640]{2,1,0:T(8,128)(2,1)S(1)} %bitcast.713), channel_id=1, source_target_pairs={{0,1},{1,2},{2,3},{4,5},{5,6},{6,7},{8,9},{9,10},{10,11},{12,13},{... | collective-permute-start | bytes 983048 | tf_op jit(solution)/shard_map/ppermute | solution.py:14
  175.3 4.5 collective-permute-start.16
  179.8 26.4 %copy-start.42 = (bf16[1,256,1280]{2,1,0:T(8,128)(2,1)}, bf16[1,256,1280]{2,1,0:T(8,128)(2,1)S(1)}, u32[]{:S(2)}) copy-start(bf16[1,256,1280]{2,1,0:T(8,128)(2,1)S(1)} %collective-permute-done.16) | copy-start | bytes 1966084
  181.5 12.4 %collective-permute-start.18 = (bf16[1,256,640]{2,1,0:T(8,128)(2,1)S(1)}, bf16[1,256,640]{2,1,0:T(8,128)(2,1)S(1)}, u32[]{:S(2)}, u32[]{:S(2)}) collective-permute-start(bf16[1,256,640]{2,1,0:T(8,128)(2,1)S(1)} %bitcast.715), channel_id=1, source_target_pairs={{1,0},{2,1},{3,2},{5,4},{6,5},{7,6},{9,8},{10,9},{11,10},{13,12},{... | collective-permute-start | bytes 983048 | tf_op jit(solution)/shard_map/ppermute | solution.py:14
  182.9 12.5 %collective-permute-start.17 = (bf16[1,256,640]{2,1,0:T(8,128)(2,1)S(1)}, bf16[1,256,640]{2,1,0:T(8,128)(2,1)S(1)}, u32[]{:S(2)}, u32[]{:S(2)}) collective-permute-start(bf16[1,256,640]{2,1,0:T(8,128)(2,1)S(1)} %bitcast.716), channel_id=1, source_target_pairs={{0,1},{1,2},{2,3},{4,5},{5,6},{6,7},{8,9},{9,10},{10,11},{12,13},{... | collective-permute-start | bytes 983048 | tf_op jit(solution)/shard_map/ppermute | solution.py:14
  204.5 4.2 collective-permute-start.19
  208.8 27.2 %copy-start.44 = (bf16[1,256,1280]{2,1,0:T(8,128)(2,1)}, bf16[1,256,1280]{2,1,0:T(8,128)(2,1)S(1)}, u32[]{:S(2)}) copy-start(bf16[1,256,1280]{2,1,0:T(8,128)(2,1)S(1)} %collective-permute-done.19) | copy-start | bytes 1966084
  210.4 12.7 %collective-permute-start.21 = (bf16[1,256,640]{2,1,0:T(8,128)(2,1)S(1)}, bf16[1,256,640]{2,1,0:T(8,128)(2,1)S(1)}, u32[]{:S(2)}, u32[]{:S(2)}) collective-permute-start(bf16[1,256,640]{2,1,0:T(8,128)(2,1)S(1)} %bitcast.718), channel_id=1, source_target_pairs={{1,0},{2,1},{3,2},{5,4},{6,5},{7,6},{9,8},{10,9},{11,10},{13,12},{... | collective-permute-start | bytes 983048 | tf_op jit(solution)/shard_map/ppermute | solution.py:14
  211.9 12.9 %collective-permute-start.20 = (bf16[1,256,640]{2,1,0:T(8,128)(2,1)S(1)}, bf16[1,256,640]{2,1,0:T(8,128)(2,1)S(1)}, u32[]{:S(2)}, u32[]{:S(2)}) collective-permute-start(bf16[1,256,640]{2,1,0:T(8,128)(2,1)S(1)} %bitcast.719), channel_id=1, source_target_pairs={{0,1},{1,2},{2,3},{4,5},{5,6},{6,7},{8,9},{9,10},{10,11},{12,13},{... | collective-permute-start | bytes 983048 | tf_op jit(solution)/shard_map/ppermute | solution.py:14
  234.5 4.0 collective-permute-start.22
  238.5 27.1 %copy-start.46 = (bf16[1,256,1280]{2,1,0:T(8,128)(2,1)}, bf16[1,256,1280]{2,1,0:T(8,128)(2,1)S(1)}, u32[]{:S(2)}) copy-start(bf16[1,256,1280]{2,1,0:T(8,128)(2,1)S(1)} %collective-permute-done.22) | copy-start | bytes 1966084
  240.2 12.7 %collective-permute-start.24 = (bf16[1,256,640]{2,1,0:T(8,128)(2,1)S(1)}, bf16[1,256,640]{2,1,0:T(8,128)(2,1)S(1)}, u32[]{:S(2)}, u32[]{:S(2)}) collective-permute-start(bf16[1,256,640]{2,1,0:T(8,128)(2,1)S(1)} %bitcast.721), channel_id=1, source_target_pairs={{1,0},{2,1},{3,2},{5,4},{6,5},{7,6},{9,8},{10,9},{11,10},{13,12},{... | collective-permute-start | bytes 983048 | tf_op jit(solution)/shard_map/ppermute | solution.py:14
  241.6 12.9 %collective-permute-start.23 = (bf16[1,256,640]{2,1,0:T(8,128)(2,1)S(1)}, bf16[1,256,640]{2,1,0:T(8,128)(2,1)S(1)}, u32[]{:S(2)}, u32[]{:S(2)}) collective-permute-start(bf16[1,256,640]{2,1,0:T(8,128)(2,1)S(1)} %bitcast.722), channel_id=1, source_target_pairs={{0,1},{1,2},{2,3},{4,5},{5,6},{6,7},{8,9},{9,10},{10,11},{12,13},{... | collective-permute-start | bytes 983048 | tf_op jit(solution)/shard_map/ppermute | solution.py:14
  258.1 10.3 %copy-start.38 = (f32[256,640]{1,0:T(8,128)}, f32[256,640]{1,0:T(8,128)S(1)}, u32[]{:S(2)}) copy-start(f32[256,640]{1,0:T(8,128)S(1)} %get-tuple-element.107) | copy-start | bytes 1966084
  264.4 7.2 collective-permute-start.25
  273.2 26.2 %collective-permute-start.27 = (bf16[1,256,640]{2,1,0:T(8,128)(2,1)S(1)}, bf16[1,256,640]{2,1,0:T(8,128)(2,1)}, u32[]{:S(2)}, u32[]{:S(2)}) collective-permute-start(bf16[1,256,640]{2,1,0:T(8,128)(2,1)S(1)} %bitcast.709), channel_id=1, source_target_pairs={{1,0},{2,1},{3,2},{5,4},{6,5},{7,6},{9,8},{10,9},{11,10},{13,12},{... | collective-permute-start | bytes 983048 | tf_op jit(solution)/shard_map/ppermute | solution.py:14
  274.5 24.9 %collective-permute-start.26 = (bf16[1,256,640]{2,1,0:T(8,128)(2,1)S(1)}, bf16[1,256,640]{2,1,0:T(8,128)(2,1)}, u32[]{:S(2)}, u32[]{:S(2)}) collective-permute-start(bf16[1,256,640]{2,1,0:T(8,128)(2,1)S(1)} %bitcast.710), channel_id=1, source_target_pairs={{0,1},{1,2},{2,3},{4,5},{5,6},{6,7},{8,9},{9,10},{10,11},{12,13},{... | collective-permute-start | bytes 983048 | tf_op jit(solution)/shard_map/ppermute | solution.py:14
  308.4 14.5 %copy-start.47 = (bf16[1,256,1280]{2,1,0:T(8,128)(2,1)S(1)}, bf16[1,256,1280]{2,1,0:T(8,128)(2,1)}, u32[]{:S(2)}) copy-start(bf16[1,256,1280]{2,1,0:T(8,128)(2,1)} %copy-done.46) | copy-start | bytes 1966084
  322.9 11.3 %copy-start.62 = (f32[256,640]{1,0:T(8,128)S(1)}, f32[256,640]{1,0:T(8,128)}, u32[]{:S(2)}) copy-start(f32[256,640]{1,0:T(8,128)} %copy-done.61) | copy-start | bytes 1966084
  322.9 11.4 %copy-start.89 = (bf16[1,1280,640]{2,1,0:T(8,128)(2,1)S(1)}, bf16[1,1280,640]{2,1,0:T(8,128)(2,1)}, u32[]{:S(2)}) copy-start(bf16[1,1280,640]{2,1,0:T(8,128)(2,1)} %param.15) | copy-start | bytes 4915204
  336.0 85.6 %copy-start.6 = (bf16[1,256,1280]{2,1,0:T(8,128)(2,1)S(1)}, bf16[1,256,1280]{2,1,0:T(8,128)(2,1)}, u32[]{:S(2)}) copy-start(bf16[1,256,1280]{2,1,0:T(8,128)(2,1)} %copy-done.4) | copy-start | bytes 1966084
  (71 other events, 207.4 us)
Sparse Core Ops, SparseCore 0:
  308.5 415.0 all-reduce.3
where the time goes:
time: 754 us; the launch traced here: 744 us
  waiting for transfers between devices  338 us (45%)
  matrix products  106 us (14%)
  blocking collectives  82.4 us (11%)
  starting transfers between devices  79 us (10%)
  other arithmetic  65.4 us (9%)
  local copies, waits for them, and re-layouts  56.4 us (7%)
  between operations  17.3 us (2%)
    psum x1, waiting for transfers between devices, body(): lax.psum((totals[0], totals[1], totals[2], totals[3], totals[4], totals[5...  296 us
    psum x1, blocking collectives, body(): lax.psum((totals[0], totals[1], totals[2], totals[3], totals[4], totals[5...  82.4 us
    ppermute x28, starting transfers between devices, passed_along(): lax.ppermute(value, axis, [(source, source + steps) for source in range(l...  79 us
    ppermute x28, waiting for transfers between devices, passed_along(): lax.ppermute(value, axis, [(source, source + steps) for source in range(l...  41.8 us
    unnamed x219, local copies, waits for them, and re-layouts  35.4 us
    dot_general x5, matrix products, backward(): jnp.einsum('brk,bro->ko', taps, low_conv, preferred_element_type=jnp.floa...  30.9 us
    dot_general x5, local copies, waits for them, and re-layouts, backward(): jnp.einsum('brk,bro->ko', taps, low_conv, preferred_element_type=jnp.floa...  18.4 us
  transfers between devices with their start and end apart: 29, of which 19 were waited for; matrix products, arithmetic and copies ran while one was open for 15% of the time, Pallas kernels for 0%

commit v1 on v0

--- a/solution.py
+++ b/solution.py
@@ -1,7 +1,394 @@
+import functools
+
 import jax
 import jax.numpy as jnp
 from jax import lax
+from jax.experimental import pallas as pl
+from jax.experimental.pallas import tpu as pltpu
 from jax.sharding import PartitionSpec as P
+
+MESH = pl.DeviceIdType.MESH
+BF = jnp.bfloat16
+F32 = jnp.float32
+GROUPS = 9
+BLOCK = 640
+LROWS = 384
+ZROWS = 256
+CH = ZROWS // 4
+KINDS = ["ru", "rv", "za", "zb", "zc", "av", "au", "ze", "zm", "zo", "ex", "ey", "ge", "gm", "go"]
+SKINDS = ["sx", "sy", "sa", "sb", "sc"]
+
+
+class Reduce:
+    def __init__(self, grad, res, r, sm, send, recv, ssend, srecv):
+        self.grad, self.res, self.r, self.sm = grad, res, r, sm
+        self.send, self.recv, self.ssend, self.srecv = send, recv, ssend, srecv
+        self.c = lax.axis_index("section")
+        self.dp = lax.axis_index("dp")
+        self.z = lax.axis_index("seq")
+        self.x = lax.rem(self.dp, 2)
+        self.y = self.dp // 2
+        z = self.z
+        self.end = jnp.logical_or(z == 0, z == 3)
+        self.mid = jnp.logical_not(self.end)
+        self.up = z // 2
+        self.px = (self.c, self.dp + 1 - 2 * self.x, z)
+        self.py = (self.c, lax.rem(self.dp + 2, 4), z)
+        self.pair = (self.c, self.dp, 1 - z + 4 * self.up)
+        self.other = (self.c, self.dp, jnp.clip(3 - z, 1, 2))
+
+    def copy(self, kind, g, src, dst, to):
+        j = KINDS.index(kind)
+        return pltpu.make_async_remote_copy(
+            src_ref=src, dst_ref=dst, send_sem=self.send.at[g, j], recv_sem=self.recv.at[g, j],
+            device_id=to, device_id_type=MESH)
+
+    def scopy(self, kind, src, dst, to):
+        j = SKINDS.index(kind)
+        return pltpu.make_async_remote_copy(
+            src_ref=src, dst_ref=dst, send_sem=self.ssend.at[j], recv_sem=self.srecv.at[j],
+            device_id=to, device_id_type=MESH)
+
+    def rows(self, ref, off, n):
+        if not isinstance(off, int):
+            off = pl.multiple_of(off, 16)
+        return ref.at[pl.ds(off, n)]
+
+    def add(self, dst, doff, srcs, n, tile=32):
+        def body(i, carry):
+            o = i * tile
+            acc = None
+            for ref, off in srcs:
+                v = ref[pl.ds(pl.multiple_of(off + o, 16), tile), :]
+                if len(srcs) > 2:
+                    v = v.astype(F32)
+                acc = v if acc is None else acc + v
+            dst[pl.ds(pl.multiple_of(doff + o, 16), tile), :] = acc.astype(BF)
+            return carry
+        lax.fori_loop(0, n // tile, body, 0, unroll=True)
+
+    def lgeo(self, g):
+        b = g * BLOCK
+        if g % 2 == 0:
+            u, v, pu, pv = self.x, self.y, self.px, self.py
+        else:
+            u, v, pu, pv = self.y, self.x, self.py, self.px
+        h, q = LROWS // 2, LROWS // 4
+        return b, h, q, u, v, pu, pv
+
+    def lcopies(self, g):
+        b, h, q, u, v, pu, pv = self.lgeo(g)
+        own_h = b + u * h
+        own_q = own_h + v * q
+        oth_q = own_h + (1 - v) * q
+        G, R = self.grad, self.res
+        rows = self.rows
+        r = self.r
+        qq = rows(R, own_q, q)
+        return dict(
+            ru=self.copy("ru", g, rows(G, b + (1 - u) * h, h), r["ru"].at[g], pu),
+            rv=self.copy("rv", g, rows(G, oth_q, q), r["rv"].at[g], pv),
+            za=self.copy("za", g, rows(G, own_q, q), r["za"].at[g], self.pair),
+            zb=self.copy("zb", g, rows(G, own_q, q), r["zb"].at[g], self.other),
+            zc=self.copy("zc", g, qq, qq, self.pair),
+            av=self.copy("av", g, qq, qq, pv),
+            au=self.copy("au", g, rows(R, own_h, h), rows(R, own_h, h), pu),
+        )
+
+    def L(self, g, level):
+        b, h, q, u, v, pu, pv = self.lgeo(g)
+        own_h = b + u * h
+        own_q = own_h + v * q
+        oth_q = own_h + (1 - v) * q
+        c = self.lcopies(g)
+        r = self.r
+        G, R = self.grad, self.res
+        if level == 0:
+            c["ru"].start()
+        elif level == 1:
+            c["ru"].wait_recv()
+            self.add(G, oth_q, [(G, oth_q), (r["ru"].at[g], (1 - v) * q)], q)
+            c["rv"].start()
+            self.add(G, own_q, [(G, own_q), (r["ru"].at[g], v * q)], q)
+        elif level == 2:
+            c["rv"].wait_recv()
+            self.add(G, own_q, [(G, own_q), (r["rv"].at[g], 0)], q)
+            pl.when(self.end)(c["za"].start)
+        elif level == 3:
+            @pl.when(self.mid)
+            def _():
+                c["za"].wait_recv()
+                self.add(G, own_q, [(G, own_q), (r["za"].at[g], 0)], q)
+                c["zb"].start()
+        elif level == 4:
+            @pl.when(self.mid)
+            def _():
+                c["zb"].wait_recv()
+                self.add(R, own_q, [(G, own_q), (r["zb"].at[g], 0)], q)
+                c["zc"].start()
+                c["av"].start()
+        elif level == 5:
+            @pl.when(self.end)
+            def _():
+                c["zc"].wait_recv()
+                c["av"].start()
+        elif level == 6:
+            c["av"].wait_recv()
+            c["au"].start()
+        elif level == 7:
+            c["au"].wait_recv()
+
+    def zcopies(self, g):
+        zb = g * BLOCK + LROWS
+        z, up = self.z, self.up
+        G, R, r, rows = self.grad, self.res, self.r, self.rows
+        e_off = zb + CH * (1 - up)
+        m_off = zb + 2 * CH * (1 - up)
+        p_off = zb + 2 * CH * up
+        o_off = zb + 3 * CH * up
+        own = zb + CH * z
+        return dict(
+            ze=self.copy("ze", g, rows(G, e_off, 3 * CH), r["ze"].at[g], self.pair),
+            zm=self.copy("zm", g, rows(G, m_off, 2 * CH), r["zm"].at[g], self.other),
+            zo=self.copy("zo", g, rows(G, o_off, CH), r["zo"].at[g], self.pair),
+            ex=self.copy("ex", g, rows(G, own, CH), r["ex"].at[g], self.px),
+            ey=self.copy("ey", g, r["tx"].at[g], r["ey"].at[g], self.py),
+            ge=self.copy("ge", g, rows(R, own, CH), rows(R, own, CH), self.pair),
+            gm=self.copy("gm", g, rows(R, p_off, 2 * CH), rows(R, p_off, 2 * CH), self.other),
+            go=self.copy("go", g, rows(R, e_off, 3 * CH), rows(R, e_off, 3 * CH), self.pair),
+        ), zb, e_off, m_off, p_off, o_off, own
+
+    def Z(self, g, level):
+        c, zb, e_off, m_off, p_off, o_off, own = self.zcopies(g)
+        z, up = self.z, self.up
+        G, R, r = self.grad, self.res, self.r
+        if level == 0:
+            pl.when(self.end)(c["ze"].start)
+        elif level == 1:
+            @pl.when(self.mid)
+            def _():
+                c["ze"].wait_recv()
+                self.add(G, m_off, [(G, m_off), (r["ze"].at[g], m_off - e_off)], 2 * CH)
+                c["zm"].start()
+        elif level == 2:
+            @pl.when(self.mid)
+            def _():
+                c["zm"].wait_recv()
+                self.add(G, o_off, [(G, o_off), (r["zm"].at[g], o_off - p_off)], CH)
+                c["zo"].start()
+                self.add(G, own, [(G, own), (r["ze"].at[g], own - e_off), (r["zm"].at[g], own - p_off)], CH)
+                c["ex"].start()
+        elif level == 3:
+            @pl.when(self.end)
+            def _():
+                c["zo"].wait_recv()
+                self.add(G, own, [(G, own), (r["zo"].at[g], 0)], CH)
+                c["ex"].start()
+        elif level == 4:
+            c["ex"].wait_recv()
+            self.add(r["tx"].at[g], 0, [(G, own), (r["ex"].at[g], 0)], CH)
+            c["ey"].start()
+        elif level == 5:
+            c["ey"].wait_recv()
+            self.add(R, own, [(r["tx"].at[g], 0), (r["ey"].at[g], 0)], CH)
+            pl.when(self.end)(c["ge"].start)
+        elif level == 6:
+            @pl.when(self.mid)
+            def _():
+                c["ge"].wait_recv()
+                c["gm"].start()
+        elif level == 7:
+            @pl.when(self.mid)
+            def _():
+                c["gm"].wait_recv()
+                c["go"].start()
+        elif level == 8:
+            pl.when(self.end)(c["go"].wait_recv)
+
+    def scopies(self):
+        s = self.sm
+        return dict(
+            sx=self.scopy("sx", s.at[0], s.at[5], self.px),
+            sy=self.scopy("sy", s.at[1], s.at[6], self.py),
+            sa=self.scopy("sa", s.at[2], s.at[7], self.pair),
+            sb=self.scopy("sb", s.at[3], s.at[8], self.other),
+            sc=self.scopy("sc", s.at[4], s.at[4], self.pair),
+        )
+
+    def S(self, level):
+        c = self.scopies()
+        s = self.sm
+        if level == 0:
+            c["sx"].start()
+        elif level == 1:
+            c["sx"].wait_recv()
+            s[1] = s[0] + s[5]
+            c["sy"].start()
+        elif level == 2:
+            c["sy"].wait_recv()
+            s[2] = s[1] + s[6]
+            pl.when(self.end)(c["sa"].start)
+        elif level == 3:
+            @pl.when(self.mid)
+            def _():
+                c["sa"].wait_recv()
+                s[3] = s[2] + s[7]
+                c["sb"].start()
+        elif level == 4:
+            @pl.when(self.mid)
+            def _():
+                c["sb"].wait_recv()
+                s[4] = s[3] + s[8]
+                c["sc"].start()
+        elif level == 5:
+            pl.when(self.end)(c["sc"].wait_recv)
+
+    def drain(self, groups=GROUPS):
+        for g in range(groups):
+            c = dict(self.lcopies(g))
+            c.update(self.zcopies(g)[0])
+            for k in ("ru", "rv", "av", "au", "ex", "ey"):
+                c[k].wait_send()
+
+            @pl.when(self.end)
+            def _():
+                for k in ("za", "ze", "ge"):
+                    c[k].wait_send()
+
+            @pl.when(self.mid)
+            def _():
+                for k in ("zb", "zc", "zm", "zo", "gm", "go"):
+                    c[k].wait_send()
+        c = self.scopies()
+        c["sx"].wait_send()
+        c["sy"].wait_send()
+        pl.when(self.end)(c["sa"].wait_send)
+
+        @pl.when(self.mid)
+        def _():
+            c["sb"].wait_send()
+            c["sc"].wait_send()
+
+
+def schedule(gap, hl, hz=None, oz=0.0, old=1):
+    hz = hl if hz is None else hz
+    ops = []
+    for g in range(GROUPS):
+        for lv in range(8):
+            ops.append((gap * g + hl * lv, old * g, 0, g, "L", lv))
+        for lv in range(9):
+            ops.append((gap * g + oz + hz * lv, old * g, 1, g, "Z", lv))
+    return [(t, p, g, k, lv) for t, _, p, g, k, lv in sorted(ops)]
+
+
+def scratch():
+    q, h = LROWS // 4, LROWS // 2
+    n = GROUPS
+    v = lambda rows: pltpu.VMEM((n, rows, BLOCK), BF)
+    bufs = dict(ru=v(h), rv=v(q), za=v(q), zb=v(q), ze=v(3 * CH), zm=v(2 * CH), zo=v(CH), ex=v(CH), ey=v(CH), tx=v(CH))
+    sems = [pltpu.SemaphoreType.DMA((n, len(KINDS))), pltpu.SemaphoreType.DMA((n, len(KINDS))),
+            pltpu.SemaphoreType.DMA((len(SKINDS),)), pltpu.SemaphoreType.DMA((len(SKINDS),))]
+    return bufs, sems
+
+
+def reduce_kernel(names, ops, g_hbm, s_hbm, o_hbm, so_hbm, grad, res, sm, *rest):
+    count = len(names)
+    r = dict(zip(names, rest[:count]))
+    send, recv, ssend, srecv, lsem = rest[count:]
+    red = Reduce(grad, res, r, sm, send, recv, ssend, srecv)
+    load = pltpu.make_async_copy(g_hbm, grad, lsem.at[0])
+    load.start()
+    load_small = pltpu.make_async_copy(s_hbm, sm.at[0], lsem.at[1])
+    load_small.start()
+    barrier = pltpu.get_barrier_semaphore()
+    for to in (red.px, red.py, red.pair):
+        pl.semaphore_signal(barrier, inc=1, device_id=to, device_id_type=MESH)
+
+    @pl.when(red.mid)
+    def _():
+        pl.semaphore_signal(barrier, inc=1, device_id=red.other, device_id_type=MESH)
+        pl.semaphore_wait(barrier, 4)
+
+    pl.when(red.end)(lambda: pl.semaphore_wait(barrier, 3))
+    load.wait()
+    load_small.wait()
+    for _, _, g, kind, level in ops:
+        if kind == "L":
+            red.L(g, level)
+            if g == GROUPS - 1 and level < 6:
+                red.S(level)
+        else:
+            red.Z(g, level)
+    red.drain()
+    store = pltpu.make_async_copy(res, o_hbm, lsem.at[2])
+    store.start()
+    store_small = pltpu.make_async_copy(sm.at[4], so_hbm, lsem.at[3])
+    store_small.start()
+    store.wait()
+    store_small.wait()
+
+
+def all_sum(rows, small):
+    bufs, sems = scratch()
+    names = list(bufs)
+    total = GROUPS * BLOCK
+    return pl.pallas_call(
+        functools.partial(reduce_kernel, names, schedule(1.0, 1.0)),
+        name="weight_sums",
+        out_shape=(
+            jax.ShapeDtypeStruct((total, BLOCK), BF),
+            jax.ShapeDtypeStruct((16, BLOCK), F32),
+        ),
+        in_specs=[pl.BlockSpec(memory_space=pl.ANY)] * 2,
+        out_specs=[pl.BlockSpec(memory_space=pl.ANY)] * 2,
+        scratch_shapes=[
+            pltpu.VMEM((total, BLOCK), BF),
+            pltpu.VMEM((total, BLOCK), BF),
+            pltpu.VMEM((9, 16, BLOCK), F32),
+        ]
+        + [bufs[k] for k in names]
+        + sems
+        + [pltpu.SemaphoreType.DMA((4,))],
+        compiler_params=pltpu.CompilerParams(
+            collective_id=1, has_side_effects=True, vmem_limit_bytes=48 * 2**20
+        ),
+    )(rows, small)
+
+
+def summed_over_items(totals, stats):
+    if (lax.axis_size("dp"), lax.axis_size("seq")) != (4, 4):
+        return lax.psum((*totals, stats), ("dp", "seq"))
+    outer_gain, inner_gains, outer_biases, inner_biases, down, conv, up = totals
+    rows = jnp.concatenate(
+        [up[:, :BLOCK], up[:, BLOCK:], conv.reshape(-1, BLOCK), down], axis=0
+    ).astype(BF)
+    small = jnp.concatenate(
+        [
+            outer_gain.reshape(-1, BLOCK),
+            inner_gains,
+            outer_biases.reshape(-1, BLOCK),
+            inner_biases,
+            jnp.pad(stats[None], ((0, 0), (0, BLOCK - 3))),
+        ],
+        axis=0,
+    )
+    used = small.shape[0]
+    small = jnp.pad(small, ((0, 16 - used), (0, 0)))
+    rows, small = all_sum(rows, small)
+    up = jnp.concatenate([rows[:BLOCK], rows[BLOCK : 2 * BLOCK]], axis=1).astype(F32)
+    conv = rows[2 * BLOCK : 7 * BLOCK].reshape(5, BLOCK, BLOCK).astype(F32)
+    down = rows[7 * BLOCK :].astype(F32)
+    return (
+        small[0:2].reshape(-1),
+        small[2:4],
+        small[4:8].reshape(2, -1),
+        small[8:12],
+        down,
+        conv,
+        up,
+        small[12, :3],
+    )
+
 
 FILTER_TAPS = 5
 FIRST_DILATION = 2
@@ -224,10 +611,7 @@
             for slot in range(micro_count)
         ]
     )[None]
-    summed = lax.psum(
-        (totals[0], totals[1], totals[2], totals[3], totals[4], totals[5], totals[6], stats),
-        ("dp", "seq"),
-    )
+    summed = summed_over_items(totals, stats)
     sums = summed[7]
     rms = jnp.sqrt(sums[:2] / (sums[2] * width))[None]
     return (

time: 754 us -> 542 us (0.72)
  waiting for transfers between devices: 338 us -> 40.9 us
  Pallas kernels: 0 us -> 141 us
  blocking collectives: 82.4 us -> 0 us
  other arithmetic: 65.4 us -> 101 us
  between operations: 17.3 us -> 3.87 us
    psum x1 -> x0, waiting for transfers between devices: 296 us -> none  [body(): lax.psum((totals[0], totals[1], totals[2], totals[3], totals[4], totals[5...]
    pallas_call x0 -> x1, Pallas kernels: none -> 141 us  [all_sum(): pl.pallas_call(functools.partial(reduce_kernel, names, schedule(1.0, 1.0)...]
    psum x1 -> x0, blocking collectives: 82.4 us -> none  [body(): lax.psum((totals[0], totals[1], totals[2], totals[3], totals[4], totals[5...]
    concatenate x0 -> x1, other arithmetic: none -> 20.7 us  [summed_over_items(): jnp.concatenate([up[:, :BLOCK], up[:, BLOCK:], conv.reshape(-1, BLOCK), d...]
    unnamed x219 -> x195, local copies, waits for them, and re-layouts: 35.4 us -> 25.6 us
    convert_element_type x0 -> x2, other arithmetic: none -> 8.15 us  [the longest x1 6.2 us: summed_over_items(): conv = rows[2 * BLOCK:7 * BLOCK].reshape(5, BLOCK, BLOCK).astype(F32)]
  transfers between devices with their start and end apart: 29 -> 28, of which waited for: 19 -> 17; matrix products, arithmetic and copies ran while one was open for 15% -> 20% of each run, Pallas kernels for 0% -> 0%
where the time goes in v1:
time: 542 us; the launch traced here: 531 us
  Pallas kernels  141 us (26%)
  matrix products  110 us (20%)
  other arithmetic  101 us (19%)
  starting transfers between devices  78.9 us (15%)
  local copies, waits for them, and re-layouts  54.6 us (10%)
  waiting for transfers between devices  40.9 us (8%)
    pallas_call x1, Pallas kernels, all_sum(): pl.pallas_call(functools.partial(reduce_kernel, names, schedule(1.0, 1.0)...  141 us
    ppermute x28, starting transfers between devices, passed_along(): lax.ppermute(value, axis, [(source, source + steps) for source in range(l...  78.9 us
    ppermute x28, waiting for transfers between devices, passed_along(): lax.ppermute(value, axis, [(source, source + steps) for source in range(l...  40.9 us
    dot_general x5, matrix products, backward(): jnp.einsum('brk,bro->ko', taps, low_conv, preferred_element_type=jnp.floa...  35.2 us
    unnamed x195, local copies, waits for them, and re-layouts  25.6 us
    concatenate x1, other arithmetic, summed_over_items(): jnp.concatenate([up[:, :BLOCK], up[:, BLOCK:], conv.reshape(-1, BLOCK), d...  20.7 us
    dot_general x5, local copies, waits for them, and re-layouts, backward(): jnp.einsum('brk,bro->ko', taps, low_conv, preferred_element_type=jnp.floa...  18.4 us
    dot_general x5, matrix products, backward(): jnp.einsum('bri,di->brd', low_proj, weight_in, preferred_element_type=jnp...  14.1 us
  transfers between devices with their start and end apart: 28, of which 17 were waited for; matrix products, arithmetic and copies ran while one was open for 20% of the time, Pallas kernels for 0%

profile of v1, /device:TPU:0, one launch (start us, length us, event | category | flops | bytes accessed | tf_op | source)
XLA Modules:
  0.0 531.1 jit_solution(3433871219206490695)
XLA Ops:
  4.1 2.8 fusion.450
  10.3 5.6 %collective-permute-start = (bf16[1,256,640]{2,1,0:T(8,128)(2,1)S(1)}, bf16[1,256,640]{2,1,0:T(8,128)(2,1)S(1)}, u32[]{:S(2)}, u32[]{:S(2)}) collective-permute-start(bf16[1,256,640]{2,1,0:T(8,128)(2,1)S(1)} %fusion.355), channel_id=1, source_target_pairs={{0,1},{1,2},{2,3},{4,5},{5,6},{6,7},{8,9},{9,10},{10,11},{12,13},{... | collective-permute-start | bytes 983048 | tf_op jit(solution)/shard_map/ppermute | solution.py:401
  15.9 5.7 %collective-permute-done.1 = bf16[1,256,640]{2,1,0:T(8,128)(2,1)S(1)} collective-permute-done((bf16[1,256,640]{2,1,0:T(8,128)(2,1)S(1)}, bf16[1,256,640]{2,1,0:T(8,128)(2,1)S(1)}, u32[]{:S(2)}, u32[]{:S(2)}) %collective-permute-start.1) | collective-permute-done | bytes 327712 | tf_op jit(solution)/shard_map/ppermute | solution.py:401
  35.8 5.1 collective-permute-start.3
  40.8 6.3 %collective-permute-done.4 = bf16[1,256,640]{2,1,0:T(8,128)(2,1)S(1)} collective-permute-done((bf16[1,256,640]{2,1,0:T(8,128)(2,1)S(1)}, bf16[1,256,640]{2,1,0:T(8,128)(2,1)S(1)}, u32[]{:S(2)}, u32[]{:S(2)}) %collective-permute-start.4) | collective-permute-done | bytes 327712 | tf_op jit(solution)/shard_map/ppermute | solution.py:401
  60.2 5.1 collective-permute-start.6
  65.2 6.3 %collective-permute-done.7 = bf16[1,256,640]{2,1,0:T(8,128)(2,1)S(1)} collective-permute-done((bf16[1,256,640]{2,1,0:T(8,128)(2,1)S(1)}, bf16[1,256,640]{2,1,0:T(8,128)(2,1)S(1)}, u32[]{:S(2)}, u32[]{:S(2)}) %collective-permute-start.7) | collective-permute-done | bytes 327712 | tf_op jit(solution)/shard_map/ppermute | solution.py:401
  84.7 5.0 collective-permute-start.9
  89.7 6.3 %collective-permute-done.10 = bf16[1,256,640]{2,1,0:T(8,128)(2,1)S(1)} collective-permute-done((bf16[1,256,640]{2,1,0:T(8,128)(2,1)S(1)}, bf16[1,256,640]{2,1,0:T(8,128)(2,1)S(1)}, u32[]{:S(2)}, u32[]{:S(2)}) %collective-permute-start.10) | collective-permute-done | bytes 327712 | tf_op jit(solution)/shard_map/ppermute | solution.py:401
  100.0 2.3 fusion.345
  102.3 2.7 collective-permute-start.11
  105.1 7.9 %copy.24 = bf16[1,5,640,640]{2,3,1,0:T(8,128)(2,1)} copy(bf16[1,5,640,640]{3,2,1,0:T(8,128)(2,1)} %param.16) | data formatting | bytes 8192000 | tf_op args[7]
  118.8 3.7 copy.29
  125.9 2.5 fusion.458
  130.3 5.8 %collective-permute-start.12 = (bf16[1,256,640]{2,1,0:T(8,128)(2,1)S(1)}, bf16[1,256,640]{2,1,0:T(8,128)(2,1)}, u32[]{:S(2)}, u32[]{:S(2)}) collective-permute-start(bf16[1,256,640]{2,1,0:T(8,128)(2,1)S(1)} %fusion.359), channel_id=1, source_target_pairs={{0,1},{1,2},{2,3},{4,5},{5,6},{6,7},{8,9},{9,10},{10,11},{12,13},{... | collective-permute-start | bytes 983048 | tf_op jit(solution)/shard_map/ppermute | solution.py:401
  137.1 3.7 copy.28
  140.7 3.7 copy.27
  144.4 2.3 multiply_reduce_fusion.4
  146.7 3.7 copy.26
  161.0 5.4 %collective-permute-start.14 = (bf16[1,256,640]{2,1,0:T(8,128)(2,1)S(1)}, bf16[1,256,640]{2,1,0:T(8,128)(2,1)}, u32[]{:S(2)}, u32[]{:S(2)}) collective-permute-start(bf16[1,256,640]{2,1,0:T(8,128)(2,1)S(1)} %bitcast.719), channel_id=1, source_target_pairs={{0,1},{1,2},{2,3},{4,5},{5,6},{6,7},{8,9},{9,10},{10,11},{12,13},{... | collective-permute-start | bytes 983048 | tf_op jit(solution)/shard_map/ppermute | solution.py:401
  166.5 3.7 copy.25
  170.2 6.2 %fusion.353 = f32[5,640,640]{2,1,0:T(8,128)} fusion(bf16[5,640,256]{2,1,0:T(8,128)(2,1)} %bitcast.713, bf16[256,640]{1,0:T(8,128)(2,1)S(1)} %get-tuple-element.143), kind=kOutput, calls=%fused_computation.488 | convolution fusion | flops 1048576000 | bytes 10158080 | tf_op jit(solution)/shard_map/brk,bro->ko/dot_general | solution.py:495
  183.6 3.9 multiply_reduce_fusion.1
  194.2 2.5 convolution_multiply_fusion.1
  199.8 4.8 collective-permute-start.17
  204.6 4.6 fusion.351
  216.7 2.5 multiply_reduce_fusion.11
  219.8 2.8 fusion.361
  229.8 5.4 %collective-permute-start.20 = (bf16[1,256,640]{2,1,0:T(8,128)(2,1)S(1)}, bf16[1,256,640]{2,1,0:T(8,128)(2,1)S(1)}, u32[]{:S(2)}, u32[]{:S(2)}) collective-permute-start(bf16[1,256,640]{2,1,0:T(8,128)(2,1)S(1)} %bitcast.725), channel_id=1, source_target_pairs={{0,1},{1,2},{2,3},{4,5},{5,6},{6,7},{8,9},{9,10},{10,11},{12,13},{... | collective-permute-start | bytes 983048 | tf_op jit(solution)/shard_map/ppermute | solution.py:401
  235.2 4.6 fusion.349
  246.3 2.4 multiply_reduce_fusion.10
  258.9 5.2 collective-permute-start.23
  264.1 4.8 fusion.347
  275.5 2.5 multiply_reduce_fusion.9
  283.5 3.1 convolution_add_fusion
  289.5 5.9 %collective-permute-start.26 = (bf16[1,256,640]{2,1,0:T(8,128)(2,1)S(1)}, bf16[1,256,640]{2,1,0:T(8,128)(2,1)}, u32[]{:S(2)}, u32[]{:S(2)}) collective-permute-start(bf16[1,256,640]{2,1,0:T(8,128)(2,1)S(1)} %bitcast.716), channel_id=1, source_target_pairs={{0,1},{1,2},{2,3},{4,5},{5,6},{6,7},{8,9},{9,10},{10,11},{12,13},{... | collective-permute-start | bytes 983048 | tf_op jit(solution)/shard_map/ppermute | solution.py:401
  295.5 15.0 %add_convert_fusion = bf16[5,640,640]{2,1,0:T(8,128)(2,1)} fusion(f32[5,640,640]{2,1,0:T(8,128)} %fusion.347, f32[5,640,640]{2,1,0:T(8,128)} %fusion.349, f32[5,640,640]{2,1,0:T(8,128)} %fusion.351, f32[5,640,640]{2,1,0:T(8,128)} %fusion.353, f32[]{:T(128)S(6)} %select_n.263, f32[]{:T(128)S(6)} %select_n.261, bf16[5,640,256]{2,1,0:T(8,128)(2,1)} %bitcast.714, ...), kind=kOutput, calls=%fused_computation | convolution fusion | flops 1062912000 | bytes 38830088 | tf_op jit(solution)/shard_map/brk,bro->ko/dot_general | solution.py:495
  310.4 3.5 fusion.98
  315.0 9.5 %fusion.392 = f32[1,3]{1,0:T(1,128)S(1)} fusion(f32[1,1]{1,0:T(1,128)} %bitcast.93, f32[1,1]{1,0:T(1,128)} %bitcast.92, f32[1,1]{1,0:T(1,128)} %bitcast.91, f32[1,1]{1,0:T(1,128)} %bitcast.96, f32[1,1]{1,0:T(1,128)} %bitcast.95, f32[1,1]{1,0:T(1,128)} %bitcast.94, f32[1,1]{1,0:T(1,128)} %bitcast.90, f32[1,1]{1,0:T(1,128)} %bitcast.89, f32[1,1]{1,0:T(1,128)} %bitcast.88, ...), kind=kLoop, calls=%fused_computation.653 | loop fusion | flops 48 | bytes 80 | tf_op jit(solution)/shard_map/add | solution.py:576
  332.1 2.7 fusion.435
  337.4 3.8 fusion.3
  341.2 20.7 %pad_maximum_fusion.g_hbm = bf16[5760,640]{1,0:T(8,128)(2,1)} fusion(bf16[1280,640]{1,0:T(8,128)(2,1)S(1)} %fusion.3, bf16[3200,640]{1,0:T(8,128)(2,1)S(1)} %bitcast.708, bf16[640,640]{1,0:T(8,128)(2,1)S(1)} %copy-done.48, bf16[640,640]{1,0:T(8,128)(2,1)S(1)} %get-tuple-element.130), kind=kLoop, calls=%fused_computation.1 | loop fusion | flops 29491200 | bytes 14745600 | tf_op jit(solution)/shard_map/concatenate | solution.py:362
  361.9 141.4 %weight_sums.1 = (bf16[5760,640]{1,0:T(8,128)(2,1)}, f32[16,640]{1,0:T(8,128)S(1)}) custom-call(bf16[5760,640]{1,0:T(8,128)(2,1)} %pad_maximum_fusion.g_hbm, f32[16,640]{1,0:T(8,128)S(1)} %pad.9.s_hbm), custom_call_target="tpu_custom_call" | custom-call | tf_op jit(solution)/shard_map/weight_sums/pallas_call | solution.py:335
  505.1 2.6 slice_bitcast_fusion.1
  507.7 3.7 bitcast_convert_fusion
  511.3 2.3 slice.108
  516.1 6.2 %convert.25 = f32[1,5,640,640]{3,2,1,0:T(8,128)} convert(bf16[1,5,640,640]{3,2,1,0:T(8,128)(2,1)} %bitcast.709) | non-fusion elementwise | flops 2048000 | bytes 12288000 | tf_op jit(solution)/shard_map/convert_element_type | solution.py:379
  527.9 2.8 maximum_bitcast_fusion
  (473 shorter events, 156.4 us)
Async XLA Ops:
  0.6 26.6 %copy-start = (bf16[1,640,1280]{2,1,0:T(8,128)(2,1)S(1)}, bf16[1,640,1280]{2,1,0:T(8,128)(2,1)}, u32[]{:S(2)}) copy-start(bf16[1,640,1280]{2,1,0:T(8,128)(2,1)} %param.17) | copy-start | bytes 4915204
  7.0 16.2 %copy-start.10 = (f32[256,640]{1,0:T(8,128)}, f32[256,640]{1,0:T(8,128)S(1)}, u32[]{:S(2)}) copy-start(f32[256,640]{1,0:T(8,128)S(1)} %get-tuple-element.154) | copy-start | bytes 1966084
  7.0 16.2 %copy-start.58 = (f32[256]{0:T(256)}, f32[256]{0:T(256)S(1)}, u32[]{:S(2)}) copy-start(f32[256]{0:T(256)S(1)} %broadcast_multiply_fusion.9) | copy-start | bytes 3076
  7.2 15.9 %copy-start.62 = (f32[256]{0:T(256)}, f32[256]{0:T(256)S(1)}, u32[]{:S(2)}) copy-start(f32[256]{0:T(256)S(1)} %fusion.376) | copy-start | bytes 3076
  9.0 12.6 %collective-permute-start.1 = (bf16[1,256,640]{2,1,0:T(8,128)(2,1)S(1)}, bf16[1,256,640]{2,1,0:T(8,128)(2,1)S(1)}, u32[]{:S(2)}, u32[]{:S(2)}) collective-permute-start(bf16[1,256,640]{2,1,0:T(8,128)(2,1)S(1)} %fusion.355), channel_id=1, source_target_pairs={{1,0},{2,1},{3,2},{5,4},{6,5},{7,6},{9,8},{10,9},{11,10},{13,12},{... | collective-permute-start | bytes 983048 | tf_op jit(solution)/shard_map/ppermute | solution.py:401
  10.3 12.5 %collective-permute-start = (bf16[1,256,640]{2,1,0:T(8,128)(2,1)S(1)}, bf16[1,256,640]{2,1,0:T(8,128)(2,1)S(1)}, u32[]{:S(2)}, u32[]{:S(2)}) collective-permute-start(bf16[1,256,640]{2,1,0:T(8,128)(2,1)S(1)} %fusion.355), channel_id=1, source_target_pairs={{0,1},{1,2},{2,3},{4,5},{5,6},{6,7},{8,9},{9,10},{10,11},{12,13},{... | collective-permute-start | bytes 983048 | tf_op jit(solution)/shard_map/ppermute | solution.py:401
  29.0 3.0 collective-permute-start.2
  33.8 14.8 %copy-start.12 = (f32[256,640]{1,0:T(8,128)}, f32[256,640]{1,0:T(8,128)S(1)}, u32[]{:S(2)}) copy-start(f32[256,640]{1,0:T(8,128)S(1)} %get-tuple-element.158) | copy-start | bytes 1966084
  34.5 12.6 %collective-permute-start.4 = (bf16[1,256,640]{2,1,0:T(8,128)(2,1)S(1)}, bf16[1,256,640]{2,1,0:T(8,128)(2,1)S(1)}, u32[]{:S(2)}, u32[]{:S(2)}) collective-permute-start(bf16[1,256,640]{2,1,0:T(8,128)(2,1)S(1)} %fusion.356), channel_id=1, source_target_pairs={{1,0},{2,1},{3,2},{5,4},{6,5},{7,6},{9,8},{10,9},{11,10},{13,12},{... | collective-permute-start | bytes 983048 | tf_op jit(solution)/shard_map/ppermute | solution.py:401
  35.8 12.5 %collective-permute-start.3 = (bf16[1,256,640]{2,1,0:T(8,128)(2,1)S(1)}, bf16[1,256,640]{2,1,0:T(8,128)(2,1)S(1)}, u32[]{:S(2)}, u32[]{:S(2)}) collective-permute-start(bf16[1,256,640]{2,1,0:T(8,128)(2,1)S(1)} %fusion.356), channel_id=1, source_target_pairs={{0,1},{1,2},{2,3},{4,5},{5,6},{6,7},{8,9},{9,10},{10,11},{12,13},{... | collective-permute-start | bytes 983048 | tf_op jit(solution)/shard_map/ppermute | solution.py:401
  53.2 3.2 collective-permute-start.5
  58.2 14.8 %copy-start.14 = (f32[256,640]{1,0:T(8,128)}, f32[256,640]{1,0:T(8,128)S(1)}, u32[]{:S(2)}) copy-start(f32[256,640]{1,0:T(8,128)S(1)} %get-tuple-element.164) | copy-start | bytes 1966084
  58.9 12.6 %collective-permute-start.7 = (bf16[1,256,640]{2,1,0:T(8,128)(2,1)S(1)}, bf16[1,256,640]{2,1,0:T(8,128)(2,1)S(1)}, u32[]{:S(2)}, u32[]{:S(2)}) collective-permute-start(bf16[1,256,640]{2,1,0:T(8,128)(2,1)S(1)} %fusion.357), channel_id=1, source_target_pairs={{1,0},{2,1},{3,2},{5,4},{6,5},{7,6},{9,8},{10,9},{11,10},{13,12},{... | collective-permute-start | bytes 983048 | tf_op jit(solution)/shard_map/ppermute | solution.py:401
  60.2 12.5 %collective-permute-start.6 = (bf16[1,256,640]{2,1,0:T(8,128)(2,1)S(1)}, bf16[1,256,640]{2,1,0:T(8,128)(2,1)S(1)}, u32[]{:S(2)}, u32[]{:S(2)}) collective-permute-start(bf16[1,256,640]{2,1,0:T(8,128)(2,1)S(1)} %fusion.357), channel_id=1, source_target_pairs={{0,1},{1,2},{2,3},{4,5},{5,6},{6,7},{8,9},{9,10},{10,11},{12,13},{... | collective-permute-start | bytes 983048 | tf_op jit(solution)/shard_map/ppermute | solution.py:401
  77.7 3.2 collective-permute-start.8
  80.9 19.2 %copy-start.5 = (bf16[1,256,1280]{2,1,0:T(8,128)(2,1)}, bf16[1,256,1280]{2,1,0:T(8,128)(2,1)S(1)}, u32[]{:S(2)}) copy-start(bf16[1,256,1280]{2,1,0:T(8,128)(2,1)S(1)} %collective-permute-done.8) | copy-start | bytes 1966084
  82.7 14.8 %copy-start.16 = (f32[256,640]{1,0:T(8,128)}, f32[256,640]{1,0:T(8,128)S(1)}, u32[]{:S(2)}) copy-start(f32[256,640]{1,0:T(8,128)S(1)} %get-tuple-element.170) | copy-start | bytes 1966084
  83.4 12.6 %collective-permute-start.10 = (bf16[1,256,640]{2,1,0:T(8,128)(2,1)S(1)}, bf16[1,256,640]{2,1,0:T(8,128)(2,1)S(1)}, u32[]{:S(2)}, u32[]{:S(2)}) collective-permute-start(bf16[1,256,640]{2,1,0:T(8,128)(2,1)S(1)} %fusion.358), channel_id=1, source_target_pairs={{1,0},{2,1},{3,2},{5,4},{6,5},{7,6},{9,8},{10,9},{11,10},{13,12},{... | collective-permute-start | bytes 983048 | tf_op jit(solution)/shard_map/ppermute | solution.py:401
  84.7 12.5 %collective-permute-start.9 = (bf16[1,256,640]{2,1,0:T(8,128)(2,1)S(1)}, bf16[1,256,640]{2,1,0:T(8,128)(2,1)S(1)}, u32[]{:S(2)}, u32[]{:S(2)}) collective-permute-start(bf16[1,256,640]{2,1,0:T(8,128)(2,1)S(1)} %fusion.358), channel_id=1, source_target_pairs={{0,1},{1,2},{2,3},{4,5},{5,6},{6,7},{8,9},{9,10},{10,11},{12,13},{... | collective-permute-start | bytes 983048 | tf_op jit(solution)/shard_map/ppermute | solution.py:401
  102.3 20.2 %collective-permute-start.11 = (bf16[1,256,1280]{2,1,0:T(8,128)(2,1)}, bf16[1,256,1280]{2,1,0:T(8,128)(2,1)}, u32[]{:S(2)}, u32[]{:S(2)}) collective-permute-start(bf16[1,256,1280]{2,1,0:T(8,128)(2,1)} %get-tuple-element.173), channel_id=1, source_target_pairs={{0,16},{1,17},{2,18},{3,19},{4,20},{5,21},{6,22},{7,23},{8,24},{9,... | collective-permute-start | bytes 1966088 | tf_op jit(solution)/shard_map/ppermute | solution.py:401
  128.4 8.7 %copy-start.18 = (f32[256,640]{1,0:T(8,128)}, f32[256,640]{1,0:T(8,128)S(1)}, u32[]{:S(2)}) copy-start(f32[256,640]{1,0:T(8,128)S(1)} %get-tuple-element.176) | copy-start | bytes 1966084
  128.4 7.7 %copy-start.36 = (f32[256,1280]{1,0:T(8,128)S(1)}, f32[256,1280]{1,0:T(8,128)}, u32[]{:S(2)}) copy-start(f32[256,1280]{1,0:T(8,128)} %get-tuple-element.162) | copy-start | bytes 3932164
  129.0 23.6 %collective-permute-start.13 = (bf16[1,256,640]{2,1,0:T(8,128)(2,1)S(1)}, bf16[1,256,640]{2,1,0:T(8,128)(2,1)}, u32[]{:S(2)}, u32[]{:S(2)}) collective-permute-start(bf16[1,256,640]{2,1,0:T(8,128)(2,1)S(1)} %fusion.359), channel_id=1, source_target_pairs={{1,0},{2,1},{3,2},{5,4},{6,5},{7,6},{9,8},{10,9},{11,10},{13,12},{... | collective-permute-start | bytes 983048 | tf_op jit(solution)/shard_map/ppermute | solution.py:401
  130.3 22.3 %collective-permute-start.12 = (bf16[1,256,640]{2,1,0:T(8,128)(2,1)S(1)}, bf16[1,256,640]{2,1,0:T(8,128)(2,1)}, u32[]{:S(2)}, u32[]{:S(2)}) collective-permute-start(bf16[1,256,640]{2,1,0:T(8,128)(2,1)S(1)} %fusion.359), channel_id=1, source_target_pairs={{0,1},{1,2},{2,3},{4,5},{5,6},{6,7},{8,9},{9,10},{10,11},{12,13},{... | collective-permute-start | bytes 983048 | tf_op jit(solution)/shard_map/ppermute | solution.py:401
  159.7 17.6 %collective-permute-start.15 = (bf16[1,256,640]{2,1,0:T(8,128)(2,1)S(1)}, bf16[1,256,640]{2,1,0:T(8,128)(2,1)}, u32[]{:S(2)}, u32[]{:S(2)}) collective-permute-start(bf16[1,256,640]{2,1,0:T(8,128)(2,1)S(1)} %bitcast.718), channel_id=1, source_target_pairs={{1,0},{2,1},{3,2},{5,4},{6,5},{7,6},{9,8},{10,9},{11,10},{13,12},{... | collective-permute-start | bytes 983048 | tf_op jit(solution)/shard_map/ppermute | solution.py:401
  161.0 16.3 %collective-permute-start.14 = (bf16[1,256,640]{2,1,0:T(8,128)(2,1)S(1)}, bf16[1,256,640]{2,1,0:T(8,128)(2,1)}, u32[]{:S(2)}, u32[]{:S(2)}) collective-permute-start(bf16[1,256,640]{2,1,0:T(8,128)(2,1)S(1)} %bitcast.719), channel_id=1, source_target_pairs={{0,1},{1,2},{2,3},{4,5},{5,6},{6,7},{8,9},{9,10},{10,11},{12,13},{... | collective-permute-start | bytes 983048 | tf_op jit(solution)/shard_map/ppermute | solution.py:401
  170.2 6.2 %copy-start.51 = (f32[256,640]{1,0:T(8,128)S(1)}, f32[256,640]{1,0:T(8,128)}, u32[]{:S(2)}) copy-start(f32[256,640]{1,0:T(8,128)} %copy-done.50) | copy-start | bytes 1966084
  191.1 5.6 %collective-permute-start.16 = (bf16[1,256,1280]{2,1,0:T(8,128)(2,1)S(1)}, bf16[1,256,1280]{2,1,0:T(8,128)(2,1)S(1)}, u32[]{:S(2)}, u32[]{:S(2)}) collective-permute-start(bf16[1,256,1280]{2,1,0:T(8,128)(2,1)S(1)} %fusion.88), channel_id=1, source_target_pairs={{16,0},{17,1},{18,2},{19,3},{20,4},{21,5},{22,6},{23,7},{24,8},{25... | collective-permute-start | bytes 1966088 | tf_op jit(solution)/shard_map/ppermute | solution.py:401
  196.7 27.3 %copy-start.30 = (bf16[1,256,1280]{2,1,0:T(8,128)(2,1)}, bf16[1,256,1280]{2,1,0:T(8,128)(2,1)S(1)}, u32[]{:S(2)}) copy-start(bf16[1,256,1280]{2,1,0:T(8,128)(2,1)S(1)} %collective-permute-done.16) | copy-start | bytes 1966084
  197.9 6.7 %copy-start.9 = (bf16[3200,256]{1,0:T(8,128)(2,1)S(1)}, bf16[3200,256]{1,0:T(8,128)(2,1)}, u32[]{:S(2)}) copy-start(bf16[3200,256]{1,0:T(8,128)(2,1)} %copy.26) | copy-start | bytes 4915204
  198.3 12.4 %collective-permute-start.18 = (bf16[1,256,640]{2,1,0:T(8,128)(2,1)S(1)}, bf16[1,256,640]{2,1,0:T(8,128)(2,1)S(1)}, u32[]{:S(2)}, u32[]{:S(2)}) collective-permute-start(bf16[1,256,640]{2,1,0:T(8,128)(2,1)S(1)} %bitcast.721), channel_id=1, source_target_pairs={{1,0},{2,1},{3,2},{5,4},{6,5},{7,6},{9,8},{10,9},{11,10},{13,12},{... | collective-permute-start | bytes 983048 | tf_op jit(solution)/shard_map/ppermute | solution.py:401
  199.8 12.6 %collective-permute-start.17 = (bf16[1,256,640]{2,1,0:T(8,128)(2,1)S(1)}, bf16[1,256,640]{2,1,0:T(8,128)(2,1)S(1)}, u32[]{:S(2)}, u32[]{:S(2)}) collective-permute-start(bf16[1,256,640]{2,1,0:T(8,128)(2,1)S(1)} %bitcast.722), channel_id=1, source_target_pairs={{0,1},{1,2},{2,3},{4,5},{5,6},{6,7},{8,9},{9,10},{10,11},{12,13},{... | collective-permute-start | bytes 983048 | tf_op jit(solution)/shard_map/ppermute | solution.py:401
  222.7 4.0 collective-permute-start.19
  226.7 26.4 %copy-start.31 = (bf16[1,256,1280]{2,1,0:T(8,128)(2,1)}, bf16[1,256,1280]{2,1,0:T(8,128)(2,1)S(1)}, u32[]{:S(2)}) copy-start(bf16[1,256,1280]{2,1,0:T(8,128)(2,1)S(1)} %collective-permute-done.19) | copy-start | bytes 1966084
  227.9 7.3 %copy-start.8 = (bf16[3200,256]{1,0:T(8,128)(2,1)S(1)}, bf16[3200,256]{1,0:T(8,128)(2,1)}, u32[]{:S(2)}) copy-start(bf16[3200,256]{1,0:T(8,128)(2,1)} %copy.27) | copy-start | bytes 4915204
  228.3 12.7 %collective-permute-start.21 = (bf16[1,256,640]{2,1,0:T(8,128)(2,1)S(1)}, bf16[1,256,640]{2,1,0:T(8,128)(2,1)S(1)}, u32[]{:S(2)}, u32[]{:S(2)}) collective-permute-start(bf16[1,256,640]{2,1,0:T(8,128)(2,1)S(1)} %bitcast.724), channel_id=1, source_target_pairs={{1,0},{2,1},{3,2},{5,4},{6,5},{7,6},{9,8},{10,9},{11,10},{13,12},{... | collective-permute-start | bytes 983048 | tf_op jit(solution)/shard_map/ppermute | solution.py:401
  229.8 12.9 %collective-permute-start.20 = (bf16[1,256,640]{2,1,0:T(8,128)(2,1)S(1)}, bf16[1,256,640]{2,1,0:T(8,128)(2,1)S(1)}, u32[]{:S(2)}, u32[]{:S(2)}) collective-permute-start(bf16[1,256,640]{2,1,0:T(8,128)(2,1)S(1)} %bitcast.725), channel_id=1, source_target_pairs={{0,1},{1,2},{2,3},{4,5},{5,6},{6,7},{8,9},{9,10},{10,11},{12,13},{... | collective-permute-start | bytes 983048 | tf_op jit(solution)/shard_map/ppermute | solution.py:401
  251.8 4.0 collective-permute-start.22
  255.8 26.4 %copy-start.35 = (bf16[1,256,1280]{2,1,0:T(8,128)(2,1)}, bf16[1,256,1280]{2,1,0:T(8,128)(2,1)S(1)}, u32[]{:S(2)}) copy-start(bf16[1,256,1280]{2,1,0:T(8,128)(2,1)S(1)} %collective-permute-done.22) | copy-start | bytes 1966084
  257.0 7.1 %copy-start.7 = (bf16[3200,256]{1,0:T(8,128)(2,1)S(1)}, bf16[3200,256]{1,0:T(8,128)(2,1)}, u32[]{:S(2)}) copy-start(bf16[3200,256]{1,0:T(8,128)(2,1)} %copy.28) | copy-start | bytes 4915204
  257.5 12.7 %collective-permute-start.24 = (bf16[1,256,640]{2,1,0:T(8,128)(2,1)S(1)}, bf16[1,256,640]{2,1,0:T(8,128)(2,1)S(1)}, u32[]{:S(2)}, u32[]{:S(2)}) collective-permute-start(bf16[1,256,640]{2,1,0:T(8,128)(2,1)S(1)} %bitcast.727), channel_id=1, source_target_pairs={{1,0},{2,1},{3,2},{5,4},{6,5},{7,6},{9,8},{10,9},{11,10},{13,12},{... | collective-permute-start | bytes 983048 | tf_op jit(solution)/shard_map/ppermute | solution.py:401
  258.9 12.9 %collective-permute-start.23 = (bf16[1,256,640]{2,1,0:T(8,128)(2,1)S(1)}, bf16[1,256,640]{2,1,0:T(8,128)(2,1)S(1)}, u32[]{:S(2)}, u32[]{:S(2)}) collective-permute-start(bf16[1,256,640]{2,1,0:T(8,128)(2,1)S(1)} %bitcast.728), channel_id=1, source_target_pairs={{0,1},{1,2},{2,3},{4,5},{5,6},{6,7},{8,9},{9,10},{10,11},{12,13},{... | collective-permute-start | bytes 983048 | tf_op jit(solution)/shard_map/ppermute | solution.py:401
  280.9 5.7 %collective-permute-start.25 = (bf16[1,256,1280]{2,1,0:T(8,128)(2,1)S(1)}, bf16[1,256,1280]{2,1,0:T(8,128)(2,1)S(1)}, u32[]{:S(2)}, u32[]{:S(2)}) collective-permute-start(bf16[1,256,1280]{2,1,0:T(8,128)(2,1)S(1)} %get-tuple-element.124), channel_id=1, source_target_pairs={{16,0},{17,1},{18,2},{19,3},{20,4},{21,5},{22,6},{23,7},{24,8},{25... | collective-permute-start | bytes 1966088 | tf_op jit(solution)/shard_map/ppermute | solution.py:401
  288.2 37.4 %collective-permute-start.27 = (bf16[1,256,640]{2,1,0:T(8,128)(2,1)S(1)}, bf16[1,256,640]{2,1,0:T(8,128)(2,1)}, u32[]{:S(2)}, u32[]{:S(2)}) collective-permute-start(bf16[1,256,640]{2,1,0:T(8,128)(2,1)S(1)} %bitcast.715), channel_id=1, source_target_pairs={{1,0},{2,1},{3,2},{5,4},{6,5},{7,6},{9,8},{10,9},{11,10},{13,12},{... | collective-permute-start | bytes 983048 | tf_op jit(solution)/shard_map/ppermute | solution.py:401
  289.5 36.1 %collective-permute-start.26 = (bf16[1,256,640]{2,1,0:T(8,128)(2,1)S(1)}, bf16[1,256,640]{2,1,0:T(8,128)(2,1)}, u32[]{:S(2)}, u32[]{:S(2)}) collective-permute-start(bf16[1,256,640]{2,1,0:T(8,128)(2,1)S(1)} %bitcast.716), channel_id=1, source_target_pairs={{0,1},{1,2},{2,3},{4,5},{5,6},{6,7},{8,9},{9,10},{10,11},{12,13},{... | collective-permute-start | bytes 983048 | tf_op jit(solution)/shard_map/ppermute | solution.py:401
  505.1 6.2 %copy-start.21 = (bf16[5760,640]{1,0:T(8,128)(2,1)S(1)}, bf16[5760,640]{1,0:T(8,128)(2,1)}, u32[]{:S(2)}) copy-start(bf16[5760,640]{1,0:T(8,128)(2,1)} %get-tuple-element.12) | copy-start | bytes 22118404
  516.1 6.2 %copy-start.49 = (bf16[1,640,640]{2,1,0:T(8,128)(2,1)S(1)}, bf16[1,640,640]{2,1,0:T(8,128)(2,1)}, u32[]{:S(2)}) copy-start(bf16[1,640,640]{2,1,0:T(8,128)(2,1)} %get-tuple-element.123) | copy-start | bytes 2457604
  516.1 8.2 %copy-start.38 = (f32[256,1280]{1,0:T(8,128)S(1)}, f32[256,1280]{1,0:T(8,128)}, u32[]{:S(2)}) copy-start(f32[256,1280]{1,0:T(8,128)} %get-tuple-element.193) | copy-start | bytes 3932164
  (59 other events, 131.5 us)

commit v2 on v0

v2 whole, which is shorter than its diff:
```python
import functools
import math

import jax
import jax.numpy as jnp
from jax import lax
from jax.experimental import pallas as pl
from jax.experimental.pallas import tpu as pltpu
from jax.sharding import PartitionSpec as P

MESH = pl.DeviceIdType.MESH
BF = jnp.bfloat16
F32 = jnp.float32
FILTER_TAPS = 5
FIRST_DILATION = 2
SECOND_DILATION = 128
REACH = FILTER_TAPS // 2
EPS = 1e-05
GELU_A = math.sqrt(2.0 / math.pi)
GELU_B = GELU_A * 0.044715
EDGE = 16

GROUPS = 9
BLOCK = 640
LROWS = 384
HALF = LROWS // 2
QUARTER = LROWS // 4
CHUNK = (BLOCK - LROWS) // 4
KINDS = (
    "ru", "rv", "za", "zb", "zc", "av", "au", "aw",
    "ze", "zm", "zo", "ex", "ey", "ge", "gn", "gd", "gf", "gp", "gq",
)
SMALL_KINDS = ("sx", "sy", "sa", "sb", "sc")
RECEIVE = dict(ru=HALF, rv=QUARTER, za=QUARTER, zb=QUARTER, fl=QUARTER, ze=3 * CHUNK, zm=2 * CHUNK,
               zo=CHUNK, ex=CHUNK, ey=CHUNK, tx=CHUNK, fz=CHUNK)
L_LEVELS = 8
Z_LEVELS = 9
TICKS = GROUPS + Z_LEVELS - 1


def aligned(offset):
    return offset if isinstance(offset, int) else pl.multiple_of(offset, 16)


def part(ref, offset, rows):
    return ref.at[pl.ds(aligned(offset), rows)]


def added(target, offset, sources, rows, tile=32):
    for start in range(0, rows, tile):
        total = None
        for ref, at in sources:
            value = ref[pl.ds(aligned(at + start), tile), :]
            if len(sources) > 2:
                value = value.astype(F32)
            total = value if total is None else total + value
        target[pl.ds(aligned(offset + start), tile), :] = total.astype(BF)


class WeightSums:
    def __init__(self, grad, res, small, buffers, send, recv, local, small_send, small_recv):
        self.grad, self.res, self.small, self.r = grad, res, small, buffers
        self.send, self.recv, self.local = send, recv, local
        self.small_send, self.small_recv = small_send, small_recv
        self.c = lax.axis_index("section")
        self.dp = lax.axis_index("dp")
        self.z = lax.axis_index("seq")
        self.x = lax.rem(self.dp, 2)
        self.y = self.dp // 2
        z = self.z
        self.upper = z // 2
        self.end = jnp.logical_or(z == 0, z == 3)
        self.mid = jnp.logical_not(self.end)
        self.dp_x = self.dp + 1 - 2 * self.x
        self.dp_y = lax.rem(self.dp + 2, 4)
        self.px = (self.c, self.dp_x, z)
        self.py = (self.c, self.dp_y, z)
        self.pair = (self.c, self.dp, 1 - z + 4 * self.upper)
        self.other = (self.c, self.dp, jnp.clip(3 - z, 1, 2))

    def copy(self, kind, g, source, target, to):
        j = KINDS.index(kind)
        return pltpu.make_async_remote_copy(
            src_ref=source, dst_ref=target, send_sem=self.send.at[g, j], recv_sem=self.recv.at[g, j],
            device_id=to, device_id_type=MESH)

    def square(self, g):
        odd = lax.rem(g, 2)
        u = jnp.where(odd == 0, self.x, self.y)
        v = jnp.where(odd == 0, self.y, self.x)
        to_u = (self.c, jnp.where(odd == 0, self.dp_x, self.dp_y), self.z)
        to_v = (self.c, jnp.where(odd == 0, self.dp_y, self.dp_x), self.z)
        base = g * BLOCK
        own_half = base + u * HALF
        own = own_half + v * QUARTER
        beside = own_half + (1 - v) * QUARTER
        return base, u, v, to_u, to_v, own, beside

    def square_copy(self, kind, g):
        base, u, v, to_u, to_v, own, beside = self.square(g)
        grad, res, r = self.grad, self.res, self.r
        final = r["fl"].at[g]
        if kind == "ru":
            return self.copy(kind, g, part(grad, base + (1 - u) * HALF, HALF), r["ru"].at[g], to_u)
        if kind == "rv":
            return self.copy(kind, g, part(grad, beside, QUARTER), r["rv"].at[g], to_v)
        if kind == "za":
            return self.copy(kind, g, part(grad, own, QUARTER), r["za"].at[g], self.pair)
        if kind == "zb":
            return self.copy(kind, g, part(grad, own, QUARTER), r["zb"].at[g], self.other)
        if kind == "zc":
            return self.copy(kind, g, final, final, self.pair)
        if kind == "av":
            return self.copy(kind, g, final, part(res, own, QUARTER), to_v)
        if kind == "au":
            return self.copy(kind, g, final, part(res, own, QUARTER), to_u)
        if kind == "aw":
            return self.copy(kind, g, part(res, beside, QUARTER), part(res, beside, QUARTER), to_u)
        return pltpu.make_async_copy(final, part(res, own, QUARTER), self.local.at[g, 0])

    def square_level(self, g, level):
        base, u, v, to_u, to_v, own, beside = self.square(g)
        grad, r = self.grad, self.r
        copy = functools.partial(self.square_copy, g=g)
        if level == 0:
            copy("ru").start()
        elif level == 1:
            copy("ru").wait_recv()
            added(grad, beside, [(grad, beside), (r["ru"].at[g], (1 - v) * QUARTER)], QUARTER)
            copy("rv").start()
            added(grad, own, [(grad, own), (r["ru"].at[g], v * QUARTER)], QUARTER)
        elif level == 2:
            copy("rv").wait_recv()
            added(grad, own, [(grad, own), (r["rv"].at[g], 0)], QUARTER)

            @pl.when(self.end)
            def _():
                copy("za").start()
        elif level == 3:

            @pl.when(self.mid)
            def _():
                copy("za").wait_recv()
                added(grad, own, [(grad, own), (r["za"].at[g], 0)], QUARTER)
                copy("zb").start()
        elif level == 4:

            @pl.when(self.mid)
            def _():
                copy("zb").wait_recv()
                added(r["fl"].at[g], 0, [(grad, own), (r["zb"].at[g], 0)], QUARTER)
                copy("zc").start()
                copy("av").start()
                copy("au").start()
                copy("fl").start()
        elif level == 5:

            @pl.when(self.end)
            def _():
                copy("zc").wait_recv()
                copy("av").start()
                copy("au").start()
                copy("fl").start()
        elif level == 6:
            copy("av").wait_recv()
            copy("aw").start()
        elif level == 7:
            copy("au").wait_recv()
            copy("aw").wait_recv()
            copy("fl").wait()

    def line(self, g):
        base = g * BLOCK + LROWS
        upper = self.upper
        three = base + CHUNK * (1 - upper)
        far = base + 2 * CHUNK * (1 - upper)
        near = base + 2 * CHUNK * upper
        outer = base + 3 * CHUNK * upper
        own = base + CHUNK * self.z
        return three, far, near, outer, own

    def line_copy(self, kind, g):
        three, far, near, outer, own = self.line(g)
        grad, res, r = self.grad, self.res, self.r
        base = g * BLOCK + LROWS
        final = r["fz"].at[g]
        here = part(res, own, CHUNK)
        if kind == "ze":
            return self.copy(kind, g, part(grad, three, 3 * CHUNK), r["ze"].at[g], self.pair)
        if kind == "zm":
            return self.copy(kind, g, part(grad, far, 2 * CHUNK), r["zm"].at[g], self.other)
        if kind == "zo":
            return self.copy(kind, g, part(grad, outer, CHUNK), r["zo"].at[g], self.pair)
        if kind == "ex":
            return self.copy(kind, g, part(grad, own, CHUNK), r["ex"].at[g], self.px)
        if kind == "ey":
            return self.copy(kind, g, r["tx"].at[g], r["ey"].at[g], self.py)
        if kind in ("ge", "gd"):
            return self.copy(kind, g, final, here, self.pair)
        if kind == "gn":
            return self.copy(kind, g, final, here, self.other)
        if kind == "gf":
            rows = part(res, outer, CHUNK)
            return self.copy(kind, g, rows, rows, self.other)
        if kind == "gp":
            rows = part(res, base + CHUNK * (3 - self.z), CHUNK)
            return self.copy(kind, g, rows, rows, self.pair)
        if kind == "gq":
            rows = part(res, base + 3 * CHUNK * (1 - self.upper), CHUNK)
            return self.copy(kind, g, rows, rows, self.pair)
        return pltpu.make_async_copy(final, here, self.local.at[g, 1])

    def line_level(self, g, level):
        three, far, near, outer, own = self.line(g)
        grad, r = self.grad, self.r
        copy = functools.partial(self.line_copy, g=g)
        if level == 0:

            @pl.when(self.end)
            def _():
                copy("ze").start()
        elif level == 1:

            @pl.when(self.mid)
            def _():
                copy("ze").wait_recv()
                added(grad, far, [(grad, far), (r["ze"].at[g], far - three)], 2 * CHUNK)
                copy("zm").start()
        elif level == 2:

            @pl.when(self.mid)
            def _():
                copy("zm").wait_recv()
                added(grad, outer, [(grad, outer), (r["zm"].at[g], outer - near)], CHUNK)
                copy("zo").start()
                added(grad, own, [(grad, own), (r["ze"].at[g], own - three), (r["zm"].at[g], own - near)], CHUNK)
                copy("ex").start()
        elif level == 3:

            @pl.when(self.end)
            def _():
                copy("zo").wait_recv()
                added(grad, own, [(grad, own), (r["zo"].at[g], 0)], CHUNK)
                copy("ex").start()
        elif level == 4:
            copy("ex").wait_recv()
            added(r["tx"].at[g], 0, [(grad, own), (r["ex"].at[g], 0)], CHUNK)
            copy("ey").start()
        elif level == 5:
            copy("ey").wait_recv()
            added(r["fz"].at[g], 0, [(r["tx"].at[g], 0), (r["ey"].at[g], 0)], CHUNK)
            copy("fz").start()

            @pl.when(self.end)
            def _():
                copy("ge").start()

            @pl.when(self.mid)
            def _():
                copy("gn").start()
                copy("gd").start()
        elif level == 6:

            @pl.when(self.mid)
            def _():
                copy("ge").wait_recv()
                copy("gf").start()
                copy("gn").wait_recv()
                copy("gp").start()
        elif level == 7:

            @pl.when(self.mid)
            def _():
                copy("gf").wait_recv()
                copy("gq").start()
        elif level == 8:
            copy("fz").wait()

            @pl.when(self.end)
            def _():
                copy("gd").wait_recv()
                copy("gp").wait_recv()
                copy("gq").wait_recv()

    def small_copy(self, kind):
        j = SMALL_KINDS.index(kind)
        s = self.small
        source, target, to = dict(
            sx=(s.at[0], s.at[5], self.px),
            sy=(s.at[1], s.at[6], self.py),
            sa=(s.at[2], s.at[7], self.pair),
            sb=(s.at[3], s.at[8], self.other),
            sc=(s.at[4], s.at[4], self.pair),
        )[kind]
        return pltpu.make_async_remote_copy(
            src_ref=source, dst_ref=target, send_sem=self.small_send.at[j], recv_sem=self.small_recv.at[j],
            device_id=to, device_id_type=MESH)

    def small_level(self, level):
        copy, s = self.small_copy, self.small
        if level == 0:
            copy("sx").start()
        elif level == 1:
            copy("sx").wait_recv()
            s[1] = s[0] + s[5]
            copy("sy").start()
        elif level == 2:
            copy("sy").wait_recv()
            s[2] = s[1] + s[6]

            @pl.when(self.end)
            def _():
                copy("sa").start()
        elif level == 3:

            @pl.when(self.mid)
            def _():
                copy("sa").wait_recv()
                s[3] = s[2] + s[7]
                copy("sb").start()
        elif level == 4:

            @pl.when(self.mid)
            def _():
                copy("sb").wait_recv()
                s[4] = s[3] + s[8]
                copy("sc").start()
        elif level == 5:

            @pl.when(self.end)
            def _():
                copy("sc").wait_recv()

    def tick(self, t):
        for level in reversed(range(Z_LEVELS)):
            g = t - level

            @pl.when(jnp.logical_and(g >= 0, g < GROUPS))
            def _():
                if level < L_LEVELS:
                    self.square_level(g, level)
                self.line_level(g, level)

        for level in range(6):

            @pl.when(t == level)
            def _():
                self.small_level(level)

    def drain(self):
        def group(g, carry):
            for kind in ("ru", "rv", "av", "au", "aw"):
                self.square_copy(kind, g).wait_send()
            for kind in ("ex", "ey"):
                self.line_copy(kind, g).wait_send()

            @pl.when(self.end)
            def _():
                self.square_copy("za", g).wait_send()
                self.line_copy("ze", g).wait_send()
                self.line_copy("ge", g).wait_send()

            @pl.when(self.mid)
            def _():
                self.square_copy("zb", g).wait_send()
                self.square_copy("zc", g).wait_send()
                for kind in ("zm", "zo", "gn", "gd", "gf", "gp", "gq"):
                    self.line_copy(kind, g).wait_send()

            return carry

        lax.fori_loop(0, GROUPS, group, 0)
        self.small_copy("sx").wait_send()
        self.small_copy("sy").wait_send()

        @pl.when(self.end)
        def _():
            self.small_copy("sa").wait_send()

        @pl.when(self.mid)
        def _():
            self.small_copy("sb").wait_send()
            self.small_copy("sc").wait_send()


def normed(value):
    mean = jnp.mean(value, axis=-1, keepdims=True)
    centred = value - mean
    spread = jnp.mean(centred * centred, axis=-1, keepdims=True)
    scale = lax.rsqrt(spread + EPS)
    return centred * scale, mean, scale


def gelu(v):
    half = 0.5 * v
    t = jnp.tanh(v * (GELU_A + GELU_B * (v * v)))
    return half + half * t


def gelu_slope(v):
    square = v * v
    t = jnp.tanh(v * (GELU_A + GELU_B * square))
    return (0.5 + 0.5 * t) + (0.5 * v) * (1.0 - t * t) * (GELU_A + (3.0 * GELU_B) * square)


def norm_gelu_back(grad, n, scale, gain, shift):
    dv = grad * gelu_slope(n * gain + shift)
    terms = dv * n
    dn = dv * gain
    first = jnp.mean(dn, axis=-1, keepdims=True)
    second = jnp.mean(dn * n, axis=-1, keepdims=True)
    return dv, terms, scale * (dn - first - n * second)


def fold(value):
    rows, width = value.shape
    return jnp.sum(value.reshape(rows // 8, 8, width), axis=0)


def nn(a, b):
    return jnp.dot(a, b, preferred_element_type=F32)


def nt(a, b):
    return lax.dot_general(a, b, (((1,), (1,)), ((), ())), preferred_element_type=F32)


def tn(a, b):
    return lax.dot_general(a, b, (((0,), (0,)), ((), ())), preferred_element_type=F32)


TILE = 32


def blocks_kernel(
    names, with_sums, last,
    ends, lengths, outer_gain, inner_gains, outer_biases, inner_biases, down_hbm, conv_hbm, up_hbm,
    ends_out, res, small_out,
    down, conv, up, X, GY, HA, CW, HC, GCW, GP, NB, NC, MA, RA, RB, RC, proj, wide, handing, taps, oacc, iacc, grad, small,
    *rest,
):
    buffers = dict(zip(names, rest[: len(names)]))
    send, recv, local, small_send, small_recv, load, hand_send, hand_recv, halo_send, halo_recv, store = rest[len(names) :]
    micro, rows, width = X.shape
    inner = down.shape[1]
    section = lax.axis_index("section")
    dp = lax.axis_index("dp")
    z = lax.axis_index("seq")
    first = section == 0
    second = section == 1
    has_left = z > 0
    has_right = z < last
    across = (1 - section, dp, z)
    left = (section, dp, jnp.maximum(z - 1, 0))
    right = (section, dp, jnp.minimum(z + 1, last))
    sums = WeightSums(grad, res, small, buffers, send, recv, local, small_send, small_recv)

    def when(condition, act):
        pl.when(condition)(lambda: act() and None)

    def weight_load(j):
        return pltpu.make_async_copy((down_hbm, conv_hbm, up_hbm)[j], (down, conv, up)[j], load.at[micro + j])

    def end_load(mb, target):
        return pltpu.make_async_copy(ends.at[mb], target.at[mb], load.at[mb])

    @pl.when(first)
    def _():
        for mb in range(micro):
            end_load(mb, X).start()
            if mb == 0:
                weight_load(0).start()
                weight_load(1).start()
                weight_load(2).start()

    @pl.when(second)
    def _():
        for j in range(3):
            weight_load(j).start()
        for mb in range(micro):
            end_load(mb, GY).start()

    barrier = pltpu.get_barrier_semaphore()

    def greet(to):
        pl.semaphore_signal(barrier, inc=1, device_id=to, device_id_type=MESH)

    greet(across)
    when(has_left, lambda: greet(left))
    when(has_right, lambda: greet(right))
    if with_sums:
        greet(sums.px)
        greet(sums.py)

    oacc[...] = jnp.zeros_like(oacc)
    iacc[...] = jnp.zeros_like(iacc)
    edge = jnp.zeros((rows, inner), BF)
    for mb in range(micro):

        @pl.when(jnp.logical_not(has_left))
        def _():
            CW[mb, 0:rows, :] = edge
            GCW[mb, 0:rows, :] = edge

        @pl.when(jnp.logical_not(has_right))
        def _():
            CW[mb, 2 * rows : 3 * rows, :] = edge
            GCW[mb, 2 * rows : 3 * rows, :] = edge

    peers = (3 if with_sums else 1) + has_left.astype(jnp.int32) + has_right.astype(jnp.int32)
    pl.semaphore_wait(barrier, peers)

    def halo_copies(ref, which, mb):
        def make(side, count):
            if side == 0:
                source, target, to = ref.at[mb, pl.ds(2 * rows - count, count)], ref.at[mb, pl.ds(rows - count, count)], right
            else:
                source, target, to = ref.at[mb, pl.ds(rows, count)], ref.at[mb, pl.ds(2 * rows, count)], left
            return pltpu.make_async_remote_copy(
                src_ref=source, dst_ref=target, send_sem=halo_send.at[which, mb, side],
                recv_sem=halo_recv.at[which, mb, side], device_id=to, device_id_type=MESH)

        return make

    def halo(ref, which, mb, act_right, act_left):
        make = halo_copies(ref, which, mb)
        for mine, count in ((first, EDGE), (second, rows)):

            @pl.when(mine)
            def _():
                when(act_right[0], lambda: act_right[1](make(0, count)))
                when(act_left[0], lambda: act_left[1](make(1, count)))

    def halo_start(ref, which, mb):
        go = lambda c: c.start()
        halo(ref, which, mb, (has_right, go), (has_left, go))

    def halo_arrived(ref, which, mb):
        go = lambda c: c.wait_recv()
        halo(ref, which, mb, (has_left, go), (has_right, go))

    def halo_sent(ref, which, mb):
        go = lambda c: c.wait_send()
        halo(ref, which, mb, (has_right, go), (has_left, go))

    def shifted(ref, mb, k, sign, target, at):
        shift = sign * (k - REACH)

        @pl.when(first)
        def _():
            target[pl.ds(at, rows), :] = ref[mb, pl.ds(rows + shift * FIRST_DILATION, rows), :]

        @pl.when(second)
        def _():
            target[pl.ds(at, rows), :] = ref[mb, pl.ds(rows + shift * SECOND_DILATION, rows), :]

    def hand_over(mb, target):
        slot = lax.rem(mb, 2)
        return pltpu.make_async_remote_copy(
            src_ref=handing.at[slot], dst_ref=target.at[mb], send_sem=hand_send.at[mb], recv_sem=hand_recv.at[mb],
            device_id=across, device_id_type=MESH)

    def store_end(mb):
        return pltpu.make_async_copy(wide.at[lax.rem(mb, 2)], ends_out.at[mb], store.at[mb])

    def tiles(act):
        def step(i, carry):
            act(pl.ds(pl.multiple_of(i * TILE, TILE), TILE), i * TILE)
            return carry

        lax.fori_loop(0, rows // TILE, step, 0)

    def valid_of(mb, start):
        position = z * rows + start + lax.broadcasted_iota(jnp.int32, (TILE, 1), 0)
        return (position < lengths[mb]).astype(F32)

    def forward_a(mb):
        when(first, lambda: end_load(mb, X).wait())
        when(second, lambda: hand_over(mb, X).wait_recv())

        def norm_a(at, start):
            value = X[mb, at, :].astype(F32)
            oacc[3] += fold(value * value * valid_of(mb, start))
            n, mean, scale = normed(value)
            MA[mb, at, :] = mean
            RA[mb, at, :] = scale
            HA[mb, at, :] = gelu(n * outer_gain[...] + outer_biases[0:1, :]).astype(BF)

        tiles(norm_a)
        when(mb == 0, lambda: weight_load(0).wait())
        proj[...] = nn(HA[mb], down[...])

        def norm_b(at, start):
            n, _, scale = normed(proj[at, :] + inner_biases[2:3, :])
            NB[mb, at, :] = n
            RB[mb, at, :] = scale
            value = gelu(n * inner_gains[0:1, :] + inner_biases[0:1, :]) * valid_of(mb, start)
            CW[mb, pl.ds(pl.multiple_of(rows + start, TILE), TILE), :] = value.astype(BF)

        tiles(norm_b)
        halo_start(CW, 0, mb)

    def forward_b(mb):
        slot = lax.rem(mb, 2)
        halo_arrived(CW, 0, mb)
        for k in range(FILTER_TAPS):
            shifted(CW, mb, k, 1, taps, k * rows)

        @pl.when(mb == 0)
        def _():
            weight_load(1).wait()
            weight_load(2).wait()

        total = nn(taps[0:rows, :], conv[0])
        for k in range(1, FILTER_TAPS):
            total = total + nn(taps[k * rows : (k + 1) * rows, :], conv[k])
        proj[...] = total

        def norm_c(at, start):
            n, _, scale = normed(proj[at, :] + inner_biases[3:4, :])
            NC[mb, at, :] = n
            RC[mb, at, :] = scale
            value = gelu(n * inner_gains[1:2, :] + inner_biases[1:2, :]) * valid_of(mb, start)
            HC[mb, at, :] = value.astype(BF)

        tiles(norm_c)

        @pl.when(mb >= 2)
        def _():
            when(first, lambda: hand_over(mb - 2, X).wait_send())
            when(second, lambda: store_end(mb - 2).wait())

        wide[slot] = nn(HC[mb], up[...])

        def close(at, start):
            branch = (wide[slot, at, :] + outer_biases[1:2, :]) * valid_of(mb, start)
            oacc[4] += fold(branch * branch)
            value = X[mb, at, :].astype(F32) + branch

            @pl.when(first)
            def _():
                handing[slot, at, :] = value.astype(BF)

            @pl.when(second)
            def _():
                wide[slot, at, :] = value

        tiles(close)
        when(first, lambda: hand_over(mb, X).start())
        when(second, lambda: store_end(mb).start())

    def backward_a(mb):
        when(first, lambda: hand_over(mb, GY).wait_recv())
        when(second, lambda: end_load(mb, GY).wait())
        proj[...] = nt(GY[mb], up[...])

        def norm_c(at, start):
            valid = valid_of(mb, start)
            oacc[2] += fold(GY[mb, at, :].astype(F32) * valid)
            dv, terms, dz = norm_gelu_back(
                proj[at, :] * valid, NC[mb, at, :], RC[mb, at, :], inner_gains[1:2, :], inner_biases[1:2, :]
            )
            iacc[3] += fold(terms)
            iacc[4] += fold(dv)
            iacc[5] += fold(dz)
            GCW[mb, pl.ds(pl.multiple_of(rows + start, TILE), TILE), :] = dz.astype(BF)

        tiles(norm_c)
        halo_start(GCW, 1, mb)

    def backward_b(mb):
        slot = lax.rem(mb, 2)
        halo_arrived(GCW, 1, mb)
        for k in range(FILTER_TAPS):
            shifted(GCW, mb, k, -1, taps, k * rows)
        total = nt(taps[0:rows, :], conv[0])
        for k in range(1, FILTER_TAPS):
            total = total + nt(taps[k * rows : (k + 1) * rows, :], conv[k])
        proj[...] = total

        def norm_b(at, start):
            dv, terms, dz = norm_gelu_back(
                proj[at, :] * valid_of(mb, start), NB[mb, at, :], RB[mb, at, :], inner_gains[0:1, :], inner_biases[0:1, :]
            )
            iacc[0] += fold(terms)
            iacc[1] += fold(dv)
            iacc[2] += fold(dz)
            GP[mb, at, :] = dz.astype(BF)

        tiles(norm_b)

        @pl.when(mb >= 2)
        def _():
            when(second, lambda: hand_over(mb - 2, GY).wait_send())
            when(first, lambda: store_end(mb - 2).wait())

        wide[slot] = nt(GP[mb], down[...])

        def norm_a(at, start):
            scale = RA[mb, at, :]
            n = (X[mb, at, :].astype(F32) - MA[mb, at, :]) * scale
            dv, terms, dz = norm_gelu_back(wide[slot, at, :], n, scale, outer_gain[...], outer_biases[0:1, :])
            oacc[0] += fold(terms)
            oacc[1] += fold(dv)
            value = GY[mb, at, :].astype(F32) + dz

            @pl.when(second)
            def _():
                handing[slot, at, :] = value.astype(BF)

            @pl.when(first)
            def _():
                wide[slot, at, :] = value

        tiles(norm_a)
        when(second, lambda: hand_over(mb, GY).start())
        when(first, lambda: store_end(mb).start())

    def staggered(a, b):
        def step(i, carry):
            when(i < micro, lambda: a(i))
            when(i >= 1, lambda: b(i - 1))
            return carry

        lax.fori_loop(0, micro + 1, step, 0)

    staggered(forward_a, forward_b)
    for mb in range(micro - 2, micro):
        when(second, functools.partial(lambda m: store_end(m).wait(), mb))
        when(first, functools.partial(lambda m: hand_over(m, X).wait_send(), mb))
    staggered(backward_a, backward_b)

    def weights_of(g):
        @pl.when(g == 0)
        def _():
            c = HC[...].reshape(micro * rows, inner)
            for h in range(2):
                y = GY[:, :, h * inner : (h + 1) * inner].reshape(micro * rows, inner)
                grad[h * BLOCK : (h + 1) * BLOCK, :] = tn(c, y).astype(BF)

        for k in range(FILTER_TAPS):

            @pl.when(g == 2 + k)
            def _():
                for mb in range(micro):
                    shifted(CW, mb, k, 1, taps, mb * rows)

        @pl.when(jnp.logical_and(g >= 2, g < 2 + FILTER_TAPS))
        def _():
            c = taps[0 : micro * rows, :]
            y = GCW[:, rows : 2 * rows, :].reshape(micro * rows, inner)
            grad[pl.ds(pl.multiple_of(g * BLOCK, BLOCK), BLOCK), :] = tn(c, y).astype(BF)

        @pl.when(g == 2 + FILTER_TAPS)
        def _():
            y = GP[...].reshape(micro * rows, inner)
            for h in range(2):
                at = (2 + FILTER_TAPS + h) * BLOCK
                a = HA[:, :, h * inner : (h + 1) * inner].reshape(micro * rows, inner)
                grad[at : at + BLOCK, :] = tn(a, y).astype(BF)

    def row(value):
        return jnp.sum(value, axis=0, keepdims=True)

    small[0] = jnp.zeros_like(small[0])
    place = 0
    for j, ref in ((0, oacc), (None, 0), (None, 3), (1, oacc), (2, oacc), (None, 1), (None, 4), (None, 2), (None, 5)):
        if j is None:
            small[0, place : place + 1, :] = row(iacc[ref])
            place += 1
        else:
            value = row(oacc[j])
            small[0, place : place + 1, :] = value[:, :inner]
            small[0, place + 1 : place + 2, :] = value[:, inner:]
            place += 2
    for j in (3, 4):
        value = row(oacc[j])
        small[0, place : place + 1, :] = value[:, :inner] + value[:, inner:]
        place += 1
    count = jnp.float32(0)
    for mb in range(micro):
        count += jnp.clip(lengths[mb] - z * rows, 0, rows).astype(F32)
    small[0, place : place + 1, :] = jnp.zeros((1, inner), F32) + count

    if with_sums:

        def step(t, carry):
            when(t < GROUPS, lambda: weights_of(t))
            sums.tick(t)
            return carry

        lax.fori_loop(0, TICKS, step, 0)
        sums.drain()
        done = pltpu.make_async_copy(small.at[4], small_out, load.at[0])
        done.start()
        done.wait()
    else:

        def step(t, carry):
            weights_of(t)
            return carry

        lax.fori_loop(0, GROUPS, step, 0)
        done = pltpu.make_async_copy(small.at[0], small_out, load.at[0])
        done.start()
        done.wait()
        done = pltpu.make_async_copy(grad, res, load.at[1])
        done.start()
        done.wait()
    for mb in range(micro):
        if mb >= micro - 2:
            when(first, functools.partial(lambda m: store_end(m).wait(), mb))
            when(second, functools.partial(lambda m: hand_over(m, GY).wait_send(), mb))
        halo_sent(CW, 0, mb)
        halo_sent(GCW, 1, mb)


def run_blocks(mesh_shape, ends, lengths, outer_gain, inner_gains, outer_biases, inner_biases, down, conv, up):
    micro, rows, width = ends.shape
    inner = down.shape[1]
    taps = conv.shape[0]
    with_sums = (mesh_shape["dp"], mesh_shape["seq"]) == (4, 4)
    buffers = {k: pltpu.VMEM((GROUPS, n, BLOCK), BF) for k, n in RECEIVE.items()} if with_sums else {}
    names = tuple(buffers)
    total = GROUPS * BLOCK
    anywhere = pl.BlockSpec(memory_space=pl.ANY)
    vmem = pl.BlockSpec(memory_space=pltpu.VMEM)
    dma = pltpu.SemaphoreType.DMA
    scratch = [
        pltpu.VMEM(down.shape, BF),
        pltpu.VMEM(conv.shape, BF),
        pltpu.VMEM(up.shape, BF),
        pltpu.VMEM((micro, rows, width), BF),
        pltpu.VMEM((micro, rows, width), BF),
        pltpu.VMEM((micro, rows, width), BF),
        pltpu.VMEM((micro, 3 * rows, inner), BF),
        pltpu.VMEM((micro, rows, inner), BF),
        pltpu.VMEM((micro, 3 * rows, inner), BF),
        pltpu.VMEM((micro, rows, inner), BF),
        pltpu.VMEM((micro, rows, inner), F32),
        pltpu.VMEM((micro, rows, inner), F32),
        pltpu.VMEM((micro, rows, 1), F32),
        pltpu.VMEM((micro, rows, 1), F32),
        pltpu.VMEM((micro, rows, 1), F32),
        pltpu.VMEM((micro, rows, 1), F32),
        pltpu.VMEM((rows, inner), F32),
        pltpu.VMEM((2, rows, width), F32),
        pltpu.VMEM((2, rows, width), BF),
        pltpu.VMEM((taps * rows, inner), BF),
        pltpu.VMEM((5, 8, width), F32),
        pltpu.VMEM((6, 8, inner), F32),
        pltpu.VMEM((total, BLOCK), BF),
        pltpu.VMEM((9, 16, inner), F32),
        *[buffers[k] for k in names],
        dma((GROUPS, len(KINDS))),
        dma((GROUPS, len(KINDS))),
        dma((GROUPS, 2)),
        dma((len(SMALL_KINDS),)),
        dma((len(SMALL_KINDS),)),
        dma((micro + 3,)),
        dma((micro,)),
        dma((micro,)),
        dma((2, micro, 2)),
        dma((2, micro, 2)),
        dma((micro,)),
    ]
    flops = 2 * 3 * micro * rows * (2 * width * inner + taps * inner * inner)
    return pl.pallas_call(
        functools.partial(blocks_kernel, names, with_sums, mesh_shape["seq"] - 1),
        name="two_blocks",
        out_shape=(
            jax.ShapeDtypeStruct((micro, rows, width), F32),
            jax.ShapeDtypeStruct((total, BLOCK), BF),
            jax.ShapeDtypeStruct((16, inner), F32),
        ),
        in_specs=[anywhere, pl.BlockSpec(memory_space=pltpu.SMEM), vmem, vmem, vmem, vmem, anywhere, anywhere, anywhere],
        out_specs=[anywhere] * 3,
        scratch_shapes=scratch,
        cost_estimate=pl.CostEstimate(flops=flops, bytes_accessed=40 * 2**20, transcendentals=0),
        compiler_params=pltpu.CompilerParams(collective_id=1, has_side_effects=True, vmem_limit_bytes=62 * 2**20),
    )(ends, lengths, outer_gain, inner_gains, outer_biases, inner_biases, down, conv, up)


def body(
    mesh_shape, ends_in, lengths, outer_gain, inner_gains, outer_biases, inner_biases, down_in, conv_weight, up_out
):
    width = ends_in.shape[-1]
    ends, rows, small = run_blocks(
        mesh_shape, ends_in.reshape(ends_in.shape[1], -1, width), lengths.reshape(-1), outer_gain, inner_gains[0],
        outer_biases[0], inner_biases[0], down_in[0], conv_weight[0], up_out[0],
    )
    if (mesh_shape["dp"], mesh_shape["seq"]) != (4, 4):
        rows, small = lax.psum((rows.astype(F32), small), ("dp", "seq"))
    up = jnp.concatenate([rows[:BLOCK], rows[BLOCK : 2 * BLOCK]], axis=1).astype(F32)
    conv = rows[2 * BLOCK : (2 + FILTER_TAPS) * BLOCK].reshape(conv_weight.shape[1:]).astype(F32)
    down = rows[(2 + FILTER_TAPS) * BLOCK :].astype(F32)
    rms = jnp.sqrt(jnp.sum(small[12:14], axis=1) / (small[14, 0] * width))
    return (
        ends.reshape(ends_in.shape),
        small[0:2].reshape(1, -1),
        small[None, 2:4],
        small[4:8].reshape(1, 2, -1),
        small[None, 8:12],
        down[None],
        conv[None],
        up[None],
        rms[None],
    )


def solution(mesh):
    in_specs = (
        P("section", None, "dp", "seq", None),
        P(None, "dp"),
        P("section", None),
        P("section", None, None),
        P("section", None, None),
        P("section", None, None),
        P("section", None, None),
        P("section", None, None, None),
        P("section", None, None),
    )
    out_specs = (
        P("section", None, "dp", "seq", None),
        P("section", None),
        P("section", None, None),
        P("section", None, None),
        P("section", None, None),
        P("section", None, None),
        P("section", None, None, None),
        P("section", None, None),
        P("section", None),
    )
    return jax.shard_map(
        functools.partial(body, dict(mesh.shape)), mesh=mesh, in_specs=in_specs, out_specs=out_specs, check_vma=False
    )
```

time: 754 us -> 263 us (0.35); the launches traced: 744 us -> 263 us
  waiting for transfers between devices: 338 us -> 0 us
  Pallas kernels: 0 us -> 241 us
  matrix products: 106 us -> 0 us
  blocking collectives: 82.4 us -> 0 us
  starting transfers between devices: 79 us -> 0 us
  other arithmetic: 65.4 us -> 10.4 us
  local copies, waits for them, and re-layouts: 56.4 us -> 9.7 us
  between operations: 17.3 us -> 1.33 us
    psum x1 -> x0, waiting for transfers between devices: 296 us -> none  [body(): lax.psum((totals[0], totals[1], totals[2], totals[3], totals[4], totals[5...]
    pallas_call x0 -> x1, Pallas kernels: none -> 241 us  [run_blocks(): pl.pallas_call(functools.partial(blocks_kernel, names, with_sums, mesh_sh...]
    dot_general x45 -> x0, matrix products: 106 us -> none  [the longest x5 30.9 us: backward(): jnp.einsum('brk,bro->ko', taps, low_conv, preferred_element_type=jnp.floa...]
    psum x1 -> x0, blocking collectives: 82.4 us -> none  [body(): lax.psum((totals[0], totals[1], totals[2], totals[3], totals[4], totals[5...]
    ppermute x28 -> x0, starting transfers between devices: 79 us -> none  [passed_along(): lax.ppermute(value, axis, [(source, source + steps) for source in range(l...]
    ppermute x28 -> x0, waiting for transfers between devices: 41.8 us -> none  [passed_along(): lax.ppermute(value, axis, [(source, source + steps) for source in range(l...]
    unnamed x219 -> x8, local copies, waits for them, and re-layouts: 35.4 us -> 4.51 us
    reduce_sum x52 -> x1, other arithmetic: 29.9 us -> 1.51 us  [body(): rms = jnp.sqrt(jnp.sum(small[12:14], axis=1) / (small[14, 0] * width))]
  transfers between devices with their start and end apart: 29 -> 0, of which waited for: 19 -> 0; matrix products, arithmetic and copies ran while one was open for 15% -> 0% of each run, Pallas kernels for 0% -> 0%
where the time goes in v2:
time: 263 us
  Pallas kernels  241 us (92%)
  other arithmetic  10.4 us (4%)
  local copies, waits for them, and re-layouts  9.7 us (4%)
    pallas_call x1, Pallas kernels, run_blocks(): pl.pallas_call(functools.partial(blocks_kernel, names, with_sums, mesh_sh...  241 us

profile of v2, /device:TPU:0, one launch (start us, length us, event | category | flops | bytes accessed | tf_op | source)
XLA Modules:
  0.0 262.9 jit_solution(7097410205373125350)
XLA Ops:
  0.6 241.5 %two_blocks.1 = (f32[4,256,1280]{2,1,0:T(8,128)}, bf16[5760,640]{1,0:T(8,128)(2,1)}, f32[16,640]{1,0:T(8,128)}) custom-call(bf16[4,256,1280]{2,1,0:T(8,128)(2,1)} %bitcast.37, s32[4]{0:T(128)} %bitcast.43, f32[1,1280]{1,0:T(1,128)} %outer_gain.1, f32[2,640]{1,0:T(2,128)} %bitcast.42, f32[2,1280]{1,0:T(2,128)} %bitcast.40, f32[4,640]{1,0:T(4,128)} %bitcast.41, ...), custom_call_target="tpu_custom_call" | custom-call | flops 22649241600 | bytes 41943040 | tf_op jit(solution)/shard_map/two_blocks/pallas_call | solution.py:868
  242.1 1.2 slice.39
  244.0 1.5 slice_reduce_fusion
  245.5 1.3 slice_bitcast_fusion.2
  246.8 0.5 sqrt_bitcast_fusion
  247.4 0.6 copy.19
  248.0 0.6 reshape.94
  248.6 0.0 copy-start
  248.6 1.7 slice_bitcast_fusion.1
  250.3 1.9 maximum_convert_fusion
  252.2 1.1 copy-done
  253.4 1.9 bitcast_convert_fusion
  255.3 0.4 slice.35
  255.6 0.0 slice-start
  255.6 0.0 slice-start.1
  255.7 4.5 %convert.3 = f32[1,5,640,640]{3,2,1,0:T(8,128)} convert(bf16[1,5,640,640]{3,2,1,0:T(8,128)(2,1)S(1)} %bitcast.31) | non-fusion elementwise | flops 2048000 | bytes 12288000 | tf_op jit(solution)/shard_map/convert_element_type | solution.py:895
  260.1 0.0 slice-done
  260.1 0.4 slice-done.1
  260.5 2.4 copy.21
  (1 shorter events, 0.0 us)
Async XLA Ops:
  248.6 4.8 %copy-start = (bf16[5760,640]{1,0:T(8,128)(2,1)S(1)}, bf16[5760,640]{1,0:T(8,128)(2,1)}, u32[]{:S(2)}) copy-start(bf16[5760,640]{1,0:T(8,128)(2,1)} %get-tuple-element.14) | copy-start | bytes 22118404
  255.6 4.5 %slice-start = ((s8[5242880]{0:T(1024)(128)(4,1)}), s8[4194304]{0:T(1024)(128)(4,1)S(1)}, s32[]{:S(2)}) async-start(s8[5242880]{0:T(1024)(128)(4,1)} %bitcast.32), calls=%async_computation | async-start | bytes 8388608
  255.6 4.9 %slice-start.1 = ((s8[5242880]{0:T(1024)(128)(4,1)}), s8[1048576]{0:T(1024)(128)(4,1)S(1)}, s32[]{:S(2)}) async-start(s8[5242880]{0:T(1024)(128)(4,1)} %bitcast.32), calls=%async_computation.1 | async-start | bytes 2097152

commit v3 on v2

--- a/solution.py
+++ b/solution.py
@@ -20,12 +20,16 @@
 GELU_B = GELU_A * 0.044715
 EDGE = 16
 
-GROUPS = 9
 BLOCK = 640
+UP_BLOCKS = 2
+DOWN_AT = UP_BLOCKS + FILTER_TAPS
+BLOCKS = DOWN_AT + 2
+GROUPS = 10
+ROWS = BLOCKS * BLOCK // GROUPS
 LROWS = 384
 HALF = LROWS // 2
 QUARTER = LROWS // 4
-CHUNK = (BLOCK - LROWS) // 4
+CHUNK = (ROWS - LROWS) // 4
 KINDS = (
     "ru", "rv", "za", "zb", "zc", "av", "au", "aw",
     "ze", "zm", "zo", "ex", "ey", "ge", "gn", "gd", "gf", "gp", "gq",
@@ -35,7 +39,31 @@
                zo=CHUNK, ex=CHUNK, ey=CHUNK, tx=CHUNK, fz=CHUNK)
 L_LEVELS = 8
 Z_LEVELS = 9
-TICKS = GROUPS + Z_LEVELS - 1
+L_STRIDE, Z_STRIDE, Z_LATE, GAP = 1, 1, 0, 1
+FA, FB, WU, BA, BB, WC, WD = range(1, 8)
+FIRST_PLAN = (
+    (FA, 0, 0), (FA, 1, 0), (FB, 0, 0), (FA, 2, 0), (FB, 1, 0), (FA, 3, 0), (FB, 2, 0), (FB, 3, 0), (BA, 0, 0), (BA, 1, 0), (BB, 0, 0), (BA, 2, 0), (BB, 1, 0), (WU, 0, 1), (BA, 3, 0), (BB, 2, 0), (BB, 3, 1), (WC, 0, 1), (WC, 1, 1), (WC, 2, 1), (WC, 3, 1), (WC, 4, 1), (WD, 0, 2),
+)
+SECOND_PLAN = (
+    (FA, 0, 0), (FA, 1, 0), (FB, 0, 0), (FA, 2, 0), (FB, 1, 0), (FA, 3, 0), (FB, 2, 0), (BA, 0, 0), (FB, 3, 0), (WU, 0, 1), (BA, 1, 0), (BA, 2, 0), (BA, 3, 0), (BB, 0, 1), (BB, 1, 1), (BB, 2, 1), (BB, 3, 1), (WC, 0, 1), (WC, 1, 1), (WC, 2, 1), (WC, 3, 1), (WC, 4, 1), (WD, 0, 2),
+)
+
+
+def begins_of(plan):
+    ready, steps = {}, 0
+    for what, k, count in plan:
+        for block in {WU: range(UP_BLOCKS), WC: (UP_BLOCKS + k,), WD: range(DOWN_AT, BLOCKS)}.get(what, ()):
+            ready[block] = steps
+        steps += count
+    begins = []
+    for g in range(GROUPS):
+        there = max(ready[block] for block in range(g * ROWS // BLOCK, ((g + 1) * ROWS - 1) // BLOCK + 1))
+        begins.append(max(there, begins[-1] + GAP) if begins else there)
+    return begins
+
+
+def steps_of(plan):
+    return begins_of(plan)[-1] + max(L_STRIDE * (L_LEVELS - 1), Z_LATE + Z_STRIDE * (Z_LEVELS - 1)) + 1
 
 
 def aligned(offset):
@@ -46,7 +74,7 @@
     return ref.at[pl.ds(aligned(offset), rows)]
 
 
-def added(target, offset, sources, rows, tile=32):
+def added(target, offset, sources, rows, tile=16):
     for start in range(0, rows, tile):
         total = None
         for ref, at in sources:
@@ -81,7 +109,7 @@
     def copy(self, kind, g, source, target, to):
         j = KINDS.index(kind)
         return pltpu.make_async_remote_copy(
-            src_ref=source, dst_ref=target, send_sem=self.send.at[g, j], recv_sem=self.recv.at[g, j],
+            src_ref=source, dst_ref=target, send_sem=self.send.at[j], recv_sem=self.recv.at[g, j],
             device_id=to, device_id_type=MESH)
 
     def square(self, g):
@@ -90,7 +118,7 @@
         v = jnp.where(odd == 0, self.y, self.x)
         to_u = (self.c, jnp.where(odd == 0, self.dp_x, self.dp_y), self.z)
         to_v = (self.c, jnp.where(odd == 0, self.dp_y, self.dp_x), self.z)
-        base = g * BLOCK
+        base = g * ROWS
         own_half = base + u * HALF
         own = own_half + v * QUARTER
         beside = own_half + (1 - v) * QUARTER
@@ -116,7 +144,7 @@
             return self.copy(kind, g, final, part(res, own, QUARTER), to_u)
         if kind == "aw":
             return self.copy(kind, g, part(res, beside, QUARTER), part(res, beside, QUARTER), to_u)
-        return pltpu.make_async_copy(final, part(res, own, QUARTER), self.local.at[g, 0])
+        return pltpu.make_async_copy(final, part(res, own, QUARTER), self.local.at[0])
 
     def square_level(self, g, level):
         base, u, v, to_u, to_v, own, beside = self.square(g)
@@ -167,10 +195,9 @@
         elif level == 7:
             copy("au").wait_recv()
             copy("aw").wait_recv()
-            copy("fl").wait()
 
     def line(self, g):
-        base = g * BLOCK + LROWS
+        base = g * ROWS + LROWS
         upper = self.upper
         three = base + CHUNK * (1 - upper)
         far = base + 2 * CHUNK * (1 - upper)
@@ -182,7 +209,7 @@
     def line_copy(self, kind, g):
         three, far, near, outer, own = self.line(g)
         grad, res, r = self.grad, self.res, self.r
-        base = g * BLOCK + LROWS
+        base = g * ROWS + LROWS
         final = r["fz"].at[g]
         here = part(res, own, CHUNK)
         if kind == "ze":
@@ -208,7 +235,7 @@
         if kind == "gq":
             rows = part(res, base + 3 * CHUNK * (1 - self.upper), CHUNK)
             return self.copy(kind, g, rows, rows, self.pair)
-        return pltpu.make_async_copy(final, here, self.local.at[g, 1])
+        return pltpu.make_async_copy(final, here, self.local.at[1])
 
     def line_level(self, g, level):
         three, far, near, outer, own = self.line(g)
@@ -274,7 +301,6 @@
                 copy("gf").wait_recv()
                 copy("gq").start()
         elif level == 8:
-            copy("fz").wait()
 
             @pl.when(self.end)
             def _():
@@ -331,45 +357,59 @@
             def _():
                 copy("sc").wait_recv()
 
-    def tick(self, t):
+    def tick(self, t, begins, small_begin):
         for level in reversed(range(Z_LEVELS)):
-            g = t - level
-
-            @pl.when(jnp.logical_and(g >= 0, g < GROUPS))
-            def _():
-                if level < L_LEVELS:
-                    self.square_level(g, level)
-                self.line_level(g, level)
+            for kind, stride, late, act in (
+                (0, L_STRIDE, 0, self.square_level),
+                (1, Z_STRIDE, Z_LATE, self.line_level),
+            ):
+                if kind == 0 and level >= L_LEVELS:
+                    continue
+                step = t - late - stride * level
+                g = jnp.int32(-1)
+                for j, begin in enumerate(begins):
+                    g = jnp.where(step == begin, j, g)
+
+                @pl.when(g >= 0)
+                def _():
+                    act(g, level)
 
         for level in range(6):
 
-            @pl.when(t == level)
+            @pl.when(t == small_begin + level)
             def _():
                 self.small_level(level)
 
+    def all_sent(self, kind, rows):
+        everything = self.grad.at[pl.ds(0, GROUPS * rows)]
+        pltpu.make_async_remote_copy(
+            src_ref=everything, dst_ref=everything, send_sem=self.send.at[KINDS.index(kind)],
+            recv_sem=self.recv.at[0, 0], device_id=self.px, device_id_type=MESH).wait_send()
+
     def drain(self):
-        def group(g, carry):
-            for kind in ("ru", "rv", "av", "au", "aw"):
-                self.square_copy(kind, g).wait_send()
-            for kind in ("ex", "ey"):
-                self.line_copy(kind, g).wait_send()
-
-            @pl.when(self.end)
-            def _():
-                self.square_copy("za", g).wait_send()
-                self.line_copy("ze", g).wait_send()
-                self.line_copy("ge", g).wait_send()
-
-            @pl.when(self.mid)
-            def _():
-                self.square_copy("zb", g).wait_send()
-                self.square_copy("zc", g).wait_send()
-                for kind in ("zm", "zo", "gn", "gd", "gf", "gp", "gq"):
-                    self.line_copy(kind, g).wait_send()
-
-            return carry
-
-        lax.fori_loop(0, GROUPS, group, 0)
+        for j, rows in ((0, QUARTER), (1, CHUNK)):
+            everything = self.grad.at[pl.ds(0, GROUPS * rows)]
+            pltpu.make_async_copy(everything, self.res.at[pl.ds(0, GROUPS * rows)], self.local.at[j]).wait()
+        self.all_sent("ru", HALF)
+        for kind in ("rv", "av", "au", "aw"):
+            self.all_sent(kind, QUARTER)
+        for kind in ("ex", "ey"):
+            self.all_sent(kind, CHUNK)
+
+        @pl.when(self.end)
+        def _():
+            self.all_sent("za", QUARTER)
+            self.all_sent("ze", 3 * CHUNK)
+            self.all_sent("ge", CHUNK)
+
+        @pl.when(self.mid)
+        def _():
+            self.all_sent("zb", QUARTER)
+            self.all_sent("zc", QUARTER)
+            self.all_sent("zm", 2 * CHUNK)
+            for kind in ("zo", "gn", "gd", "gf", "gp", "gq"):
+                self.all_sent(kind, CHUNK)
+
         self.small_copy("sx").wait_send()
         self.small_copy("sy").wait_send()
 
@@ -388,27 +428,27 @@
     centred = value - mean
     spread = jnp.mean(centred * centred, axis=-1, keepdims=True)
     scale = lax.rsqrt(spread + EPS)
-    return centred * scale, mean, scale
-
-
-def gelu(v):
-    half = 0.5 * v
-    t = jnp.tanh(v * (GELU_A + GELU_B * (v * v)))
-    return half + half * t
-
-
-def gelu_slope(v):
-    square = v * v
-    t = jnp.tanh(v * (GELU_A + GELU_B * square))
-    return (0.5 + 0.5 * t) + (0.5 * v) * (1.0 - t * t) * (GELU_A + (3.0 * GELU_B) * square)
-
-
-def norm_gelu_back(grad, n, scale, gain, shift):
-    dv = grad * gelu_slope(n * gain + shift)
+    return centred * scale, mean, scale, spread
+
+
+def gelu(w):
+    t = jnp.tanh(w * (2.0 * GELU_A + (8.0 * GELU_B) * (w * w)))
+    return w + w * t
+
+
+def gelu_slope(w):
+    square = w * w
+    t = jnp.tanh(w * (2.0 * GELU_A + (8.0 * GELU_B) * square))
+    q = w * (GELU_A + (12.0 * GELU_B) * square)
+    return (0.5 + q) + t * (0.5 - q * t)
+
+
+def norm_gelu_back(grad, n, scale, gain, half_gain, half_shift):
+    dv = grad * gelu_slope(n * half_gain + half_shift)
     terms = dv * n
     dn = dv * gain
     first = jnp.mean(dn, axis=-1, keepdims=True)
-    second = jnp.mean(dn * n, axis=-1, keepdims=True)
+    second = jnp.mean(terms * gain, axis=-1, keepdims=True)
     return dv, terms, scale * (dn - first - n * second)
 
 
@@ -427,16 +467,13 @@
 
 def tn(a, b):
     return lax.dot_general(a, b, (((0,), (0,)), ((), ())), preferred_element_type=F32)
-
-
-TILE = 32
 
 
 def blocks_kernel(
     names, with_sums, last,
     ends, lengths, outer_gain, inner_gains, outer_biases, inner_biases, down_hbm, conv_hbm, up_hbm,
     ends_out, res, small_out,
-    down, conv, up, X, GY, HA, CW, HC, GCW, GP, NB, NC, MA, RA, RB, RC, proj, wide, handing, taps, oacc, iacc, grad, small,
+    down, conv, up, X, GY, HA, CW, HC, GCW, GP, NB, NC, ST, XS, wide, handing, taps, lhs, oacc, iacc, grad, small,
     *rest,
 ):
     buffers = dict(zip(names, rest[: len(names)]))
@@ -466,12 +503,49 @@
 
     @pl.when(first)
     def _():
-        for mb in range(micro):
+        end_load(0, X).start()
+        weight_load(0).start()
+
+    barrier = pltpu.get_barrier_semaphore()
+
+    def greet(to):
+        pl.semaphore_signal(barrier, inc=1, device_id=to, device_id_type=MESH)
+
+    greet(across)
+    when(has_left, lambda: greet(left))
+    when(has_right, lambda: greet(right))
+    if with_sums:
+        greet(sums.px)
+        greet(sums.py)
+
+    def met():
+        peers = (3 if with_sums else 1) + has_left.astype(jnp.int32) + has_right.astype(jnp.int32)
+        pl.semaphore_wait(barrier, peers)
+
+    XS[...] = jnp.zeros_like(XS)
+    oacc[...] = jnp.zeros_like(oacc)
+    iacc[...] = jnp.zeros_like(iacc)
+    edge = jnp.zeros((rows, inner), BF)
+    for mb in range(micro):
+
+        @pl.when(jnp.logical_not(has_left))
+        def _():
+            CW[mb, 0:rows, :] = edge
+            GCW[mb, 0:rows, :] = edge
+
+        @pl.when(jnp.logical_not(has_right))
+        def _():
+            CW[mb, 2 * rows : 3 * rows, :] = edge
+            GCW[mb, 2 * rows : 3 * rows, :] = edge
+
+    @pl.when(first)
+    def _():
+        end_load(0, X).wait()
+        weight_load(0).wait()
+        weight_load(1).start()
+        weight_load(2).start()
+        for mb in range(1, micro):
             end_load(mb, X).start()
-            if mb == 0:
-                weight_load(0).start()
-                weight_load(1).start()
-                weight_load(2).start()
 
     @pl.when(second)
     def _():
@@ -479,36 +553,6 @@
             weight_load(j).start()
         for mb in range(micro):
             end_load(mb, GY).start()
-
-    barrier = pltpu.get_barrier_semaphore()
-
-    def greet(to):
-        pl.semaphore_signal(barrier, inc=1, device_id=to, device_id_type=MESH)
-
-    greet(across)
-    when(has_left, lambda: greet(left))
-    when(has_right, lambda: greet(right))
-    if with_sums:
-        greet(sums.px)
-        greet(sums.py)
-
-    oacc[...] = jnp.zeros_like(oacc)
-    iacc[...] = jnp.zeros_like(iacc)
-    edge = jnp.zeros((rows, inner), BF)
-    for mb in range(micro):
-
-        @pl.when(jnp.logical_not(has_left))
-        def _():
-            CW[mb, 0:rows, :] = edge
-            GCW[mb, 0:rows, :] = edge
-
-        @pl.when(jnp.logical_not(has_right))
-        def _():
-            CW[mb, 2 * rows : 3 * rows, :] = edge
-            GCW[mb, 2 * rows : 3 * rows, :] = edge
-
-    peers = (3 if with_sums else 1) + has_left.astype(jnp.int32) + has_right.astype(jnp.int32)
-    pl.semaphore_wait(barrier, peers)
 
     def halo_copies(ref, which, mb):
         def make(side, count):
@@ -543,16 +587,25 @@
         go = lambda c: c.wait_send()
         halo(ref, which, mb, (has_right, go), (has_left, go))
 
-    def shifted(ref, mb, k, sign, target, at):
+    def shifted(ref, mb, k, sign, target, at, column):
         shift = sign * (k - REACH)
 
         @pl.when(first)
         def _():
-            target[pl.ds(at, rows), :] = ref[mb, pl.ds(rows + shift * FIRST_DILATION, rows), :]
+            target[at : at + rows, column : column + inner] = ref[mb, pl.ds(rows + shift * FIRST_DILATION, rows), :]
 
         @pl.when(second)
         def _():
-            target[pl.ds(at, rows), :] = ref[mb, pl.ds(rows + shift * SECOND_DILATION, rows), :]
+            target[at : at + rows, column : column + inner] = ref[mb, pl.ds(rows + shift * SECOND_DILATION, rows), :]
+
+    def all_shifted(ref, mb, sign):
+        for mine, dilation in ((first, FIRST_DILATION), (second, SECOND_DILATION)):
+
+            @pl.when(mine)
+            def _():
+                for k in range(FILTER_TAPS):
+                    at = rows + sign * (k - REACH) * dilation
+                    taps[:, k * inner : (k + 1) * inner] = ref[mb, pl.ds(at, rows), :]
 
     def hand_over(mb, target):
         slot = lax.rem(mb, 2)
@@ -563,244 +616,203 @@
     def store_end(mb):
         return pltpu.make_async_copy(wide.at[lax.rem(mb, 2)], ends_out.at[mb], store.at[mb])
 
-    def tiles(act):
-        def step(i, carry):
-            act(pl.ds(pl.multiple_of(i * TILE, TILE), TILE), i * TILE)
-            return carry
-
-        lax.fori_loop(0, rows // TILE, step, 0)
-
-    def valid_of(mb, start):
-        position = z * rows + start + lax.broadcasted_iota(jnp.int32, (TILE, 1), 0)
+    own = pl.ds(rows, rows)
+    outer_shift, inner_shift_b, inner_shift_c = 0.5 * outer_biases[0:1, :], 0.5 * inner_biases[0:1, :], 0.5 * inner_biases[1:2, :]
+    outer_half, inner_half_b, inner_half_c = 0.5 * outer_gain[...], 0.5 * inner_gains[0:1, :], 0.5 * inner_gains[1:2, :]
+
+    def valid_of(mb):
+        position = z * rows + lax.broadcasted_iota(jnp.int32, (rows, 1), 0)
         return (position < lengths[mb]).astype(F32)
 
     def forward_a(mb):
-        when(first, lambda: end_load(mb, X).wait())
+        when(jnp.logical_and(first, mb > 0), lambda: end_load(mb, X).wait())
         when(second, lambda: hand_over(mb, X).wait_recv())
-
-        def norm_a(at, start):
-            value = X[mb, at, :].astype(F32)
-            oacc[3] += fold(value * value * valid_of(mb, start))
-            n, mean, scale = normed(value)
-            MA[mb, at, :] = mean
-            RA[mb, at, :] = scale
-            HA[mb, at, :] = gelu(n * outer_gain[...] + outer_biases[0:1, :]).astype(BF)
-
-        tiles(norm_a)
-        when(mb == 0, lambda: weight_load(0).wait())
-        proj[...] = nn(HA[mb], down[...])
-
-        def norm_b(at, start):
-            n, _, scale = normed(proj[at, :] + inner_biases[2:3, :])
-            NB[mb, at, :] = n
-            RB[mb, at, :] = scale
-            value = gelu(n * inner_gains[0:1, :] + inner_biases[0:1, :]) * valid_of(mb, start)
-            CW[mb, pl.ds(pl.multiple_of(rows + start, TILE), TILE), :] = value.astype(BF)
-
-        tiles(norm_b)
+        when(jnp.logical_and(second, mb == 0), lambda: weight_load(0).wait())
+        n, mean, scale, spread = normed(X[mb].astype(F32))
+        XS[...] += (spread + mean * mean) * valid_of(mb)
+        ST[mb, :, 0:1] = mean
+        ST[mb, :, 1:2] = scale
+        hidden = gelu(n * outer_half + outer_shift).astype(BF)
+        HA[mb] = hidden
+        n, _, scale, _ = normed(nn(hidden, down[...]) + inner_biases[2:3, :])
+        NB[mb] = n
+        ST[mb, :, 2:3] = scale
+        CW[mb, own, :] = (gelu(n * inner_half_b + inner_shift_b) * valid_of(mb)).astype(BF)
+        when(jnp.logical_and(first, mb == 0), met)
         halo_start(CW, 0, mb)
 
     def forward_b(mb):
         slot = lax.rem(mb, 2)
         halo_arrived(CW, 0, mb)
-        for k in range(FILTER_TAPS):
-            shifted(CW, mb, k, 1, taps, k * rows)
 
         @pl.when(mb == 0)
         def _():
             weight_load(1).wait()
             weight_load(2).wait()
 
-        total = nn(taps[0:rows, :], conv[0])
-        for k in range(1, FILTER_TAPS):
-            total = total + nn(taps[k * rows : (k + 1) * rows, :], conv[k])
-        proj[...] = total
-
-        def norm_c(at, start):
-            n, _, scale = normed(proj[at, :] + inner_biases[3:4, :])
-            NC[mb, at, :] = n
-            RC[mb, at, :] = scale
-            value = gelu(n * inner_gains[1:2, :] + inner_biases[1:2, :]) * valid_of(mb, start)
-            HC[mb, at, :] = value.astype(BF)
-
-        tiles(norm_c)
-
         @pl.when(mb >= 2)
         def _():
             when(first, lambda: hand_over(mb - 2, X).wait_send())
             when(second, lambda: store_end(mb - 2).wait())
 
-        wide[slot] = nn(HC[mb], up[...])
-
-        def close(at, start):
-            branch = (wide[slot, at, :] + outer_biases[1:2, :]) * valid_of(mb, start)
-            oacc[4] += fold(branch * branch)
-            value = X[mb, at, :].astype(F32) + branch
-
-            @pl.when(first)
-            def _():
-                handing[slot, at, :] = value.astype(BF)
-
-            @pl.when(second)
-            def _():
-                wide[slot, at, :] = value
-
-        tiles(close)
+        all_shifted(CW, mb, 1)
+        n, _, scale, _ = normed(nn(taps[...], conv[...]) + inner_biases[3:4, :])
+        NC[mb] = n
+        ST[mb, :, 3:4] = scale
+        valid = valid_of(mb)
+        hidden = (gelu(n * inner_half_c + inner_shift_c) * valid).astype(BF)
+        HC[mb] = hidden
+        branch = (nn(hidden, up[...]) + outer_biases[1:2, :]) * valid
+        oacc[3] += fold(branch * branch)
+        value = X[mb].astype(F32) + branch
+        wide[slot] = value
+        handing[slot] = value.astype(BF)
         when(first, lambda: hand_over(mb, X).start())
         when(second, lambda: store_end(mb).start())
 
     def backward_a(mb):
-        when(first, lambda: hand_over(mb, GY).wait_recv())
-        when(second, lambda: end_load(mb, GY).wait())
-        proj[...] = nt(GY[mb], up[...])
-
-        def norm_c(at, start):
-            valid = valid_of(mb, start)
-            oacc[2] += fold(GY[mb, at, :].astype(F32) * valid)
-            dv, terms, dz = norm_gelu_back(
-                proj[at, :] * valid, NC[mb, at, :], RC[mb, at, :], inner_gains[1:2, :], inner_biases[1:2, :]
-            )
-            iacc[3] += fold(terms)
-            iacc[4] += fold(dv)
-            iacc[5] += fold(dz)
-            GCW[mb, pl.ds(pl.multiple_of(rows + start, TILE), TILE), :] = dz.astype(BF)
-
-        tiles(norm_c)
+        when(jnp.logical_and(first, mb < micro - 1), lambda: hand_over(mb, GY).wait_recv())
+
+        @pl.when(jnp.logical_and(second, mb == 0))
+        def _():
+            for k in range(micro):
+                end_load(k, GY).wait()
+
+        valid = valid_of(mb)
+        oacc[2] += fold(GY[mb].astype(F32) * valid)
+        dv, terms, dz = norm_gelu_back(
+            nt(GY[mb], up[...]) * valid, NC[mb], ST[mb, :, 3:4], inner_gains[1:2, :], inner_half_c, inner_shift_c
+        )
+        iacc[3] += fold(terms)
+        iacc[4] += fold(dv)
+        iacc[5] += fold(dz)
+        GCW[mb, own, :] = dz.astype(BF)
         halo_start(GCW, 1, mb)
 
     def backward_b(mb):
         slot = lax.rem(mb, 2)
         halo_arrived(GCW, 1, mb)
-        for k in range(FILTER_TAPS):
-            shifted(GCW, mb, k, -1, taps, k * rows)
-        total = nt(taps[0:rows, :], conv[0])
-        for k in range(1, FILTER_TAPS):
-            total = total + nt(taps[k * rows : (k + 1) * rows, :], conv[k])
-        proj[...] = total
-
-        def norm_b(at, start):
-            dv, terms, dz = norm_gelu_back(
-                proj[at, :] * valid_of(mb, start), NB[mb, at, :], RB[mb, at, :], inner_gains[0:1, :], inner_biases[0:1, :]
-            )
-            iacc[0] += fold(terms)
-            iacc[1] += fold(dv)
-            iacc[2] += fold(dz)
-            GP[mb, at, :] = dz.astype(BF)
-
-        tiles(norm_b)
+
+        @pl.when(mb < 2)
+        def _():
+            when(first, lambda: hand_over(mb + micro - 2, X).wait_send())
+            when(second, lambda: store_end(mb + micro - 2).wait())
 
         @pl.when(mb >= 2)
         def _():
             when(second, lambda: hand_over(mb - 2, GY).wait_send())
             when(first, lambda: store_end(mb - 2).wait())
 
-        wide[slot] = nt(GP[mb], down[...])
-
-        def norm_a(at, start):
-            scale = RA[mb, at, :]
-            n = (X[mb, at, :].astype(F32) - MA[mb, at, :]) * scale
-            dv, terms, dz = norm_gelu_back(wide[slot, at, :], n, scale, outer_gain[...], outer_biases[0:1, :])
-            oacc[0] += fold(terms)
-            oacc[1] += fold(dv)
-            value = GY[mb, at, :].astype(F32) + dz
-
-            @pl.when(second)
-            def _():
-                handing[slot, at, :] = value.astype(BF)
-
-            @pl.when(first)
-            def _():
-                wide[slot, at, :] = value
-
-        tiles(norm_a)
+        all_shifted(GCW, mb, -1)
+        total = nt(taps[:, 0:inner], conv[0:inner, :])
+        for k in range(1, FILTER_TAPS):
+            total = total + nt(taps[:, k * inner : (k + 1) * inner], conv[k * inner : (k + 1) * inner, :])
+        dv, terms, dz = norm_gelu_back(
+            total * valid_of(mb), NB[mb], ST[mb, :, 2:3], inner_gains[0:1, :], inner_half_b, inner_shift_b
+        )
+        iacc[0] += fold(terms)
+        iacc[1] += fold(dv)
+        iacc[2] += fold(dz)
+        low = dz.astype(BF)
+        GP[mb] = low
+        scale = ST[mb, :, 1:2]
+        n = (X[mb].astype(F32) - ST[mb, :, 0:1]) * scale
+        dv, terms, dz = norm_gelu_back(nt(low, down[...]), n, scale, outer_gain[...], outer_half, outer_shift)
+        oacc[0] += fold(terms)
+        oacc[1] += fold(dv)
+        value = GY[mb].astype(F32) + dz
+        wide[slot] = value
+        handing[slot] = value.astype(BF)
         when(second, lambda: hand_over(mb, GY).start())
         when(first, lambda: store_end(mb).start())
 
-    def staggered(a, b):
-        def step(i, carry):
-            when(i < micro, lambda: a(i))
-            when(i >= 1, lambda: b(i - 1))
-            return carry
-
-        lax.fori_loop(0, micro + 1, step, 0)
-
-    staggered(forward_a, forward_b)
-    for mb in range(micro - 2, micro):
-        when(second, functools.partial(lambda m: store_end(m).wait(), mb))
-        when(first, functools.partial(lambda m: hand_over(m, X).wait_send(), mb))
-    staggered(backward_a, backward_b)
-
-    def weights_of(g):
-        @pl.when(g == 0)
-        def _():
-            c = HC[...].reshape(micro * rows, inner)
-            for h in range(2):
-                y = GY[:, :, h * inner : (h + 1) * inner].reshape(micro * rows, inner)
-                grad[h * BLOCK : (h + 1) * BLOCK, :] = tn(c, y).astype(BF)
-
+    def weight_up():
+        when(first, lambda: hand_over(micro - 1, GY).wait_recv())
+        c = HC[...].reshape(micro * rows, inner)
+        for h in range(UP_BLOCKS):
+            y = GY[:, :, h * inner : (h + 1) * inner].reshape(micro * rows, inner)
+            grad[h * BLOCK : (h + 1) * BLOCK, :] = tn(c, y).astype(BF)
+
+    def weight_tap(tap):
         for k in range(FILTER_TAPS):
 
-            @pl.when(g == 2 + k)
+            @pl.when(tap == k)
             def _():
                 for mb in range(micro):
-                    shifted(CW, mb, k, 1, taps, mb * rows)
-
-        @pl.when(jnp.logical_and(g >= 2, g < 2 + FILTER_TAPS))
-        def _():
-            c = taps[0 : micro * rows, :]
-            y = GCW[:, rows : 2 * rows, :].reshape(micro * rows, inner)
-            grad[pl.ds(pl.multiple_of(g * BLOCK, BLOCK), BLOCK), :] = tn(c, y).astype(BF)
-
-        @pl.when(g == 2 + FILTER_TAPS)
-        def _():
-            y = GP[...].reshape(micro * rows, inner)
-            for h in range(2):
-                at = (2 + FILTER_TAPS + h) * BLOCK
-                a = HA[:, :, h * inner : (h + 1) * inner].reshape(micro * rows, inner)
-                grad[at : at + BLOCK, :] = tn(a, y).astype(BF)
+                    shifted(CW, mb, k, 1, lhs, mb * rows, 0)
+
+        y = GCW[:, own, :].reshape(micro * rows, inner)
+        at = pl.multiple_of((UP_BLOCKS + tap) * BLOCK, BLOCK)
+        grad[pl.ds(at, BLOCK), :] = tn(lhs[...], y).astype(BF)
+
+    def weight_down():
+        y = GP[...].reshape(micro * rows, inner)
+        for h in range(BLOCKS - DOWN_AT):
+            at = (DOWN_AT + h) * BLOCK
+            a = HA[:, :, h * inner : (h + 1) * inner].reshape(micro * rows, inner)
+            grad[at : at + BLOCK, :] = tn(a, y).astype(BF)
 
     def row(value):
         return jnp.sum(value, axis=0, keepdims=True)
 
-    small[0] = jnp.zeros_like(small[0])
-    place = 0
-    for j, ref in ((0, oacc), (None, 0), (None, 3), (1, oacc), (2, oacc), (None, 1), (None, 4), (None, 2), (None, 5)):
-        if j is None:
-            small[0, place : place + 1, :] = row(iacc[ref])
-            place += 1
-        else:
-            value = row(oacc[j])
-            small[0, place : place + 1, :] = value[:, :inner]
-            small[0, place + 1 : place + 2, :] = value[:, inner:]
-            place += 2
-    for j in (3, 4):
-        value = row(oacc[j])
-        small[0, place : place + 1, :] = value[:, :inner] + value[:, inner:]
-        place += 1
-    count = jnp.float32(0)
-    for mb in range(micro):
-        count += jnp.clip(lengths[mb] - z * rows, 0, rows).astype(F32)
-    small[0, place : place + 1, :] = jnp.zeros((1, inner), F32) + count
+    def smalls():
+        place = 0
+
+        def put(value):
+            nonlocal place
+            for at in range(0, value.shape[1], inner):
+                small[0, place : place + 1, :] = value[:, at : at + inner]
+                place += 1
+
+        small[0] = jnp.zeros_like(small[0])
+        for ref, j in ((oacc, 0), (iacc, 0), (iacc, 3), (oacc, 1), (oacc, 2), (iacc, 1), (iacc, 4), (iacc, 2), (iacc, 5)):
+            put(row(ref[j]))
+        lane = lax.broadcasted_iota(jnp.int32, (1, inner), 1)
+        put(jnp.where(lane == 0, row(XS[...]) * width, 0.0))
+        value = row(oacc[3])
+        put(value[:, :inner] + value[:, inner:])
+        count = jnp.float32(0)
+        for mb in range(micro):
+            count += jnp.clip(lengths[mb] - z * rows, 0, rows).astype(F32)
+        put(jnp.zeros((1, inner), F32) + count)
+
+    when(second, met)
+    plans = [[(p * 8 + k) * 8 + steps for p, k, steps in plan] for plan in (FIRST_PLAN, SECOND_PLAN)]
+    begins = [jnp.where(first, a, b) for a, b in zip(begins_of(FIRST_PLAN), begins_of(SECOND_PLAN))]
+    ticks = jnp.where(first, steps_of(FIRST_PLAN), steps_of(SECOND_PLAN))
+
+    def tick(t, carry):
+        sums.tick(t, begins, begins[-1])
+        return carry
+
+    def step(i, t):
+        entry = jnp.int32(0)
+        for j, (a, b) in enumerate(zip(*plans)):
+            entry = jnp.where(i == j, jnp.where(first, a, b), entry)
+        what, k = entry // 64, lax.rem(entry // 8, 8)
+        for p, act in ((FA, forward_a), (FB, forward_b), (BA, backward_a), (BB, backward_b), (WC, weight_tap)):
+            when(what == p, functools.partial(act, k))
+        when(what == WU, weight_up)
+
+        @pl.when(what == WD)
+        def _():
+            smalls()
+            weight_down()
+
+        then = t + lax.rem(entry, 8)
+        if with_sums:
+            lax.fori_loop(t, then, tick, 0)
+        return then
+
+    t = lax.fori_loop(0, len(FIRST_PLAN), step, jnp.int32(0))
 
     if with_sums:
-
-        def step(t, carry):
-            when(t < GROUPS, lambda: weights_of(t))
-            sums.tick(t)
-            return carry
-
-        lax.fori_loop(0, TICKS, step, 0)
+        lax.fori_loop(t, ticks, tick, 0)
         sums.drain()
         done = pltpu.make_async_copy(small.at[4], small_out, load.at[0])
         done.start()
         done.wait()
     else:
-
-        def step(t, carry):
-            weights_of(t)
-            return carry
-
-        lax.fori_loop(0, GROUPS, step, 0)
         done = pltpu.make_async_copy(small.at[0], small_out, load.at[0])
         done.start()
         done.wait()
@@ -818,11 +830,11 @@
 def run_blocks(mesh_shape, ends, lengths, outer_gain, inner_gains, outer_biases, inner_biases, down, conv, up):
     micro, rows, width = ends.shape
     inner = down.shape[1]
-    taps = conv.shape[0]
+    taps = FILTER_TAPS
     with_sums = (mesh_shape["dp"], mesh_shape["seq"]) == (4, 4)
     buffers = {k: pltpu.VMEM((GROUPS, n, BLOCK), BF) for k, n in RECEIVE.items()} if with_sums else {}
     names = tuple(buffers)
-    total = GROUPS * BLOCK
+    total = BLOCKS * BLOCK
     anywhere = pl.BlockSpec(memory_space=pl.ANY)
     vmem = pl.BlockSpec(memory_space=pltpu.VMEM)
     dma = pltpu.SemaphoreType.DMA
@@ -839,22 +851,20 @@
         pltpu.VMEM((micro, rows, inner), BF),
         pltpu.VMEM((micro, rows, inner), F32),
         pltpu.VMEM((micro, rows, inner), F32),
-        pltpu.VMEM((micro, rows, 1), F32),
-        pltpu.VMEM((micro, rows, 1), F32),
-        pltpu.VMEM((micro, rows, 1), F32),
-        pltpu.VMEM((micro, rows, 1), F32),
-        pltpu.VMEM((rows, inner), F32),
+        pltpu.VMEM((micro, rows, 128), F32),
+        pltpu.VMEM((rows, 1), F32),
         pltpu.VMEM((2, rows, width), F32),
         pltpu.VMEM((2, rows, width), BF),
-        pltpu.VMEM((taps * rows, inner), BF),
-        pltpu.VMEM((5, 8, width), F32),
+        pltpu.VMEM((rows, taps * inner), BF),
+        pltpu.VMEM((micro * rows, inner), BF),
+        pltpu.VMEM((4, 8, width), F32),
         pltpu.VMEM((6, 8, inner), F32),
         pltpu.VMEM((total, BLOCK), BF),
         pltpu.VMEM((9, 16, inner), F32),
         *[buffers[k] for k in names],
+        dma((len(KINDS),)),
         dma((GROUPS, len(KINDS))),
-        dma((GROUPS, len(KINDS))),
-        dma((GROUPS, 2)),
+        dma((2,)),
         dma((len(SMALL_KINDS),)),
         dma((len(SMALL_KINDS),)),
         dma((micro + 3,)),
@@ -881,19 +891,83 @@
     )(ends, lengths, outer_gain, inner_gains, outer_biases, inner_biases, down, conv, up)
 
 
+def finish_kernel(
+    ends, rows, small, ends_out, outer_gain, inner_gains, outer_biases, inner_biases, down, conv, up, rms, raw, full, held,
+    ends_load, ends_store, load, store,
+):
+    micro, width = ends.shape[0], ends.shape[2]
+    into = [pltpu.make_async_copy(ends.at[mb], held.at[mb], ends_load.at[mb]) for mb in range(micro)]
+    out = [pltpu.make_async_copy(held.at[mb], ends_out.at[0, mb, 0], ends_store.at[mb]) for mb in range(micro)]
+    loads = [
+        pltpu.make_async_copy(rows.at[pl.ds(g * BLOCK, BLOCK)], raw.at[g], load.at[g]) for g in range(BLOCKS)
+    ]
+    for copy in into + loads:
+        copy.start()
+    outer_gain[0:1, 0:BLOCK] = small[0:1, :]
+    outer_gain[0:1, BLOCK:] = small[1:2, :]
+    inner_gains[0] = small[2:4, :]
+    for j in range(2):
+        outer_biases[0, j : j + 1, 0:BLOCK] = small[4 + 2 * j : 5 + 2 * j, :]
+        outer_biases[0, j : j + 1, BLOCK:] = small[5 + 2 * j : 6 + 2 * j, :]
+    inner_biases[0] = small[8:12, :]
+    squares = jnp.sum(small[12:14, :], axis=1, keepdims=True)
+    roots = jnp.sqrt(squares / (small[14:15, 0:1] * width))
+    rms[0:1, 0:1] = roots[0:1, :]
+    rms[0:1, 1:2] = roots[1:2, :]
+    places = [up.at[0, :, pl.ds(h * BLOCK, BLOCK)] for h in range(UP_BLOCKS)]
+    places += [conv.at[0, k] for k in range(FILTER_TAPS)]
+    places += [down.at[0, pl.ds(h * BLOCK, BLOCK)] for h in range(BLOCKS - DOWN_AT)]
+    stores = []
+    for mb in range(micro):
+        into[mb].wait()
+        out[mb].start()
+    for g in range(BLOCKS):
+        loads[g].wait()
+        full[g] = raw[g].astype(F32)
+        stores.append(pltpu.make_async_copy(full.at[g], places[g], store.at[g]))
+        stores[-1].start()
+    for copy in out + stores:
+        copy.wait()
+
+
+def finish(shapes, ends, rows, small):
+    anywhere = pl.BlockSpec(memory_space=pl.ANY)
+    vmem = pl.BlockSpec(memory_space=pltpu.VMEM)
+    dma = pltpu.SemaphoreType.DMA
+    return pl.pallas_call(
+        finish_kernel,
+        name="outputs",
+        out_shape=tuple(jax.ShapeDtypeStruct(shape, F32) for shape in shapes),
+        in_specs=[anywhere, anywhere, vmem],
+        out_specs=[anywhere, vmem, vmem, vmem, vmem, anywhere, anywhere, anywhere, vmem],
+        scratch_shapes=[
+            pltpu.VMEM((BLOCKS, BLOCK, BLOCK), BF),
+            pltpu.VMEM((BLOCKS, BLOCK, BLOCK), F32),
+            pltpu.VMEM(ends.shape, F32),
+            dma((ends.shape[0],)),
+            dma((ends.shape[0],)),
+            dma((BLOCKS,)),
+            dma((BLOCKS,)),
+        ],
+        compiler_params=pltpu.CompilerParams(vmem_limit_bytes=60 * 2**20),
+    )(ends, rows, small)
+
+
 def body(
     mesh_shape, ends_in, lengths, outer_gain, inner_gains, outer_biases, inner_biases, down_in, conv_weight, up_out
 ):
     width = ends_in.shape[-1]
     ends, rows, small = run_blocks(
         mesh_shape, ends_in.reshape(ends_in.shape[1], -1, width), lengths.reshape(-1), outer_gain, inner_gains[0],
-        outer_biases[0], inner_biases[0], down_in[0], conv_weight[0], up_out[0],
+        outer_biases[0], inner_biases[0], down_in[0], conv_weight[0].reshape(-1, conv_weight.shape[-1]), up_out[0],
     )
-    if (mesh_shape["dp"], mesh_shape["seq"]) != (4, 4):
-        rows, small = lax.psum((rows.astype(F32), small), ("dp", "seq"))
-    up = jnp.concatenate([rows[:BLOCK], rows[BLOCK : 2 * BLOCK]], axis=1).astype(F32)
-    conv = rows[2 * BLOCK : (2 + FILTER_TAPS) * BLOCK].reshape(conv_weight.shape[1:]).astype(F32)
-    down = rows[(2 + FILTER_TAPS) * BLOCK :].astype(F32)
+    if (mesh_shape["dp"], mesh_shape["seq"]) == (4, 4):
+        weights = (outer_gain, inner_gains, outer_biases, inner_biases, down_in, conv_weight, up_out)
+        return finish((ends_in.shape, *(w.shape for w in weights), (1, 2)), ends, rows, small)
+    rows, small = lax.psum((rows.astype(F32), small), ("dp", "seq"))
+    up = jnp.concatenate([rows[:BLOCK], rows[BLOCK : 2 * BLOCK]], axis=1)
+    conv = rows[UP_BLOCKS * BLOCK : DOWN_AT * BLOCK].reshape(conv_weight.shape[1:])
+    down = rows[DOWN_AT * BLOCK :]
     rms = jnp.sqrt(jnp.sum(small[12:14], axis=1) / (small[14, 0] * width))
     return (
         ends.reshape(ends_in.shape),

time: 263 us -> 204 us (0.78)
  Pallas kernels: 241 us -> 203 us
  other arithmetic: 10.4 us -> 0 us
  local copies, waits for them, and re-layouts: 9.7 us -> 0 us
    pallas_call x1, Pallas kernels: 241 us -> 191 us  [run_blocks(): pl.pallas_call(functools.partial(blocks_kernel, names, with_sums, mesh_sh...]
    pallas_call x0 -> x1, Pallas kernels: none -> 12.6 us  [finish(): pl.pallas_call(finish_kernel, name='outputs', out_shape=tuple((jax.ShapeD...]
    convert_element_type x2 -> x0, other arithmetic: 6.41 us -> none  [the longest x1 4.47 us: body(): rows[2 * BLOCK:(2 + FILTER_TAPS) * BLOCK].reshape(conv_weight.shape[1:])]
    unnamed x8 -> x0, local copies, waits for them, and re-layouts: 4.51 us -> none
where the time goes in v3:
time: 204 us
  Pallas kernels  203 us (100%)
    pallas_call x1, Pallas kernels, run_blocks(): pl.pallas_call(functools.partial(blocks_kernel, names, with_sums, mesh_sh...  191 us
    pallas_call x1, Pallas kernels, finish(): pl.pallas_call(finish_kernel, name='outputs', out_shape=tuple((jax.ShapeD...  12.6 us

profile of v3, /device:TPU:0, one launch (start us, length us, event | category | flops | bytes accessed | tf_op | source)
XLA Modules:
  0.0 204.1 jit_solution(9518999736147418041)
XLA Ops:
  0.6 190.7 %two_blocks.1 = (f32[4,256,1280]{2,1,0:T(8,128)}, bf16[5760,640]{1,0:T(8,128)(2,1)}, f32[16,640]{1,0:T(8,128)}) custom-call(bf16[4,256,1280]{2,1,0:T(8,128)(2,1)} %bitcast.9, s32[4]{0:T(128)} %bitcast.15, f32[1,1280]{1,0:T(1,128)} %outer_gain.1, f32[2,640]{1,0:T(2,128)} %bitcast.14, f32[2,1280]{1,0:T(2,128)} %bitcast.12, f32[4,640]{1,0:T(4,128)} %bitcast.13, ...), custom_call_target="tpu_custom_call" | custom-call | flops 22649241600 | bytes 41943040 | tf_op jit(solution)/shard_map/two_blocks/pallas_call | solution.py:878
  191.3 12.6 %outputs.1 = (f32[1,4,1,256,1280]{4,3,2,1,0:T(8,128)}, f32[1,1280]{1,0:T(1,128)}, f32[1,2,640]{2,1,0:T(2,128)}, f32[1,2,1280]{2,1,0:T(2,128)}, f32[1,4,640]{2,1,...) custom-call(f32[4,256,1280]{2,1,0:T(8,128)} %get-tuple-element.12.en, ...), custom_call_target="tpu_custom_call" | custom-call | tf_op jit(solution)/shard_map/outputs/pallas_call | solution.py:937

commit v4 on v3

--- a/solution.py
+++ b/solution.py
@@ -34,18 +34,20 @@
     "ru", "rv", "za", "zb", "zc", "av", "au", "aw",
     "ze", "zm", "zo", "ex", "ey", "ge", "gn", "gd", "gf", "gp", "gq",
 )
+ARRIVES = dict(ru=0, rv=1, av=2, au=3, aw=4, ex=5, ey=6, za=7, zb=8, ze=9, zm=10, ge=11, gn=12, gf=13,
+               zc=7, zo=8, gd=9, gp=10, gq=11)
 SMALL_KINDS = ("sx", "sy", "sa", "sb", "sc")
 RECEIVE = dict(ru=HALF, rv=QUARTER, za=QUARTER, zb=QUARTER, fl=QUARTER, ze=3 * CHUNK, zm=2 * CHUNK,
                zo=CHUNK, ex=CHUNK, ey=CHUNK, tx=CHUNK, fz=CHUNK)
 L_LEVELS = 8
 Z_LEVELS = 9
-L_STRIDE, Z_STRIDE, Z_LATE, GAP = 1, 1, 0, 1
-FA, FB, WU, BA, BB, WC, WD = range(1, 8)
+L_STRIDE, Z_STRIDE, Z_LATE, GAP = 2, 2, 0, 1
+FA, FB, WU, BA, BB, BC, WC, WD = range(1, 9)
 FIRST_PLAN = (
-    (FA, 0, 0), (FA, 1, 0), (FB, 0, 0), (FA, 2, 0), (FB, 1, 0), (FA, 3, 0), (FB, 2, 0), (FB, 3, 0), (BA, 0, 0), (BA, 1, 0), (BB, 0, 0), (BA, 2, 0), (BB, 1, 0), (WU, 0, 1), (BA, 3, 0), (BB, 2, 0), (BB, 3, 1), (WC, 0, 1), (WC, 1, 1), (WC, 2, 1), (WC, 3, 1), (WC, 4, 1), (WD, 0, 2),
+    (FA, 0, 0), (FA, 1, 0), (FB, 0, 0), (FA, 2, 0), (FB, 1, 0), (FA, 3, 0), (FB, 2, 0), (FB, 3, 0), (BA, 0, 0), (BA, 1, 0), (BB, 0, 0), (BC, 0, 0), (BA, 2, 0), (BB, 1, 0), (BC, 1, 0), (WU, 0, 0), (BA, 3, 1), (BB, 2, 0), (BC, 2, 1), (BB, 3, 0), (BC, 3, 1), (WC, 0, 0), (WC, 1, 0), (WC, 2, 3), (WC, 3, 3), (WC, 4, 1), (WD, 0, 0),
 )
 SECOND_PLAN = (
-    (FA, 0, 0), (FA, 1, 0), (FB, 0, 0), (FA, 2, 0), (FB, 1, 0), (FA, 3, 0), (FB, 2, 0), (BA, 0, 0), (FB, 3, 0), (WU, 0, 1), (BA, 1, 0), (BA, 2, 0), (BA, 3, 0), (BB, 0, 1), (BB, 1, 1), (BB, 2, 1), (BB, 3, 1), (WC, 0, 1), (WC, 1, 1), (WC, 2, 1), (WC, 3, 1), (WC, 4, 1), (WD, 0, 2),
+    (FA, 0, 0), (FA, 1, 0), (FB, 0, 0), (FA, 2, 0), (FB, 1, 0), (FA, 3, 0), (FB, 2, 0), (BA, 0, 0), (FB, 3, 0), (WU, 0, 1), (BA, 1, 0), (BB, 0, 0), (BC, 0, 1), (BA, 2, 1), (BB, 1, 0), (BC, 1, 1), (BA, 3, 1), (BB, 2, 0), (BC, 2, 1), (WC, 0, 1), (WC, 1, 1), (BB, 3, 0), (BC, 3, 1), (WC, 2, 1), (WC, 3, 1), (WC, 4, 1), (WD, 0, 1),
 )
 
 
@@ -109,7 +111,7 @@
     def copy(self, kind, g, source, target, to):
         j = KINDS.index(kind)
         return pltpu.make_async_remote_copy(
-            src_ref=source, dst_ref=target, send_sem=self.send.at[j], recv_sem=self.recv.at[g, j],
+            src_ref=source, dst_ref=target, send_sem=self.send.at[j], recv_sem=self.recv.at[g, ARRIVES[kind]],
             device_id=to, device_id_type=MESH)
 
     def square(self, g):
@@ -641,6 +643,8 @@
         when(jnp.logical_and(first, mb == 0), met)
         halo_start(CW, 0, mb)
 
+    halves = [slice(h * (rows // 2), (h + 1) * (rows // 2)) for h in range(2)]
+
     def forward_b(mb):
         slot = lax.rem(mb, 2)
         halo_arrived(CW, 0, mb)
@@ -656,17 +660,30 @@
             when(second, lambda: store_end(mb - 2).wait())
 
         all_shifted(CW, mb, 1)
-        n, _, scale, _ = normed(nn(taps[...], conv[...]) + inner_biases[3:4, :])
-        NC[mb] = n
-        ST[mb, :, 3:4] = scale
-        valid = valid_of(mb)
-        hidden = (gelu(n * inner_half_c + inner_shift_c) * valid).astype(BF)
-        HC[mb] = hidden
-        branch = (nn(hidden, up[...]) + outer_biases[1:2, :]) * valid
-        oacc[3] += fold(branch * branch)
-        value = X[mb].astype(F32) + branch
-        wide[slot] = value
-        handing[slot] = value.astype(BF)
+
+        def norm_c(half, product):
+            n, _, scale, _ = normed(product + inner_biases[3:4, :])
+            NC[mb, half, :] = n
+            ST[mb, half, 3:4] = scale
+            hidden = (gelu(n * inner_half_c + inner_shift_c) * valid_of(mb)[half, :]).astype(BF)
+            HC[mb, half, :] = hidden
+            return hidden
+
+        def close(half, product):
+            branch = (product + outer_biases[1:2, :]) * valid_of(mb)[half, :]
+            oacc[3] += fold(branch * branch)
+            value = X[mb, half, :].astype(F32) + branch
+            wide[slot, half, :] = value
+            handing[slot, half, :] = value.astype(BF)
+
+        lower = nn(taps[halves[0], :], conv[...])
+        upper = nn(taps[halves[1], :], conv[...])
+        hidden = norm_c(halves[0], lower)
+        lower = nn(hidden, up[...])
+        hidden = norm_c(halves[1], upper)
+        upper = nn(hidden, up[...])
+        close(halves[0], lower)
+        close(halves[1], upper)
         when(first, lambda: hand_over(mb, X).start())
         when(second, lambda: store_end(mb).start())
 
@@ -690,19 +707,7 @@
         halo_start(GCW, 1, mb)
 
     def backward_b(mb):
-        slot = lax.rem(mb, 2)
         halo_arrived(GCW, 1, mb)
-
-        @pl.when(mb < 2)
-        def _():
-            when(first, lambda: hand_over(mb + micro - 2, X).wait_send())
-            when(second, lambda: store_end(mb + micro - 2).wait())
-
-        @pl.when(mb >= 2)
-        def _():
-            when(second, lambda: hand_over(mb - 2, GY).wait_send())
-            when(first, lambda: store_end(mb - 2).wait())
-
         all_shifted(GCW, mb, -1)
         total = nt(taps[:, 0:inner], conv[0:inner, :])
         for k in range(1, FILTER_TAPS):
@@ -713,11 +718,24 @@
         iacc[0] += fold(terms)
         iacc[1] += fold(dv)
         iacc[2] += fold(dz)
-        low = dz.astype(BF)
-        GP[mb] = low
+        GP[mb] = dz.astype(BF)
+
+    def backward_c(mb):
+        slot = lax.rem(mb, 2)
+
+        @pl.when(mb < 2)
+        def _():
+            when(first, lambda: hand_over(mb + micro - 2, X).wait_send())
+            when(second, lambda: store_end(mb + micro - 2).wait())
+
+        @pl.when(mb >= 2)
+        def _():
+            when(second, lambda: hand_over(mb - 2, GY).wait_send())
+            when(first, lambda: store_end(mb - 2).wait())
+
         scale = ST[mb, :, 1:2]
         n = (X[mb].astype(F32) - ST[mb, :, 0:1]) * scale
-        dv, terms, dz = norm_gelu_back(nt(low, down[...]), n, scale, outer_gain[...], outer_half, outer_shift)
+        dv, terms, dz = norm_gelu_back(nt(GP[mb], down[...]), n, scale, outer_gain[...], outer_half, outer_shift)
         oacc[0] += fold(terms)
         oacc[1] += fold(dv)
         value = GY[mb].astype(F32) + dz
@@ -790,7 +808,7 @@
         for j, (a, b) in enumerate(zip(*plans)):
             entry = jnp.where(i == j, jnp.where(first, a, b), entry)
         what, k = entry // 64, lax.rem(entry // 8, 8)
-        for p, act in ((FA, forward_a), (FB, forward_b), (BA, backward_a), (BB, backward_b), (WC, weight_tap)):
+        for p, act in ((FA, forward_a), (FB, forward_b), (BA, backward_a), (BB, backward_b), (BC, backward_c), (WC, weight_tap)):
             when(what == p, functools.partial(act, k))
         when(what == WU, weight_up)
 
@@ -863,7 +881,7 @@
         pltpu.VMEM((9, 16, inner), F32),
         *[buffers[k] for k in names],
         dma((len(KINDS),)),
-        dma((GROUPS, len(KINDS))),
+        dma((GROUPS, max(ARRIVES.values()) + 1)),
         dma((2,)),
         dma((len(SMALL_KINDS),)),
         dma((len(SMALL_KINDS),)),

time: 204 us -> 188 us (0.922)
  Pallas kernels: 203 us -> 187 us
    pallas_call x1, Pallas kernels: 191 us -> 175 us  [run_blocks(): pl.pallas_call(functools.partial(blocks_kernel, names, with_sums, mesh_sh...]
where the time goes in v4:
time: 188 us
  Pallas kernels  187 us (99%)
    pallas_call x1, Pallas kernels, run_blocks(): pl.pallas_call(functools.partial(blocks_kernel, names, with_sums, mesh_sh...  175 us
    pallas_call x1, Pallas kernels, finish(): pl.pallas_call(finish_kernel, name='outputs', out_shape=tuple((jax.ShapeD...  12.6 us

profile of v4, /device:TPU:0, one launch (start us, length us, event | category | flops | bytes accessed | tf_op | source)
XLA Modules:
  0.0 188.1 jit_solution(1921777014086053425)
XLA Ops:
  0.6 174.9 %two_blocks.1 = (f32[4,256,1280]{2,1,0:T(8,128)}, bf16[5760,640]{1,0:T(8,128)(2,1)}, f32[16,640]{1,0:T(8,128)}) custom-call(bf16[4,256,1280]{2,1,0:T(8,128)(2,1)} %bitcast.9, s32[4]{0:T(128)} %bitcast.15, f32[1,1280]{1,0:T(1,128)} %outer_gain.1, f32[2,640]{1,0:T(2,128)} %bitcast.14, f32[2,1280]{1,0:T(2,128)} %bitcast.12, f32[4,640]{1,0:T(4,128)} %bitcast.13, ...), custom_call_target="tpu_custom_call" | custom-call | flops 22649241600 | bytes 41943040 | tf_op jit(solution)/shard_map/two_blocks/pallas_call | solution.py:896
  175.6 12.6 %outputs.1 = (f32[1,4,1,256,1280]{4,3,2,1,0:T(8,128)}, f32[1,1280]{1,0:T(1,128)}, f32[1,2,640]{2,1,0:T(2,128)}, f32[1,2,1280]{2,1,0:T(2,128)}, f32[1,4,640]{2,1,...) custom-call(f32[4,256,1280]{2,1,0:T(8,128)} %get-tuple-element.12.en, ...), custom_call_target="tpu_custom_call" | custom-call | tf_op jit(solution)/shard_map/outputs/pallas_call | solution.py:955

commit v5 on v4

--- a/solution.py
+++ b/solution.py
@@ -41,7 +41,9 @@
                zo=CHUNK, ex=CHUNK, ey=CHUNK, tx=CHUNK, fz=CHUNK)
 L_LEVELS = 8
 Z_LEVELS = 9
-L_STRIDE, Z_STRIDE, Z_LATE, GAP = 2, 2, 0, 1
+FIRST_PACE = (2, 2, 0, 1)
+SECOND_PACE = (2, 2, 0, 1)
+
 FA, FB, WU, BA, BB, BC, WC, WD = range(1, 9)
 FIRST_PLAN = (
     (FA, 0, 0), (FA, 1, 0), (FB, 0, 0), (FA, 2, 0), (FB, 1, 0), (FA, 3, 0), (FB, 2, 0), (FB, 3, 0), (BA, 0, 0), (BA, 1, 0), (BB, 0, 0), (BC, 0, 0), (BA, 2, 0), (BB, 1, 0), (BC, 1, 0), (WU, 0, 0), (BA, 3, 1), (BB, 2, 0), (BC, 2, 1), (BB, 3, 0), (BC, 3, 1), (WC, 0, 0), (WC, 1, 0), (WC, 2, 3), (WC, 3, 3), (WC, 4, 1), (WD, 0, 0),
@@ -51,7 +53,7 @@
 )
 
 
-def begins_of(plan):
+def begins_of(plan, pace):
     ready, steps = {}, 0
     for what, k, count in plan:
         for block in {WU: range(UP_BLOCKS), WC: (UP_BLOCKS + k,), WD: range(DOWN_AT, BLOCKS)}.get(what, ()):
@@ -60,12 +62,18 @@
     begins = []
     for g in range(GROUPS):
         there = max(ready[block] for block in range(g * ROWS // BLOCK, ((g + 1) * ROWS - 1) // BLOCK + 1))
-        begins.append(max(there, begins[-1] + GAP) if begins else there)
+        begins.append(max(there, begins[-1] + pace[3]) if begins else there)
     return begins
 
 
-def steps_of(plan):
-    return begins_of(plan)[-1] + max(L_STRIDE * (L_LEVELS - 1), Z_LATE + Z_STRIDE * (Z_LEVELS - 1)) + 1
+def planned_steps(plan):
+    return sum(entry[2] for entry in plan)
+
+
+def steps_of(plan, pace):
+    square, line, late, _ = pace
+    last = begins_of(plan, pace)[-1] + max(square * (L_LEVELS - 1), late + line * (Z_LEVELS - 1))
+    return max(last + 1, planned_steps(plan) + 6)
 
 
 def aligned(offset):
@@ -359,22 +367,28 @@
             def _():
                 copy("sc").wait_recv()
 
-    def tick(self, t, begins, small_begin):
+    def tick(self, t, begins, pace, small_begin):
+        square, line, late = pace
+
+        def beginning(step):
+            g = jnp.int32(-1)
+            for j, begin in enumerate(begins):
+                g = jnp.where(step == begin, j, g)
+            return g
+
         for level in reversed(range(Z_LEVELS)):
-            for kind, stride, late, act in (
-                (0, L_STRIDE, 0, self.square_level),
-                (1, Z_STRIDE, Z_LATE, self.line_level),
-            ):
-                if kind == 0 and level >= L_LEVELS:
-                    continue
-                step = t - late - stride * level
-                g = jnp.int32(-1)
-                for j, begin in enumerate(begins):
-                    g = jnp.where(step == begin, j, g)
-
-                @pl.when(g >= 0)
+            g = beginning(t - late - line * level)
+            if level < L_LEVELS:
+                same = square is line and isinstance(late, int) and late == 0
+                g_square = g if same else beginning(t - square * level)
+
+                @pl.when(g_square >= 0)
                 def _():
-                    act(g, level)
+                    self.square_level(g_square, level)
+
+            @pl.when(g >= 0)
+            def _():
+                self.line_level(g, level)
 
         for level in range(6):
 
@@ -475,7 +489,7 @@
     names, with_sums, last,
     ends, lengths, outer_gain, inner_gains, outer_biases, inner_biases, down_hbm, conv_hbm, up_hbm,
     ends_out, res, small_out,
-    down, conv, up, X, GY, HA, CW, HC, GCW, GP, NB, NC, ST, XS, wide, handing, taps, lhs, oacc, iacc, grad, small,
+    down, conv, up, X, GY, HA, CW, HC, GCW, GP, NB, NC, ST, XS, handing, taps, lhs, oacc, iacc, grad, small,
     *rest,
 ):
     buffers = dict(zip(names, rest[: len(names)]))
@@ -616,7 +630,7 @@
             device_id=across, device_id_type=MESH)
 
     def store_end(mb):
-        return pltpu.make_async_copy(wide.at[lax.rem(mb, 2)], ends_out.at[mb], store.at[mb])
+        return pltpu.make_async_copy(handing.at[lax.rem(mb, 2)], ends_out.at[mb], store.at[mb])
 
     own = pl.ds(rows, rows)
     outer_shift, inner_shift_b, inner_shift_c = 0.5 * outer_biases[0:1, :], 0.5 * inner_biases[0:1, :], 0.5 * inner_biases[1:2, :]
@@ -673,7 +687,6 @@
             branch = (product + outer_biases[1:2, :]) * valid_of(mb)[half, :]
             oacc[3] += fold(branch * branch)
             value = X[mb, half, :].astype(F32) + branch
-            wide[slot, half, :] = value
             handing[slot, half, :] = value.astype(BF)
 
         lower = nn(taps[halves[0], :], conv[...])
@@ -739,17 +752,15 @@
         oacc[0] += fold(terms)
         oacc[1] += fold(dv)
         value = GY[mb].astype(F32) + dz
-        wide[slot] = value
         handing[slot] = value.astype(BF)
         when(second, lambda: hand_over(mb, GY).start())
         when(first, lambda: store_end(mb).start())
 
     def weight_up():
         when(first, lambda: hand_over(micro - 1, GY).wait_recv())
-        c = HC[...].reshape(micro * rows, inner)
+        total = tn(HC[...].reshape(micro * rows, inner), GY[...].reshape(micro * rows, width)).astype(BF)
         for h in range(UP_BLOCKS):
-            y = GY[:, :, h * inner : (h + 1) * inner].reshape(micro * rows, inner)
-            grad[h * BLOCK : (h + 1) * BLOCK, :] = tn(c, y).astype(BF)
+            grad[h * BLOCK : (h + 1) * BLOCK, :] = total[:, h * inner : (h + 1) * inner]
 
     def weight_tap(tap):
         for k in range(FILTER_TAPS):
@@ -796,11 +807,18 @@
 
     when(second, met)
     plans = [[(p * 8 + k) * 8 + steps for p, k, steps in plan] for plan in (FIRST_PLAN, SECOND_PLAN)]
-    begins = [jnp.where(first, a, b) for a, b in zip(begins_of(FIRST_PLAN), begins_of(SECOND_PLAN))]
-    ticks = jnp.where(first, steps_of(FIRST_PLAN), steps_of(SECOND_PLAN))
+    def mine(a, b):
+        return a if a == b else jnp.where(first, a, b)
+
+    begins = [mine(a, b) for a, b in zip(begins_of(FIRST_PLAN, FIRST_PACE), begins_of(SECOND_PLAN, SECOND_PACE))]
+    square, line, late = (mine(a, b) for a, b in zip(FIRST_PACE[:3], SECOND_PACE[:3]))
+    same = FIRST_PACE[0] == FIRST_PACE[1] and SECOND_PACE[0] == SECOND_PACE[1]
+    pace = (line if same else square, line, late)
+    planned = mine(planned_steps(FIRST_PLAN), planned_steps(SECOND_PLAN))
+    ticks = mine(steps_of(FIRST_PLAN, FIRST_PACE), steps_of(SECOND_PLAN, SECOND_PACE))
 
     def tick(t, carry):
-        sums.tick(t, begins, begins[-1])
+        sums.tick(t, begins, pace, planned)
         return carry
 
     def step(i, t):
@@ -811,18 +829,14 @@
         for p, act in ((FA, forward_a), (FB, forward_b), (BA, backward_a), (BB, backward_b), (BC, backward_c), (WC, weight_tap)):
             when(what == p, functools.partial(act, k))
         when(what == WU, weight_up)
-
-        @pl.when(what == WD)
-        def _():
-            smalls()
-            weight_down()
-
+        when(what == WD, weight_down)
         then = t + lax.rem(entry, 8)
         if with_sums:
             lax.fori_loop(t, then, tick, 0)
         return then
 
     t = lax.fori_loop(0, len(FIRST_PLAN), step, jnp.int32(0))
+    smalls()
 
     if with_sums:
         lax.fori_loop(t, ticks, tick, 0)
@@ -871,7 +885,6 @@
         pltpu.VMEM((micro, rows, inner), F32),
         pltpu.VMEM((micro, rows, 128), F32),
         pltpu.VMEM((rows, 1), F32),
-        pltpu.VMEM((2, rows, width), F32),
         pltpu.VMEM((2, rows, width), BF),
         pltpu.VMEM((rows, taps * inner), BF),
         pltpu.VMEM((micro * rows, inner), BF),
@@ -897,7 +910,7 @@
         functools.partial(blocks_kernel, names, with_sums, mesh_shape["seq"] - 1),
         name="two_blocks",
         out_shape=(
-            jax.ShapeDtypeStruct((micro, rows, width), F32),
+            jax.ShapeDtypeStruct((micro, rows, width), BF),
             jax.ShapeDtypeStruct((total, BLOCK), BF),
             jax.ShapeDtypeStruct((16, inner), F32),
         ),
@@ -909,17 +922,22 @@
     )(ends, lengths, outer_gain, inner_gains, outer_biases, inner_biases, down, conv, up)
 
 
+AHEAD = 6
+
+
 def finish_kernel(
-    ends, rows, small, ends_out, outer_gain, inner_gains, outer_biases, inner_biases, down, conv, up, rms, raw, full, held,
-    ends_load, ends_store, load, store,
+    ends, rows, small, ends_out, outer_gain, inner_gains, outer_biases, inner_biases, down, conv, up, rms,
+    raw, full, held, wide, load, store,
 ):
     micro, width = ends.shape[0], ends.shape[2]
-    into = [pltpu.make_async_copy(ends.at[mb], held.at[mb], ends_load.at[mb]) for mb in range(micro)]
-    out = [pltpu.make_async_copy(held.at[mb], ends_out.at[0, mb, 0], ends_store.at[mb]) for mb in range(micro)]
-    loads = [
-        pltpu.make_async_copy(rows.at[pl.ds(g * BLOCK, BLOCK)], raw.at[g], load.at[g]) for g in range(BLOCKS)
-    ]
-    for copy in into + loads:
+    places = [up.at[0, :, pl.ds(h * BLOCK, BLOCK)] for h in range(UP_BLOCKS)]
+    places += [conv.at[0, k] for k in range(FILTER_TAPS)]
+    places += [down.at[0, pl.ds(h * BLOCK, BLOCK)] for h in range(BLOCKS - DOWN_AT)]
+    moves = [(rows.at[pl.ds(g * BLOCK, BLOCK)], raw.at[g], full.at[g], places[g]) for g in range(BLOCKS)]
+    moves += [(ends.at[mb], held.at[mb], wide.at[mb], ends_out.at[0, mb, 0]) for mb in range(micro)]
+    loads = [pltpu.make_async_copy(m[0], m[1], load.at[i]) for i, m in enumerate(moves)]
+    stores = [pltpu.make_async_copy(m[2], m[3], store.at[i]) for i, m in enumerate(moves)]
+    for copy in loads[:AHEAD]:
         copy.start()
     outer_gain[0:1, 0:BLOCK] = small[0:1, :]
     outer_gain[0:1, BLOCK:] = small[1:2, :]
@@ -932,19 +950,13 @@
     roots = jnp.sqrt(squares / (small[14:15, 0:1] * width))
     rms[0:1, 0:1] = roots[0:1, :]
     rms[0:1, 1:2] = roots[1:2, :]
-    places = [up.at[0, :, pl.ds(h * BLOCK, BLOCK)] for h in range(UP_BLOCKS)]
-    places += [conv.at[0, k] for k in range(FILTER_TAPS)]
-    places += [down.at[0, pl.ds(h * BLOCK, BLOCK)] for h in range(BLOCKS - DOWN_AT)]
-    stores = []
-    for mb in range(micro):
-        into[mb].wait()
-        out[mb].start()
-    for g in range(BLOCKS):
-        loads[g].wait()
-        full[g] = raw[g].astype(F32)
-        stores.append(pltpu.make_async_copy(full.at[g], places[g], store.at[g]))
-        stores[-1].start()
-    for copy in out + stores:
+    for i, (_, source, target, _) in enumerate(moves):
+        loads[i].wait()
+        if i + AHEAD < len(moves):
+            loads[i + AHEAD].start()
+        target[...] = source[...].astype(F32)
+        stores[i].start()
+    for copy in stores:
         copy.wait()
 
 
@@ -961,11 +973,10 @@
         scratch_shapes=[
             pltpu.VMEM((BLOCKS, BLOCK, BLOCK), BF),
             pltpu.VMEM((BLOCKS, BLOCK, BLOCK), F32),
+            pltpu.VMEM(ends.shape, BF),
             pltpu.VMEM(ends.shape, F32),
-            dma((ends.shape[0],)),
-            dma((ends.shape[0],)),
-            dma((BLOCKS,)),
-            dma((BLOCKS,)),
+            dma((BLOCKS + ends.shape[0],)),
+            dma((BLOCKS + ends.shape[0],)),
         ],
         compiler_params=pltpu.CompilerParams(vmem_limit_bytes=60 * 2**20),
     )(ends, rows, small)
@@ -988,7 +999,7 @@
     down = rows[DOWN_AT * BLOCK :]
     rms = jnp.sqrt(jnp.sum(small[12:14], axis=1) / (small[14, 0] * width))
     return (
-        ends.reshape(ends_in.shape),
+        ends.astype(F32).reshape(ends_in.shape),
         small[0:2].reshape(1, -1),
         small[None, 2:4],
         small[4:8].reshape(1, 2, -1),

time: 188 us -> 185 us (0.984)
  Pallas kernels: 187 us -> 184 us
    pallas_call x1, Pallas kernels: 175 us -> 172 us  [run_blocks(): pl.pallas_call(functools.partial(blocks_kernel, names, with_sums, mesh_sh...]
where the time goes in v5:
time: 185 us; the launch traced here: 184 us
  Pallas kernels  184 us (99%)
    pallas_call x1, Pallas kernels, run_blocks(): pl.pallas_call(functools.partial(blocks_kernel, names, with_sums, mesh_sh...  172 us
    pallas_call x1, Pallas kernels, finish(): pl.pallas_call(finish_kernel, name='outputs', out_shape=tuple((jax.ShapeD...  11.2 us

profile of v5, /device:TPU:0, one launch (start us, length us, event | category | flops | bytes accessed | tf_op | source)
XLA Modules:
  0.0 184.4 jit_solution(16968953797270360438)
XLA Ops:
  0.6 172.5 %two_blocks.1 = (bf16[4,256,1280]{2,1,0:T(8,128)(2,1)}, bf16[5760,640]{1,0:T(8,128)(2,1)}, f32[16,640]{1,0:T(8,128)}) custom-call(bf16[4,256,1280]{2,1,0:T(8,128)(2,1)} %bitcast.9, s32[4]{0:T(128)} %bitcast.15, f32[1,1280]{1,0:T(1,128)} %outer_gain.1, f32[2,640]{1,0:T(2,128)} %bitcast.14, f32[2,1280]{1,0:T(2,128)} %bitcast.12, f32[4,640]{1,0:T(4,128)} %bitcast.13, ...), custom_call_target="tpu_custom_call" | custom-call | flops 22649241600 | bytes 41943040 | tf_op jit(solution)/shard_map/two_blocks/pallas_call | solution.py:909
  173.1 11.2 %outputs.1 = (f32[1,4,1,256,1280]{4,3,2,1,0:T(8,128)}, f32[1,1280]{1,0:T(1,128)}, f32[1,2,640]{2,1,0:T(2,128)}, f32[1,2,1280]{2,1,0:T(2,128)}, f32[1,4,640]{2,1,...) custom-call(bf16[4,256,1280]{2,1,0:T(8,128)(2,1)} %get-tuple-element, ...), custom_call_target="tpu_custom_call" | custom-call | tf_op jit(solution)/shard_map/outputs/pallas_call | solution.py:967

commit v6 on v5

--- a/solution.py
+++ b/solution.py
@@ -46,10 +46,10 @@
 
 FA, FB, WU, BA, BB, BC, WC, WD = range(1, 9)
 FIRST_PLAN = (
-    (FA, 0, 0), (FA, 1, 0), (FB, 0, 0), (FA, 2, 0), (FB, 1, 0), (FA, 3, 0), (FB, 2, 0), (FB, 3, 0), (BA, 0, 0), (BA, 1, 0), (BB, 0, 0), (BC, 0, 0), (BA, 2, 0), (BB, 1, 0), (BC, 1, 0), (WU, 0, 0), (BA, 3, 1), (BB, 2, 0), (BC, 2, 1), (BB, 3, 0), (BC, 3, 1), (WC, 0, 0), (WC, 1, 0), (WC, 2, 3), (WC, 3, 3), (WC, 4, 1), (WD, 0, 0),
+    (FA, 0, 0), (FA, 1, 0), (FB, 0, 0), (FA, 2, 0), (FB, 1, 0), (FA, 3, 0), (FB, 2, 0), (FB, 3, 0), (BA, 0, 0), (BA, 1, 0), (BB, 0, 0), (BC, 0, 0), (BA, 2, 0), (BB, 1, 0), (BC, 1, 0), (BB, 2, 0), (WU, 0, 0), (BA, 3, 1), (BC, 2, 3), (BB, 3, 0), (BC, 3, 1), (WC, 0, 0), (WC, 1, 0), (WC, 2, 3), (WC, 3, 2), (WC, 4, 1), (WD, 0, 0),
 )
 SECOND_PLAN = (
-    (FA, 0, 0), (FA, 1, 0), (FB, 0, 0), (FA, 2, 0), (FB, 1, 0), (FA, 3, 0), (FB, 2, 0), (BA, 0, 0), (FB, 3, 0), (WU, 0, 1), (BA, 1, 0), (BB, 0, 0), (BC, 0, 1), (BA, 2, 1), (BB, 1, 0), (BC, 1, 1), (BA, 3, 1), (BB, 2, 0), (BC, 2, 1), (WC, 0, 1), (WC, 1, 1), (BB, 3, 0), (BC, 3, 1), (WC, 2, 1), (WC, 3, 1), (WC, 4, 1), (WD, 0, 1),
+    (FA, 0, 0), (FA, 1, 0), (FB, 0, 0), (FA, 2, 0), (FB, 1, 0), (FA, 3, 0), (FB, 2, 0), (BA, 0, 0), (FB, 3, 0), (WU, 0, 1), (BA, 1, 0), (BB, 0, 0), (BC, 0, 1), (BA, 2, 1), (BB, 1, 0), (BC, 1, 1), (BA, 3, 1), (BB, 2, 0), (BC, 2, 1), (WC, 0, 1), (WC, 1, 0), (BB, 3, 1), (WC, 2, 1), (BC, 3, 0), (WC, 3, 1), (WC, 4, 1), (WD, 0, 1),
 )
 
 

time: 185 us -> 182 us (0.984)
  Pallas kernels: 184 us -> 181 us
    pallas_call x1, Pallas kernels: 172 us -> 170 us  [run_blocks(): pl.pallas_call(functools.partial(blocks_kernel, names, with_sums, mesh_sh...]
where the time goes in v6:
time: 182 us
  Pallas kernels  181 us (99%)
    pallas_call x1, Pallas kernels, run_blocks(): pl.pallas_call(functools.partial(blocks_kernel, names, with_sums, mesh_sh...  170 us
    pallas_call x1, Pallas kernels, finish(): pl.pallas_call(finish_kernel, name='outputs', out_shape=tuple((jax.ShapeD...  11.2 us

profile of v6, /device:TPU:0, one launch (start us, length us, event | category | flops | bytes accessed | tf_op | source)
XLA Modules:
  0.0 182.2 jit_solution(16193725538912899138)
XLA Ops:
  0.6 170.2 %two_blocks.1 = (bf16[4,256,1280]{2,1,0:T(8,128)(2,1)}, bf16[5760,640]{1,0:T(8,128)(2,1)}, f32[16,640]{1,0:T(8,128)}) custom-call(bf16[4,256,1280]{2,1,0:T(8,128)(2,1)} %bitcast.9, s32[4]{0:T(128)} %bitcast.15, f32[1,1280]{1,0:T(1,128)} %outer_gain.1, f32[2,640]{1,0:T(2,128)} %bitcast.14, f32[2,1280]{1,0:T(2,128)} %bitcast.12, f32[4,640]{1,0:T(4,128)} %bitcast.13, ...), custom_call_target="tpu_custom_call" | custom-call | flops 22649241600 | bytes 41943040 | tf_op jit(solution)/shard_map/two_blocks/pallas_call | solution.py:909
  170.8 11.2 %outputs.1 = (f32[1,4,1,256,1280]{4,3,2,1,0:T(8,128)}, f32[1,1280]{1,0:T(1,128)}, f32[1,2,640]{2,1,0:T(2,128)}, f32[1,2,1280]{2,1,0:T(2,128)}, f32[1,4,640]{2,1,...) custom-call(bf16[4,256,1280]{2,1,0:T(8,128)(2,1)} %get-tuple-element, ...), custom_call_target="tpu_custom_call" | custom-call | tf_op jit(solution)/shard_map/outputs/pallas_call | solution.py:967

commit v7 on v6

--- a/solution.py
+++ b/solution.py
@@ -46,10 +46,10 @@
 
 FA, FB, WU, BA, BB, BC, WC, WD = range(1, 9)
 FIRST_PLAN = (
-    (FA, 0, 0), (FA, 1, 0), (FB, 0, 0), (FA, 2, 0), (FB, 1, 0), (FA, 3, 0), (FB, 2, 0), (FB, 3, 0), (BA, 0, 0), (BA, 1, 0), (BB, 0, 0), (BC, 0, 0), (BA, 2, 0), (BB, 1, 0), (BC, 1, 0), (BB, 2, 0), (WU, 0, 0), (BA, 3, 1), (BC, 2, 3), (BB, 3, 0), (BC, 3, 1), (WC, 0, 0), (WC, 1, 0), (WC, 2, 3), (WC, 3, 2), (WC, 4, 1), (WD, 0, 0),
+    (FA, 0, 0), (FA, 1, 0), (FB, 0, 0), (FA, 2, 0), (FB, 1, 0), (FA, 3, 0), (FB, 2, 0), (FB, 3, 0), (BA, 0, 0), (BA, 1, 0), (BB, 0, 0), (BC, 0, 0), (BA, 2, 0), (BB, 1, 0), (BC, 1, 0), (BB, 2, 0), (WU, 0, 0), (BA, 3, 1), (BC, 2, 3), (BB, 3, 0), (BC, 3, 2), (WC, 0, 0), (WC, 1, 0), (WC, 2, 3), (WC, 3, 0), (WC, 4, 1), (WD, 0, 0),
 )
 SECOND_PLAN = (
-    (FA, 0, 0), (FA, 1, 0), (FB, 0, 0), (FA, 2, 0), (FB, 1, 0), (FA, 3, 0), (FB, 2, 0), (BA, 0, 0), (FB, 3, 0), (WU, 0, 1), (BA, 1, 0), (BB, 0, 0), (BC, 0, 1), (BA, 2, 1), (BB, 1, 0), (BC, 1, 1), (BA, 3, 1), (BB, 2, 0), (BC, 2, 1), (WC, 0, 1), (WC, 1, 0), (BB, 3, 1), (WC, 2, 1), (BC, 3, 0), (WC, 3, 1), (WC, 4, 1), (WD, 0, 1),
+    (FA, 0, 0), (FA, 1, 0), (FB, 0, 0), (FA, 2, 0), (FB, 1, 0), (FA, 3, 0), (FB, 2, 0), (BA, 0, 0), (FB, 3, 0), (WU, 0, 1), (BA, 1, 0), (BB, 0, 0), (BC, 0, 1), (BA, 2, 1), (BB, 1, 0), (BC, 1, 1), (BA, 3, 1), (BB, 2, 0), (BC, 2, 1), (WC, 0, 1), (WC, 1, 0), (BB, 3, 1), (WC, 2, 1), (BC, 3, 1), (WC, 3, 1), (WC, 4, 1), (WD, 0, 1),
 )
 
 
@@ -623,11 +623,29 @@
                     at = rows + sign * (k - REACH) * dilation
                     taps[:, k * inner : (k + 1) * inner] = ref[mb, pl.ds(at, rows), :]
 
-    def hand_over(mb, target):
-        slot = lax.rem(mb, 2)
-        return pltpu.make_async_remote_copy(
-            src_ref=handing.at[slot], dst_ref=target.at[mb], send_sem=hand_send.at[mb], recv_sem=hand_recv.at[mb],
-            device_id=across, device_id_type=MESH)
+    class HandOver:
+        def __init__(self, mb, target):
+            slot, half = lax.rem(mb, 2), rows // 2
+            self.halves = [
+                pltpu.make_async_remote_copy(
+                    src_ref=handing.at[slot, pl.ds(h * half, half)], dst_ref=target.at[mb, pl.ds(h * half, half)],
+                    send_sem=hand_send.at[mb, h], recv_sem=hand_recv.at[mb, h], device_id=across, device_id_type=MESH)
+                for h in range(2)
+            ]
+
+        def start(self):
+            for copy in self.halves:
+                copy.start()
+
+        def wait_send(self):
+            for copy in self.halves:
+                copy.wait_send()
+
+        def wait_recv(self):
+            for copy in self.halves:
+                copy.wait_recv()
+
+    hand_over = HandOver
 
     def store_end(mb):
         return pltpu.make_async_copy(handing.at[lax.rem(mb, 2)], ends_out.at[mb], store.at[mb])
@@ -696,8 +714,9 @@
         hidden = norm_c(halves[1], upper)
         upper = nn(hidden, up[...])
         close(halves[0], lower)
+        when(first, lambda: hand_over(mb, X).halves[0].start())
         close(halves[1], upper)
-        when(first, lambda: hand_over(mb, X).start())
+        when(first, lambda: hand_over(mb, X).halves[1].start())
         when(second, lambda: store_end(mb).start())
 
     def backward_a(mb):
@@ -899,8 +918,8 @@
         dma((len(SMALL_KINDS),)),
         dma((len(SMALL_KINDS),)),
         dma((micro + 3,)),
-        dma((micro,)),
-        dma((micro,)),
+        dma((micro, 2)),
+        dma((micro, 2)),
         dma((2, micro, 2)),
         dma((2, micro, 2)),
         dma((micro,)),

time: 182 us -> 182 us (level)
  no operation moved by 1% of the time
where the time goes in v7:
time: 182 us
  Pallas kernels  181 us (99%)
    pallas_call x1, Pallas kernels, run_blocks(): pl.pallas_call(functools.partial(blocks_kernel, names, with_sums, mesh_sh...  170 us
    pallas_call x1, Pallas kernels, finish(): pl.pallas_call(finish_kernel, name='outputs', out_shape=tuple((jax.ShapeD...  11.2 us

profile of v7, /device:TPU:0, one launch (start us, length us, event | category | flops | bytes accessed | tf_op | source)
XLA Modules:
  0.0 181.8 jit_solution(7098508303949761751)
XLA Ops:
  0.6 169.8 %two_blocks.1 = (bf16[4,256,1280]{2,1,0:T(8,128)(2,1)}, bf16[5760,640]{1,0:T(8,128)(2,1)}, f32[16,640]{1,0:T(8,128)}) custom-call(bf16[4,256,1280]{2,1,0:T(8,128)(2,1)} %bitcast.9, s32[4]{0:T(128)} %bitcast.15, f32[1,1280]{1,0:T(1,128)} %outer_gain.1, f32[2,640]{1,0:T(2,128)} %bitcast.14, f32[2,1280]{1,0:T(2,128)} %bitcast.12, f32[4,640]{1,0:T(4,128)} %bitcast.13, ...), custom_call_target="tpu_custom_call" | custom-call | flops 22649241600 | bytes 41943040 | tf_op jit(solution)/shard_map/two_blocks/pallas_call | solution.py:928
  170.5 11.2 %outputs.1 = (f32[1,4,1,256,1280]{4,3,2,1,0:T(8,128)}, f32[1,1280]{1,0:T(1,128)}, f32[1,2,640]{2,1,0:T(2,128)}, f32[1,2,1280]{2,1,0:T(2,128)}, f32[1,4,640]{2,1,...) custom-call(bf16[4,256,1280]{2,1,0:T(8,128)(2,1)} %get-tuple-element, ...), custom_call_target="tpu_custom_call" | custom-call | tf_op jit(solution)/shard_map/outputs/pallas_call | solution.py:986
